TPU v7x, 32 devices: a whole 2x2x4 slice. The times are simulated.
32 devices in a mesh: exp: 16 (over z, x, core), ten: 2 (over y).
Axes of the slice: x: 2, y: 2, z: 4, core: 2. Of those that a mesh axis runs over, the one named last changes fastest.
Arguments:
- tokens: bfloat16 [768, 4096], P('exp', 'ten'), may hold values from -6 to 6
- expert_ids: int32 [768, 8], P('exp'), may hold values from 0 to 15, all different within a row; in each aligned block of 48 rows (0 to 47, 48 to 95, ...) at most 30 rows name the same one
- combine_weights: float32 [768, 8], P('exp'), may hold values from 0.05 to 1
- gate_proj: bfloat16 [16, 1536, 4096], P('exp', 'ten'), may hold values from -0.09375 to 0.09375
- up_proj: bfloat16 [16, 1536, 4096], P('exp', 'ten'), may hold values from -0.09375 to 0.09375
- down_proj: bfloat16 [16, 1536, 4096], P('exp', 'ten'), may hold values from -0.15625 to 0.15625
Outputs:
- moe_out: bfloat16 [768, 4096], P('exp', 'ten')
Inputs may be any that keep to these rules, and one draw needn't show every extreme that they name: `expert_ids`: each row names 8 different experts. Within each aligned block of 48 rows (the rows of one index of exp) no expert is named by more than 30 rows.
All inputs are finite; a program needn't handle non-finite values.
Results may differ from a plain program's by a relative error of at most 0.01.
Values may be sent and summed in bfloat16 or wider, within the bound.
No kernel may reach another device: no remote copies, remote signals or barrier semaphores. Data moves between devices by JAX's collectives and lax.ppermute only.
A program may use at most 128 MiB of HBM per device.

v0:
```python
import jax
import jax.numpy as jnp
from jax import lax
from jax.sharding import PartitionSpec as P


def on_device(tokens, expert_ids, combine_weights, gate_proj, up_proj, down_proj):
    groups = lax.axis_size("exp")
    local_count = gate_proj.shape[0]
    experts = groups * local_count
    held = tokens.shape[0]
    picks = expert_ids.shape[1]
    capacity = min(held, max(2, held * picks * 5 // (4 * experts)))
    flattened = expert_ids.reshape(-1)
    matches = (flattened[:, None] == jnp.arange(experts, dtype=jnp.int32)[None, :]).astype(
        jnp.int32
    )
    earlier = jnp.cumsum(matches, axis=0) - matches
    slots = jnp.sum(earlier * matches, axis=1)
    targets = flattened * capacity + slots
    owners = jnp.arange(held * picks, dtype=jnp.int32) // picks
    columns = tokens.shape[1]
    buffer = jnp.zeros((experts * capacity, columns), tokens.dtype).at[targets].set(tokens[owners])
    arrived = lax.all_to_all(
        buffer.reshape(groups, local_count, capacity, columns),
        "exp",
        split_axis=0,
        concat_axis=0,
        tiled=True,
    )
    portion = lax.all_gather(arrived, "ten", axis=3, tiled=True)
    gate_add = jnp.einsum("secd,efd->secf", portion, gate_proj, preferred_element_type=jnp.float32)
    up_add = jnp.einsum("secd,efd->secf", portion, up_proj, preferred_element_type=jnp.float32)
    hidden = (jax.nn.silu(gate_add) * up_add).astype(jnp.bfloat16)
    weights = combine_weights.reshape(held, picks, 1)
    partial_value = jnp.einsum(
        "secf,efd->secd", hidden, down_proj, preferred_element_type=jnp.float32
    )
    summed = lax.psum_scatter(
        partial_value.astype(jnp.bfloat16), "ten", scatter_dimension=3, tiled=True
    ).astype(jnp.float32)
    returned = lax.all_to_all(
        summed.astype(jnp.bfloat16), "exp", split_axis=0, concat_axis=0, tiled=True
    ).astype(summed.dtype)
    picked = returned.reshape(experts * capacity, returned.shape[3])[targets]
    result = jnp.sum(weights * picked.reshape(held, picks, picked.shape[1]), axis=1)
    return result.astype(jnp.bfloat16)


def solution(mesh):
    return jax.shard_map(
        on_device,
        mesh=mesh,
        in_specs=(
            P("exp", "ten"),
            P("exp", None),
            P("exp", None),
            P("exp", "ten", None),
            P("exp", "ten", None),
            P("exp", "ten", None),
        ),
        out_specs=P("exp", "ten"),
        check_vma=False,
    )
```

profile of v0, /device:TPU:11, one launch (start us, length us, event | category | flops | bytes accessed | tf_op | source)
XLA Modules:
  0.0 280.4 jit_solution(7801478979243127973)
XLA Ops:
  6.5 0.0 copy-start
  6.5 0.0 all-gather.2.cloned.1.call-start
  6.5 0.8 copy.15
  7.3 0.1 eq.29
  7.4 0.1 eq.25
  7.5 0.7 broadcast_multiply_fusion
  8.3 0.9 reduce-window.6
  9.1 0.2 slice_reduce_fusion
  9.4 0.1 copy.14
  9.5 0.1 mul.37
  9.6 0.1 fusion.37
  9.7 0.0 copy-done
  9.7 9.3 %scatter_custom_fusion = bf16[480,2048]{1,0:T(8,128)(2,1)} fusion(s32[384]{0:T(512)S(1)} %fusion.39, bf16[48,2048]{1,0:T(8,128)(2,1)S(1)} %copy-done, s32[1024]{0:T(1024)S(1)} %pad_clamp_fusion.1, bf16[]{:T(256)} %constant.26.clone.1), kind=kCustom, calls=%fused_computation.22 | custom fusion | bytes 1966082 | tf_op jit(solution)/shard_map/scatter | solution.py:23
  19.0 1.8 reshape.124
  20.8 53.8 %all_to_all.10 = bf16[16,1,30,2048]{3,2,1,0:T(8,128)(2,1)} all-to-all(bf16[16,1,30,2048]{3,2,1,0:T(8,128)(2,1)S(1)} %bitcast.104), channel_id=1, replica_groups=mesh['exp'=16,'ten'=2] {'exp'}, dimensions={0} | all-to-all | bytes 3932160 | tf_op jit(solution)/shard_map/all_to_all | solution.py:24
  74.6 0.0 all-gather.2.cloned.1.call-update
  74.6 0.2 reduce-scatter.2.cloned.1.call-start
  74.8 56.4 %all-gather.2.cloned.1.call-done = bf16[16,1,30,4096]{3,2,0,1:T(8,128)(2,1)} async-done(((bf16[16,1,30,2048]{3,2,0,1:T(8,128)(2,1)}), bf16[16,1,30,4096]{3,2,0,1:T(8,128)(2,1)}) %all-gather.2.cloned.1.call-update) | async-done | bytes 3932176 | tf_op jit(solution)/shard_map/all_gather | solution.py:31
  131.2 7.1 %fusion.4 = f32[16,30,768]{2,1,0:T(8,128)S(1)} fusion(bf16[1,768,4096]{2,1,0:T(8,128)(2,1)} %param.9, bf16[16,1,30,4096]{3,2,0,1:T(8,128)(2,1)} %all-gather.2.cloned.1.call-done), kind=kOutput, calls=%fused_computation.7 | convolution fusion | flops 3019898880 | bytes 11698176 | tf_op jit(solution)/shard_map/secd,efd->secf/dot_general | solution.py:32
  138.3 16.6 %fusion.9 = bf16[16,1,30,4096]{3,2,0,1:T(8,128)(2,1)} fusion(bf16[1,768,4096]{2,1,0:T(8,128)(2,1)} %param.11, bf16[1,768,4096]{2,1,0:T(8,128)(2,1)} %param.10, bf16[16,1,30,4096]{3,2,0,1:T(8,128)(2,1)} %all-gather.2.cloned.1.call-done, f32[16,30,768]{2,1,0:T(8,128)S(1)} %fusion.4), kind=kOutput, calls=%fused_computation.10 | convolution fusion | flops 6043975680 | bytes 21921792 | tf_op jit(solution)/shard_map/secf,efd->secd/dot_general | solution.py:36
  155.0 0.0 reduce-scatter.2.cloned.1.call-update
  155.0 0.0 copy-start.1
  155.0 54.4 %reduce-scatter.2.cloned.1.call-done = bf16[16,1,30,2048]{3,2,0,1:T(8,128)(2,1)} async-done(((bf16[16,1,30,4096]{3,2,0,1:T(8,128)(2,1)}), bf16[16,1,30,2048]{3,2,0,1:T(8,128)(2,1)}) %reduce-scatter.2.cloned.1.call-update) | async-done | bytes 1966096 | tf_op jit(solution)/shard_map/reduce_scatter | solution.py:39
  209.4 6.4 %all-to-all-start.1 = ((bf16[16,1,30,2048]{3,2,1,0:T(8,128)(2,1)}), bf16[16,1,30,2048]{3,2,1,0:T(8,128)(2,1)S(1)}, u32[]{:S(2)}, u32[]{:S(2)}) async-start(bf16[16,1,30,2048]{3,2,1,0:T(8,128)(2,1)} %bitcast.105), calls=%async_computation.2 | async-start | bytes 4194304 | tf_op jit(solution)/shard_map/all_to_all | solution.py:42
  215.8 0.0 copy-done.1
  215.8 0.1 copy.13
  215.9 47.3 %all-to-all-done.1 = bf16[16,1,30,2048]{3,2,1,0:T(8,128)(2,1)S(1)} async-done(((bf16[16,1,30,2048]{3,2,1,0:T(8,128)(2,1)}), bf16[16,1,30,2048]{3,2,1,0:T(8,128)(2,1)S(1)}, u32[]{:S(2)}, u32[]{:S(2)}) %all-to-all-start.1) | async-done | bytes 1966112 | tf_op jit(solution)/shard_map/all_to_all | solution.py:42
  263.2 2.1 reshape.134
  265.3 6.4 %gather_fusion = f32[384,2048]{1,0:T(8,128)S(1)} fusion(f32[480,2048]{1,0:T(8,128)} %reshape.134, s32[1024]{0:T(1024)S(1)} %pad_clamp_fusion), kind=kCustom, calls=%fused_computation.1 | custom fusion | bytes 6292992 | tf_op jit(solution)/shard_map/gather | solution.py:45
  271.8 1.7 fusion.14
  (6 shorter events, 0.1 us)
Async XLA Ops:
  6.5 3.2 %copy-start = (bf16[48,2048]{1,0:T(8,128)(2,1)S(1)}, bf16[48,2048]{1,0:T(8,128)(2,1)}, u32[]{:S(2)}) copy-start(bf16[48,2048]{1,0:T(8,128)(2,1)} %param.6) | copy-start | bytes 589828
  6.5 124.7 %all-gather.2.cloned.1.call-start = ((), (), s32[]{:S(2)}) async-start(), calls=%async_computation.3 | async-start | bytes 6291456 | tf_op jit(solution)/shard_map/all_gather | solution.py:31
  74.6 134.9 %reduce-scatter.2.cloned.1.call-start = ((), (), s32[]{:S(2)}) async-start(), calls=%async_computation.4 | async-start | bytes 6291456 | tf_op jit(solution)/shard_map/reduce_scatter | solution.py:39
  155.0 60.8 %copy-start.1 = (f32[48,8]{0,1:T(8,128)S(1)}, f32[48,8]{0,1:T(8,128)}, u32[]{:S(2)}) copy-start(f32[48,8]{0,1:T(8,128)} %param.8) | copy-start | bytes 4612
  209.4 53.8 %all-to-all-start.1 = ((bf16[16,1,30,2048]{3,2,1,0:T(8,128)(2,1)}), bf16[16,1,30,2048]{3,2,1,0:T(8,128)(2,1)S(1)}, u32[]{:S(2)}, u32[]{:S(2)}) async-start(bf16[16,1,30,2048]{3,2,1,0:T(8,128)(2,1)} %bitcast.105), calls=%async_computation.2 | async-start | bytes 4194304 | tf_op jit(solution)/shard_map/all_to_all | solution.py:42
Sparse Core Ops, SparseCore 0:
  74.7 56.4 all-gather.1
  155.1 54.2 reduce-scatter.1
where the time goes:
time: 281 us; the launch traced here: 280 us
  waiting for transfers between devices  158 us (56%)
  blocking collectives  53.8 us (19%)
  matrix products  23.8 us (8%)
  local copies, waits for them, and re-layouts  21.1 us (8%)
  between operations  13.5 us (5%)
  starting transfers between devices  6.6 us (2%)
  other arithmetic  3.51 us (1%)
    all_gather x1, waiting for transfers between devices, on_device(): portion = lax.all_gather(arrived, 'ten', axis=3, tiled=True)  56.4 us
    reduce_scatter x1, waiting for transfers between devices, on_device(): lax.psum_scatter(partial_value.astype(jnp.bfloat16), 'ten', scatter_dimen...  54.4 us
    all_to_all x1, blocking collectives, on_device(): lax.all_to_all(buffer.reshape(groups, local_count, capacity, columns), 'e...  53.8 us
    all_to_all x1, waiting for transfers between devices, on_device(): lax.all_to_all(summed.astype(jnp.bfloat16), 'exp', split_axis=0, concat_a...  47.3 us
    dot_general x1, matrix products, on_device(): jnp.einsum('secf,efd->secd', hidden, down_proj, preferred_element_type=jn...  16.6 us
    scatter x1, local copies, waits for them, and re-layouts, on_device(): jnp.zeros((experts * capacity, columns), tokens.dtype).at[targets]  9.31 us
    dot_general x1, matrix products, on_device(): jnp.einsum('secd,efd->secf', portion, gate_proj, preferred_element_type=j...  7.14 us
    gather x1, local copies, waits for them, and re-layouts, on_device(): picked = returned.reshape(experts * capacity, returned.shape[3])[targets]  6.45 us
  transfers between devices with their start and end apart: 3, of which 3 were waited for; matrix products, arithmetic and copies ran while one was open for 0% of the time, Pallas kernels for 0%

commit v1 on v0

v1 whole, which is shorter than its diff:
```python
import functools

import jax
import jax.numpy as jnp
from jax import lax
from jax.experimental import pallas as pl
from jax.experimental.pallas import tpu as pltpu
from jax.sharding import Mesh, PartitionSpec as P

BF = jnp.bfloat16
F32 = jnp.float32
NT = (((1,), (1,)), ((), ()))


def block_of(extent, want):
    size = min(extent, want)
    while extent % size:
        size //= 2
    return size


def ffn_kernel(steps, halves, pieces, own_cols, sc, *refs):
    n = pieces
    own, oth = refs[:n], refs[n : 2 * n]
    wg, wu, wd = refs[2 * n : 2 * n + 3]
    outs = refs[2 * n + 3 : -3]
    x_s, h_s, w_s = refs[-3:]
    i = pl.program_id(0)
    rows = own[0].shape[0]
    n_hidden, n_down = steps

    @pl.when(i == 0)
    def _():
        mine = pl.multiple_of(sc[0] * own_cols, 128)
        other = pl.multiple_of((1 - sc[0]) * own_cols, 128)
        lane = lax.broadcasted_iota(jnp.int32, (rows, 128), 1)
        chosen = (lane == sc[1]) | (lane == sc[1] + 64)
        for j in range(n):
            r = pl.ds(j * rows, rows)
            x_s[r, pl.ds(mine, own_cols)] = own[j][:, :own_cols]
            x_s[r, pl.ds(other, own_cols)] = oth[j][:, :own_cols]
            tail = own[j][:, own_cols:].astype(F32)
            w_s[r, :] = jnp.broadcast_to(
                jnp.sum(jnp.where(chosen, tail, 0.0), axis=1, keepdims=True), (rows, 128)
            )

    @pl.when(i < n_hidden)
    def _():
        x = x_s[...]
        g = lax.dot_general(x, wg[...], NT, preferred_element_type=F32)
        u = lax.dot_general(x, wu[...], NT, preferred_element_type=F32)
        h_s[i] = (g / (1.0 + jnp.exp(-g)) * u * w_s[:, :1]).astype(BF)

    def down(group):
        h = jnp.concatenate([h_s[k] for k in range(n_hidden)], axis=1)
        o = jnp.dot(h, wd[...], preferred_element_type=F32).astype(BF)
        per = n // len(group) * rows
        for k, ref in enumerate(group):
            ref[...] = o[k * per : (k + 1) * per]

    half = len(outs) // 2

    @pl.when((i >= n_hidden) & (i < n_hidden + n_down // 2))
    def _():
        down(outs[:half])

    @pl.when(i >= n_hidden + n_down // 2)
    def _():
        down(outs[half:])


def ffn(own, oth, sc, wg, wu, wd):
    n = len(own)
    rows, wide = own[0].shape
    cols = wide - 128
    ff, d = wg.shape
    fb, nb = block_of(ff, 256), block_of(cols, 1024)
    nh, nd = ff // fb, d // nb
    hd = nd // 2
    total = n * rows
    piece = pl.BlockSpec((rows, wide), lambda i, s: (0, 0))
    up = pl.BlockSpec((fb, d), lambda i, s: (jnp.minimum(i, nh - 1), 0))

    def down_col(i, s):
        return (0, (s[0] * hd + jnp.maximum(i - nh, 0)) % nd)

    out_own = pl.BlockSpec((total // 2, nb), lambda i, s: (0, jnp.clip(i - nh, 0, hd - 1)))
    out_oth = pl.BlockSpec((total // 2, nb), lambda i, s: (0, jnp.clip(i - nh - hd, 0, hd - 1)))
    shape = jax.ShapeDtypeStruct((total // 2, cols), BF)
    return pl.pallas_call(
        functools.partial(ffn_kernel_entry, (nh, nd), n, cols),
        grid_spec=pltpu.PrefetchScalarGridSpec(
            num_scalar_prefetch=1,
            grid=(nh + nd,),
            in_specs=[piece] * (2 * n) + [up, up, pl.BlockSpec((ff, nb), down_col)],
            out_specs=[out_own, out_own, out_oth, out_oth],
            scratch_shapes=[
                pltpu.VMEM((total, d), BF),
                pltpu.VMEM((nh, total, fb), BF),
                pltpu.VMEM((total, 128), F32),
            ],
        ),
        out_shape=[shape] * 4,
        compiler_params=pltpu.CompilerParams(vmem_limit_bytes=48 << 20),
        cost_estimate=pl.CostEstimate(
            flops=6 * total * ff * d, bytes_accessed=6 * ff * d + 4 * total * d, transcendentals=total * ff
        ),
        name="ffn",
    )(sc, *own, *oth, wg, wu, wd)


def ffn_kernel_entry(steps, pieces, cols, sc, *refs):
    ffn_kernel(steps, 4, pieces, cols, sc, *refs)


def dense_weights(expert_ids, combine_weights, experts):
    hits = expert_ids[:, :, None] == jnp.arange(experts, dtype=jnp.int32)
    return jnp.sum(jnp.where(hits, combine_weights[:, :, None], 0.0), axis=1)


def on_device(tokens, expert_ids, combine_weights, gate_proj, up_proj, down_proj):
    held, cols = tokens.shape
    nz, nx = lax.axis_size("z"), lax.axis_size("x")
    experts = nz * nx * 2
    wg, wu, wd = gate_proj[0], up_proj[0], down_proj[0]
    z, x, c, y = (lax.axis_index(a) for a in ("z", "x", "c", "y"))
    sc = jnp.stack([y, (z * nx + x) * 2 + c]).astype(jnp.int32)

    swap = [(0, 1), (1, 0)]
    px = lambda a: lax.ppermute(a, "x", swap)
    py = lambda a: lax.ppermute(a, "y", swap)
    pc = lambda a: lax.ppermute(a, "c", swap)
    ahead = lambda a, k: lax.ppermute(a, "z", [(i, (i + k) % nz) for i in range(nz)])

    w = dense_weights(expert_ids, combine_weights, experts)
    hi = w.astype(BF)
    lo = (w - hi.astype(F32)).astype(BF)
    pad = jnp.zeros((held, 64 - experts), BF)
    t = [jnp.concatenate([tokens, hi, pad, lo, pad], axis=1)]

    for k in range(1, nz):
        t.append(ahead(t[-1], 1))
    xs = [px(a) for a in t]
    ys = [py(a) for a in t]
    early, late = list(range(nz // 2)), list(range(nz // 2, nz))
    ds = [py(xs[k]) for k in early] + [px(ys[k]) for k in late]

    first = ffn(t + [pc(a) for a in t], ys + [pc(a) for a in ys], sc, wg, wu, wd)
    last = ffn(xs + [pc(a) for a in xs], ds + [pc(a) for a in ds], sc, wg, wu, wd)

    def plane_sum(own_c, oth_c):
        s = own_c.astype(F32) + pc(oth_c).astype(F32)
        return s.reshape(nz, held, cols)

    s1_own, s1_oth = plane_sum(first[0], first[1]), plane_sum(first[2], first[3])
    s2_own, s2_oth = plane_sum(last[0], last[1]), plane_sum(last[2], last[3])

    ga, gb = [1, 3], [2, 0]
    done = {}
    ry1 = {k: py(s1_oth[k].astype(BF)) for k in gb}
    ry2 = {k: py(s2_oth[k].astype(BF)) for k in gb}
    for k in ga:
        r = px(jnp.stack([s2_own[k], s2_oth[k]]).astype(BF)).astype(F32)
        back = py((s1_oth[k] + r[1]).astype(BF)).astype(F32)
        done[k] = s1_own[k] + r[0] + back
    for k in gb:
        v = px((s2_own[k] + ry2[k].astype(F32)).astype(BF)).astype(F32)
        done[k] = s1_own[k] + ry1[k].astype(F32) + v
    total = done[0]
    for k in range(1, nz):
        total = total + ahead(done[k].astype(BF), nz - k).astype(F32)
    return total.astype(BF)


def on_device_any(tokens, expert_ids, combine_weights, gate_proj, up_proj, down_proj):
    groups = lax.axis_size("exp")
    held, cols = tokens.shape
    local = gate_proj.shape[0]
    w = lax.all_gather(dense_weights(expert_ids, combine_weights, groups * local), "exp", axis=0, tiled=True)
    rows = lax.all_gather(lax.all_gather(tokens, "ten", axis=1, tiled=True), "exp", axis=0, tiled=True)
    total = jnp.zeros((rows.shape[0], rows.shape[1]), F32)
    for j in range(local):
        g = lax.dot_general(rows, gate_proj[j], NT, preferred_element_type=F32)
        u = lax.dot_general(rows, up_proj[j], NT, preferred_element_type=F32)
        mine = jnp.take(w, lax.axis_index("exp") * local + j, axis=1)[:, None]
        h = (jax.nn.silu(g) * u * mine).astype(BF)
        total = total + jnp.dot(h, down_proj[j], preferred_element_type=F32)
    part = lax.psum_scatter(total.astype(BF), "exp", scatter_dimension=0, tiled=True)
    return lax.psum_scatter(part, "ten", scatter_dimension=1, tiled=True).astype(BF)


def solution(mesh):
    sizes = (mesh.shape["exp"], mesh.shape["ten"])
    if sizes == (16, 2):
        mesh = Mesh(mesh.devices.reshape(4, 2, 2, 2), ("z", "x", "c", "y"))
        exp, ten, body = ("z", "x", "c"), "y", on_device
    else:
        exp, ten, body = "exp", "ten", on_device_any
    return jax.shard_map(
        body,
        mesh=mesh,
        in_specs=(
            P(exp, ten),
            P(exp, None),
            P(exp, None),
            P(exp, ten, None),
            P(exp, ten, None),
            P(exp, ten, None),
        ),
        out_specs=P(exp, ten),
        check_vma=False,
    )
```

time: 281 us -> 146 us (0.52)
  the two profiles are of different devices: /device:TPU:11 before, /device:TPU:0 now
where the time goes in v1:
time: 146 us
  waiting for transfers between devices  68 us (47%)
  starting transfers between devices  37.4 us (26%)
  Pallas kernels  31.4 us (22%)
  local copies, waits for them, and re-layouts  5.25 us (4%)
  other arithmetic  3.3 us (2%)
    pallas_call x2, Pallas kernels, ffn(): pl.pallas_call(functools.partial(ffn_kernel_entry, (nh, nd), n, cols), gr...  31.4 us
    ppermute x6, waiting for transfers between devices, on_device(): lax.ppermute(a, 'z', [(i, (i + k) % nz) for i in range(nz)])  24 us
    ppermute x10, waiting for transfers between devices, on_device(): px = lambda a: lax.ppermute(a, 'x', swap)  23.3 us
    ppermute x12, waiting for transfers between devices, on_device(): py = lambda a: lax.ppermute(a, 'y', swap)  20 us
    ppermute x12, starting transfers between devices, on_device(): py = lambda a: lax.ppermute(a, 'y', swap)  14.9 us
    ppermute x10, starting transfers between devices, on_device(): px = lambda a: lax.ppermute(a, 'x', swap)  9.86 us
    ppermute x6, starting transfers between devices, on_device(): lax.ppermute(a, 'z', [(i, (i + k) % nz) for i in range(nz)])  8.97 us
    unnamed x12, local copies, waits for them, and re-layouts  3.92 us
  transfers between devices with their start and end apart: 48, of which 19 were waited for; matrix products, arithmetic and copies ran while one was open for 1% of the time, Pallas kernels for 22%

profile of v1, /device:TPU:0, one launch (start us, length us, event | category | flops | bytes accessed | tf_op | source)
XLA Modules:
  0.0 145.6 jit_solution(8987850502018251897)
XLA Ops:
  0.9 1.0 concatenate.3.refs_0_
  2.0 3.1 %collective-permute-start = (bf16[48,2176]{1,0:T(8,128)(2,1)S(1)}, bf16[48,2176]{1,0:T(8,128)(2,1)S(1)}, u32[]{:S(2)}, u32[]{:S(2)}) collective-permute-start(bf16[48,2176]{1,0:T(8,128)(2,1)S(1)} %concatenate.3.refs_0_), channel_id=1, source_target_pairs={{0,8},{8,16},{16,24},{24,0},{1,9},{9,17},{17,25},{25,1},{2,10},{10... | collective-permute-start | bytes 626696 | tf_op jit(solution)/shard_map/ppermute | solution.py:133
  5.0 1.5 %collective-permute-start.18 = (bf16[48,2176]{1,0:T(8,128)(2,1)S(1)}, bf16[48,2176]{1,0:T(8,128)(2,1)S(1)}, u32[]{:S(2)}, u32[]{:S(2)}) collective-permute-start(bf16[48,2176]{1,0:T(8,128)(2,1)S(1)} %concatenate.3.refs_0_), channel_id=1, source_target_pairs={{0,4},{4,0},{1,5},{5,1},{2,6},{6,2},{3,7},{7,3},{8,12},{12,8},{9,1... | collective-permute-start | bytes 626696 | tf_op jit(solution)/shard_map/ppermute | solution.py:130
  6.5 1.5 %collective-permute-start.7 = (bf16[48,2176]{1,0:T(8,128)(2,1)S(1)}, bf16[48,2176]{1,0:T(8,128)(2,1)S(1)}, u32[]{:S(2)}, u32[]{:S(2)}) collective-permute-start(bf16[48,2176]{1,0:T(8,128)(2,1)S(1)} %concatenate.3.refs_0_), channel_id=1, source_target_pairs={{0,1},{1,0},{2,3},{3,2},{4,5},{5,4},{6,7},{7,6},{8,9},{9,8},{10,11... | collective-permute-start | bytes 626696 | tf_op jit(solution)/shard_map/ppermute | solution.py:131
  8.0 4.2 %collective-permute-done.refs_1_ = bf16[48,2176]{1,0:T(8,128)(2,1)S(1)} collective-permute-done((bf16[48,2176]{1,0:T(8,128)(2,1)S(1)}, bf16[48,2176]{1,0:T(8,128)(2,1)S(1)}, u32[]{:S(2)}, u32[]{:S(2)}) %collective-permute-start) | collective-permute-done | bytes 208928 | tf_op jit(solution)/shard_map/ppermute | solution.py:133
  12.2 1.5 %collective-permute-start.19 = (bf16[48,2176]{1,0:T(8,128)(2,1)S(1)}, bf16[48,2176]{1,0:T(8,128)(2,1)S(1)}, u32[]{:S(2)}, u32[]{:S(2)}) collective-permute-start(bf16[48,2176]{1,0:T(8,128)(2,1)S(1)} %collective-permute-done.refs_1_), channel_id=1, source_target_pairs={{0,4},{4,0},{1,5},{5,1},{2,6},{6,2},{3,7},{7,3},{8,12},{12,8},{9,1... | collective-permute-start | bytes 626696 | tf_op jit(solution)/shard_map/ppermute | solution.py:130
  13.7 1.5 %collective-permute-start.26 = (bf16[48,2176]{1,0:T(8,128)(2,1)S(1)}, bf16[48,2176]{1,0:T(8,128)(2,1)S(1)}, u32[]{:S(2)}, u32[]{:S(2)}) collective-permute-start(bf16[48,2176]{1,0:T(8,128)(2,1)S(1)} %collective-permute-done.18.refs_0_), channel_id=1, source_target_pairs={{0,1},{1,0},{2,3},{3,2},{4,5},{5,4},{6,7},{7,6},{8,9},{9,8},{10,11... | collective-permute-start | bytes 626696 | tf_op jit(solution)/shard_map/ppermute | solution.py:131
  15.8 4.5 %collective-permute-done.1.refs_2_ = bf16[48,2176]{1,0:T(8,128)(2,1)S(1)} collective-permute-done((bf16[48,2176]{1,0:T(8,128)(2,1)S(1)}, bf16[48,2176]{1,0:T(8,128)(2,1)S(1)}, u32[]{:S(2)}, u32[]{:S(2)}) %collective-permute-start.1) | collective-permute-done | bytes 208928 | tf_op jit(solution)/shard_map/ppermute | solution.py:133
  20.9 1.1 collective-permute-start.2
  22.0 2.5 %collective-permute-start.9 = (bf16[48,2176]{1,0:T(8,128)(2,1)S(1)}, bf16[48,2176]{1,0:T(8,128)(2,1)}, u32[]{:S(2)}, u32[]{:S(2)}) collective-permute-start(bf16[48,2176]{1,0:T(8,128)(2,1)S(1)} %collective-permute-done.1.refs_2_), channel_id=1, source_target_pairs={{0,1},{1,0},{2,3},{3,2},{4,5},{5,4},{6,7},{7,6},{8,9},{9,8},{10,11... | collective-permute-start | bytes 626696 | tf_op jit(solution)/shard_map/ppermute | solution.py:131
  25.1 1.1 collective-permute-start.27
  26.1 3.7 %collective-permute-done.2.refs_3_ = bf16[48,2176]{1,0:T(8,128)(2,1)S(1)} collective-permute-done((bf16[48,2176]{1,0:T(8,128)(2,1)S(1)}, bf16[48,2176]{1,0:T(8,128)(2,1)S(1)}, u32[]{:S(2)}, u32[]{:S(2)}) %collective-permute-start.2) | collective-permute-done | bytes 208928 | tf_op jit(solution)/shard_map/ppermute | solution.py:133
  31.2 1.8 %collective-permute-done.27.refs_9_ = bf16[48,2176]{1,0:T(8,128)(2,1)S(1)} collective-permute-done((bf16[48,2176]{1,0:T(8,128)(2,1)S(1)}, bf16[48,2176]{1,0:T(8,128)(2,1)S(1)}, u32[]{:S(2)}, u32[]{:S(2)}) %collective-permute-start.27) | collective-permute-done | bytes 208928 | tf_op jit(solution)/shard_map/ppermute | solution.py:131
  33.0 1.5 %collective-permute-start.10 = (bf16[48,2176]{1,0:T(8,128)(2,1)S(1)}, bf16[48,2176]{1,0:T(8,128)(2,1)}, u32[]{:S(2)}, u32[]{:S(2)}) collective-permute-start(bf16[48,2176]{1,0:T(8,128)(2,1)S(1)} %collective-permute-done.2.refs_3_), channel_id=1, source_target_pairs={{0,1},{1,0},{2,3},{3,2},{4,5},{5,4},{6,7},{7,6},{8,9},{9,8},{10,11... | collective-permute-start | bytes 626696 | tf_op jit(solution)/shard_map/ppermute | solution.py:131
  35.3 1.2 collective-permute-start.28
  39.7 2.9 %collective-permute-done.21.refs_3_ = bf16[48,2176]{1,0:T(8,128)(2,1)S(1)} collective-permute-done((bf16[48,2176]{1,0:T(8,128)(2,1)S(1)}, bf16[48,2176]{1,0:T(8,128)(2,1)S(1)}, u32[]{:S(2)}, u32[]{:S(2)}) %collective-permute-start.21) | collective-permute-done | bytes 208928 | tf_op jit(solution)/shard_map/ppermute | solution.py:130
  43.4 3.2 %collective-permute-done.28.refs_10_ = bf16[48,2176]{1,0:T(8,128)(2,1)} collective-permute-done((bf16[48,2176]{1,0:T(8,128)(2,1)}, bf16[48,2176]{1,0:T(8,128)(2,1)}, u32[]{:S(2)}, u32[]{:S(2)}) %collective-permute-start.28) | collective-permute-done | bytes 208928 | tf_op jit(solution)/shard_map/ppermute | solution.py:130
  47.1 1.6 %collective-permute-done.29.refs_11_ = bf16[48,2176]{1,0:T(8,128)(2,1)} collective-permute-done((bf16[48,2176]{1,0:T(8,128)(2,1)}, bf16[48,2176]{1,0:T(8,128)(2,1)}, u32[]{:S(2)}, u32[]{:S(2)}) %collective-permute-start.29) | collective-permute-done | bytes 208928 | tf_op jit(solution)/shard_map/ppermute | solution.py:130
  51.2 15.8 %ffn.2 = (bf16[192,2048]{1,0:T(8,128)(2,1)S(1)}, bf16[192,2048]{1,0:T(8,128)(2,1)S(1)}, bf16[192,2048]{1,0:T(8,128)(2,1)S(1)}, bf16[192,2048]{1,0:T(8,128)(2,1)}) custom-call(s32[2]{0:T(128)S(1)} %pad_add_fusion.sc, bf16[48,2176]{1,0:T(8,128)(2,1)S(1)} %concatenate.3.refs_0_, bf16[48,2176]{1,0:T(8,128)(2,1)S(1)} %collective-permute-done.refs_1_, ...), custom_call_target="tpu_custom_call" | custom-call | flops 7247757312 | bytes 25165824 | tf_op jit(solution)/shard_map/ffn/pallas_call | solution.py:90
  67.6 15.6 %ffn.3 = (bf16[192,2048]{1,0:T(8,128)(2,1)S(1)}, bf16[192,2048]{1,0:T(8,128)(2,1)S(1)}, bf16[192,2048]{1,0:T(8,128)(2,1)S(1)}, bf16[192,2048]{1,0:T(8,128)(2,1)}) custom-call(s32[2]{0:T(128)S(1)} %pad_add_fusion.sc, bf16[48,2176]{1,0:T(8,128)(2,1)S(1)} %collective-permute-done.18.refs_0_, bf16[48,2176]{1,0:T(8,128)(2,1)S(1)} %collective-permute-done.19.refs_1_, ...), custom_call_target="tpu_custom_call" | custom-call | flops 7247757312 | bytes 25165824 | tf_op jit(solution)/shard_map/ffn/pallas_call | solution.py:90
  84.4 1.7 %collective-permute-start.17 = (bf16[48,2048]{1,0:T(8,128)(2,1)S(1)}, bf16[48,2048]{1,0:T(8,128)(2,1)S(1)}, u32[]{:S(2)}, u32[]{:S(2)}) collective-permute-start(bf16[48,2048]{1,0:T(8,128)(2,1)S(1)} %get-tuple-element.32), channel_id=1, source_target_pairs={{0,1},{1,0},{2,3},{3,2},{4,5},{5,4},{6,7},{7,6},{8,9},{9,8},{10,11... | collective-permute-start | bytes 589832 | tf_op jit(solution)/shard_map/ppermute | solution.py:131
  87.6 1.7 %collective-permute-start.42 = (bf16[48,2048]{1,0:T(8,128)(2,1)S(1)}, bf16[48,2048]{1,0:T(8,128)(2,1)S(1)}, u32[]{:S(2)}, u32[]{:S(2)}) collective-permute-start(bf16[48,2048]{1,0:T(8,128)(2,1)S(1)} %get-tuple-element.36), channel_id=1, source_target_pairs={{0,1},{1,0},{2,3},{3,2},{4,5},{5,4},{6,7},{7,6},{8,9},{9,8},{10,11... | collective-permute-start | bytes 589832 | tf_op jit(solution)/shard_map/ppermute | solution.py:131
  89.6 10.6 %collective-permute-done.36 = bf16[48,2048]{1,0:T(8,128)(2,1)S(1)} collective-permute-done((bf16[48,2048]{1,0:T(8,128)(2,1)S(1)}, bf16[48,2048]{1,0:T(8,128)(2,1)S(1)}, u32[]{:S(2)}, u32[]{:S(2)}) %collective-permute-start.36) | collective-permute-done | bytes 196640 | tf_op jit(solution)/shard_map/ppermute | solution.py:131
  101.1 2.5 %collective-permute-done.42 = bf16[48,2048]{1,0:T(8,128)(2,1)S(1)} collective-permute-done((bf16[48,2048]{1,0:T(8,128)(2,1)S(1)}, bf16[48,2048]{1,0:T(8,128)(2,1)S(1)}, u32[]{:S(2)}, u32[]{:S(2)}) %collective-permute-start.42) | collective-permute-done | bytes 196640 | tf_op jit(solution)/shard_map/ppermute | solution.py:131
  104.5 7.8 %collective-permute-done.45 = bf16[2,48,2048]{2,1,0:T(8,128)(2,1)S(1)} collective-permute-done((bf16[2,48,2048]{2,1,0:T(8,128)(2,1)S(1)}, bf16[2,48,2048]{2,1,0:T(8,128)(2,1)S(1)}, u32[]{:S(2)}, u32[]{:S(2)}) %collective-permute-start.45) | collective-permute-done | bytes 393248 | tf_op jit(solution)/shard_map/ppermute | solution.py:130
  113.2 7.0 %collective-permute-done.38 = bf16[2,48,2048]{2,1,0:T(8,128)(2,1)S(1)} collective-permute-done((bf16[2,48,2048]{2,1,0:T(8,128)(2,1)S(1)}, bf16[2,48,2048]{2,1,0:T(8,128)(2,1)S(1)}, u32[]{:S(2)}, u32[]{:S(2)}) %collective-permute-start.38) | collective-permute-done | bytes 393248 | tf_op jit(solution)/shard_map/ppermute | solution.py:130
  120.8 1.7 %collective-permute-start.46 = (bf16[48,2048]{1,0:T(8,128)(2,1)S(1)}, bf16[48,2048]{1,0:T(8,128)(2,1)S(1)}, u32[]{:S(2)}, u32[]{:S(2)}) collective-permute-start(bf16[48,2048]{1,0:T(8,128)(2,1)S(1)} %get-tuple-element.27), channel_id=1, source_target_pairs={{0,1},{1,0},{2,3},{3,2},{4,5},{5,4},{6,7},{7,6},{8,9},{9,8},{10,11... | collective-permute-start | bytes 589832 | tf_op jit(solution)/shard_map/ppermute | solution.py:131
  124.4 1.7 %collective-permute-done.39 = bf16[48,2048]{1,0:T(8,128)(2,1)S(1)} collective-permute-done((bf16[48,2048]{1,0:T(8,128)(2,1)S(1)}, bf16[48,2048]{1,0:T(8,128)(2,1)S(1)}, u32[]{:S(2)}, u32[]{:S(2)}) %collective-permute-start.39) | collective-permute-done | bytes 196640 | tf_op jit(solution)/shard_map/ppermute | solution.py:131
  126.1 2.1 %collective-permute-done.46 = bf16[48,2048]{1,0:T(8,128)(2,1)S(1)} collective-permute-done((bf16[48,2048]{1,0:T(8,128)(2,1)S(1)}, bf16[48,2048]{1,0:T(8,128)(2,1)S(1)}, u32[]{:S(2)}, u32[]{:S(2)}) %collective-permute-start.46) | collective-permute-done | bytes 196640 | tf_op jit(solution)/shard_map/ppermute | solution.py:131
  128.4 4.1 %collective-permute-start.40 = (bf16[48,2048]{1,0:T(8,128)(2,1)S(1)}, bf16[48,2048]{1,0:T(8,128)(2,1)S(1)}, u32[]{:S(2)}, u32[]{:S(2)}) collective-permute-start(bf16[48,2048]{1,0:T(8,128)(2,1)S(1)} %get-tuple-element.23), channel_id=1, source_target_pairs={{0,24},{8,0},{16,8},{24,16},{1,25},{9,1},{17,9},{25,17},{2,26},{10... | collective-permute-start | bytes 589832 | tf_op jit(solution)/shard_map/ppermute | solution.py:133
  133.2 4.1 %collective-permute-done.40 = bf16[48,2048]{1,0:T(8,128)(2,1)S(1)} collective-permute-done((bf16[48,2048]{1,0:T(8,128)(2,1)S(1)}, bf16[48,2048]{1,0:T(8,128)(2,1)S(1)}, u32[]{:S(2)}, u32[]{:S(2)}) %collective-permute-start.40) | collective-permute-done | bytes 196640 | tf_op jit(solution)/shard_map/ppermute | solution.py:133
  137.3 7.4 %collective-permute-done.44 = bf16[48,2048]{1,0:T(8,128)(2,1)S(1)} collective-permute-done((bf16[48,2048]{1,0:T(8,128)(2,1)S(1)}, bf16[48,2048]{1,0:T(8,128)(2,1)S(1)}, u32[]{:S(2)}, u32[]{:S(2)}) %collective-permute-start.44) | collective-permute-done | bytes 196640 | tf_op jit(solution)/shard_map/ppermute | solution.py:133
  (101 shorter events, 22.3 us)
Async XLA Ops:
  2.0 10.3 %collective-permute-start = (bf16[48,2176]{1,0:T(8,128)(2,1)S(1)}, bf16[48,2176]{1,0:T(8,128)(2,1)S(1)}, u32[]{:S(2)}, u32[]{:S(2)}) collective-permute-start(bf16[48,2176]{1,0:T(8,128)(2,1)S(1)} %concatenate.3.refs_0_), channel_id=1, source_target_pairs={{0,8},{8,16},{16,24},{24,0},{1,9},{9,17},{17,25},{25,1},{2,10},{10... | collective-permute-start | bytes 626696 | tf_op jit(solution)/shard_map/ppermute | solution.py:133
  5.0 8.7 %collective-permute-start.18 = (bf16[48,2176]{1,0:T(8,128)(2,1)S(1)}, bf16[48,2176]{1,0:T(8,128)(2,1)S(1)}, u32[]{:S(2)}, u32[]{:S(2)}) collective-permute-start(bf16[48,2176]{1,0:T(8,128)(2,1)S(1)} %concatenate.3.refs_0_), channel_id=1, source_target_pairs={{0,4},{4,0},{1,5},{5,1},{2,6},{6,2},{3,7},{7,3},{8,12},{12,8},{9,1... | collective-permute-start | bytes 626696 | tf_op jit(solution)/shard_map/ppermute | solution.py:130
  6.5 8.7 %collective-permute-start.7 = (bf16[48,2176]{1,0:T(8,128)(2,1)S(1)}, bf16[48,2176]{1,0:T(8,128)(2,1)S(1)}, u32[]{:S(2)}, u32[]{:S(2)}) collective-permute-start(bf16[48,2176]{1,0:T(8,128)(2,1)S(1)} %concatenate.3.refs_0_), channel_id=1, source_target_pairs={{0,1},{1,0},{2,3},{3,2},{4,5},{5,4},{6,7},{7,6},{8,9},{9,8},{10,11... | collective-permute-start | bytes 626696 | tf_op jit(solution)/shard_map/ppermute | solution.py:131
  12.2 8.1 %collective-permute-start.1 = (bf16[48,2176]{1,0:T(8,128)(2,1)S(1)}, bf16[48,2176]{1,0:T(8,128)(2,1)S(1)}, u32[]{:S(2)}, u32[]{:S(2)}) collective-permute-start(bf16[48,2176]{1,0:T(8,128)(2,1)S(1)} %collective-permute-done.refs_1_), channel_id=1, source_target_pairs={{0,8},{8,16},{16,24},{24,0},{1,9},{9,17},{17,25},{25,1},{2,10},{10... | collective-permute-start | bytes 626696 | tf_op jit(solution)/shard_map/ppermute | solution.py:133
  12.2 8.2 %collective-permute-start.19 = (bf16[48,2176]{1,0:T(8,128)(2,1)S(1)}, bf16[48,2176]{1,0:T(8,128)(2,1)S(1)}, u32[]{:S(2)}, u32[]{:S(2)}) collective-permute-start(bf16[48,2176]{1,0:T(8,128)(2,1)S(1)} %collective-permute-done.refs_1_), channel_id=1, source_target_pairs={{0,4},{4,0},{1,5},{5,1},{2,6},{6,2},{3,7},{7,3},{8,12},{12,8},{9,1... | collective-permute-start | bytes 626696 | tf_op jit(solution)/shard_map/ppermute | solution.py:130
  15.2 9.3 %collective-permute-start.8 = (bf16[48,2176]{1,0:T(8,128)(2,1)S(1)}, bf16[48,2176]{1,0:T(8,128)(2,1)S(1)}, u32[]{:S(2)}, u32[]{:S(2)}) collective-permute-start(bf16[48,2176]{1,0:T(8,128)(2,1)S(1)} %collective-permute-done.refs_1_), channel_id=1, source_target_pairs={{0,1},{1,0},{2,3},{3,2},{4,5},{5,4},{6,7},{7,6},{8,9},{9,8},{10,11... | collective-permute-start | bytes 626696 | tf_op jit(solution)/shard_map/ppermute | solution.py:131
  20.9 8.9 %collective-permute-start.2 = (bf16[48,2176]{1,0:T(8,128)(2,1)S(1)}, bf16[48,2176]{1,0:T(8,128)(2,1)S(1)}, u32[]{:S(2)}, u32[]{:S(2)}) collective-permute-start(bf16[48,2176]{1,0:T(8,128)(2,1)S(1)} %collective-permute-done.1.refs_2_), channel_id=1, source_target_pairs={{0,8},{8,16},{16,24},{24,0},{1,9},{9,17},{17,25},{25,1},{2,10},{10... | collective-permute-start | bytes 626696 | tf_op jit(solution)/shard_map/ppermute | solution.py:133
  22.0 8.7 %collective-permute-start.9 = (bf16[48,2176]{1,0:T(8,128)(2,1)S(1)}, bf16[48,2176]{1,0:T(8,128)(2,1)}, u32[]{:S(2)}, u32[]{:S(2)}) collective-permute-start(bf16[48,2176]{1,0:T(8,128)(2,1)S(1)} %collective-permute-done.1.refs_2_), channel_id=1, source_target_pairs={{0,1},{1,0},{2,3},{3,2},{4,5},{5,4},{6,7},{7,6},{8,9},{9,8},{10,11... | collective-permute-start | bytes 626696 | tf_op jit(solution)/shard_map/ppermute | solution.py:131
  26.1 8.4 %collective-permute-start.23 = (bf16[48,2176]{1,0:T(8,128)(2,1)S(1)}, bf16[48,2176]{1,0:T(8,128)(2,1)S(1)}, u32[]{:S(2)}, u32[]{:S(2)}) collective-permute-start(bf16[48,2176]{1,0:T(8,128)(2,1)S(1)} %collective-permute-done.19.refs_1_), channel_id=1, source_target_pairs={{0,2},{2,0},{1,3},{3,1},{4,6},{6,4},{5,7},{7,5},{8,10},{10,8},{9,1... | collective-permute-start | bytes 626696 | tf_op jit(solution)/shard_map/ppermute | solution.py:132
  34.5 8.1 %collective-permute-start.21 = (bf16[48,2176]{1,0:T(8,128)(2,1)S(1)}, bf16[48,2176]{1,0:T(8,128)(2,1)S(1)}, u32[]{:S(2)}, u32[]{:S(2)}) collective-permute-start(bf16[48,2176]{1,0:T(8,128)(2,1)S(1)} %collective-permute-done.2.refs_3_), channel_id=1, source_target_pairs={{0,4},{4,0},{1,5},{5,1},{2,6},{6,2},{3,7},{7,3},{8,12},{12,8},{9,1... | collective-permute-start | bytes 626696 | tf_op jit(solution)/shard_map/ppermute | solution.py:130
  35.3 11.2 %collective-permute-start.28 = (bf16[48,2176]{1,0:T(8,128)(2,1)}, bf16[48,2176]{1,0:T(8,128)(2,1)}, u32[]{:S(2)}, u32[]{:S(2)}) collective-permute-start(bf16[48,2176]{1,0:T(8,128)(2,1)} %collective-permute-done.9.refs_10_), channel_id=1, source_target_pairs={{0,4},{4,0},{1,5},{5,1},{2,6},{6,2},{3,7},{7,3},{8,12},{12,8},{9,1... | collective-permute-start | bytes 626696 | tf_op jit(solution)/shard_map/ppermute | solution.py:130
  37.2 9.4 %collective-permute-start.6 = (bf16[48,2176]{1,0:T(8,128)(2,1)S(1)}, bf16[48,2176]{1,0:T(8,128)(2,1)}, u32[]{:S(2)}, u32[]{:S(2)}) collective-permute-start(bf16[48,2176]{1,0:T(8,128)(2,1)S(1)} %collective-permute-done.2.refs_3_), channel_id=1, source_target_pairs={{0,2},{2,0},{1,3},{3,1},{4,6},{6,4},{5,7},{7,5},{8,10},{10,8},{9,1... | collective-permute-start | bytes 626696 | tf_op jit(solution)/shard_map/ppermute | solution.py:132
  37.9 9.2 %collective-permute-start.13 = (bf16[48,2176]{1,0:T(8,128)(2,1)}, bf16[48,2176]{1,0:T(8,128)(2,1)}, u32[]{:S(2)}, u32[]{:S(2)}) collective-permute-start(bf16[48,2176]{1,0:T(8,128)(2,1)} %collective-permute-done.9.refs_10_), channel_id=1, source_target_pairs={{0,2},{2,0},{1,3},{3,1},{4,6},{6,4},{5,7},{7,5},{8,10},{10,8},{9,1... | collective-permute-start | bytes 626696 | tf_op jit(solution)/shard_map/ppermute | solution.py:132
  38.9 9.9 %collective-permute-start.29 = (bf16[48,2176]{1,0:T(8,128)(2,1)}, bf16[48,2176]{1,0:T(8,128)(2,1)}, u32[]{:S(2)}, u32[]{:S(2)}) collective-permute-start(bf16[48,2176]{1,0:T(8,128)(2,1)} %collective-permute-done.10.refs_11_), channel_id=1, source_target_pairs={{0,4},{4,0},{1,5},{5,1},{2,6},{6,2},{3,7},{7,3},{8,12},{12,8},{9,1... | collective-permute-start | bytes 626696 | tf_op jit(solution)/shard_map/ppermute | solution.py:130
  46.6 20.5 %collective-permute-start.24 = (bf16[48,2176]{1,0:T(8,128)(2,1)S(1)}, bf16[48,2176]{1,0:T(8,128)(2,1)S(1)}, u32[]{:S(2)}, u32[]{:S(2)}) collective-permute-start(bf16[48,2176]{1,0:T(8,128)(2,1)S(1)} %collective-permute-done.20.refs_2_), channel_id=1, source_target_pairs={{0,2},{2,0},{1,3},{3,1},{4,6},{6,4},{5,7},{7,5},{8,10},{10,8},{9,1... | collective-permute-start | bytes 626696 | tf_op jit(solution)/shard_map/ppermute | solution.py:132
  46.6 20.5 %collective-permute-start.31 = (bf16[48,2176]{1,0:T(8,128)(2,1)S(1)}, bf16[48,2176]{1,0:T(8,128)(2,1)S(1)}, u32[]{:S(2)}, u32[]{:S(2)}) collective-permute-start(bf16[48,2176]{1,0:T(8,128)(2,1)S(1)} %collective-permute-done.27.refs_9_), channel_id=1, source_target_pairs={{0,2},{2,0},{1,3},{3,1},{4,6},{6,4},{5,7},{7,5},{8,10},{10,8},{9,1... | collective-permute-start | bytes 626696 | tf_op jit(solution)/shard_map/ppermute | solution.py:132
  47.1 20.5 %collective-permute-start.25 = (bf16[48,2176]{1,0:T(8,128)(2,1)}, bf16[48,2176]{1,0:T(8,128)(2,1)S(1)}, u32[]{:S(2)}, u32[]{:S(2)}) collective-permute-start(bf16[48,2176]{1,0:T(8,128)(2,1)} %copy-done), channel_id=1, source_target_pairs={{0,2},{2,0},{1,3},{3,1},{4,6},{6,4},{5,7},{7,5},{8,10},{10,8},{9,1... | collective-permute-start | bytes 626696 | tf_op jit(solution)/shard_map/ppermute | solution.py:132
  48.8 18.8 %collective-permute-start.32 = (bf16[48,2176]{1,0:T(8,128)(2,1)}, bf16[48,2176]{1,0:T(8,128)(2,1)S(1)}, u32[]{:S(2)}, u32[]{:S(2)}) collective-permute-start(bf16[48,2176]{1,0:T(8,128)(2,1)} %collective-permute-done.28.refs_10_), channel_id=1, source_target_pairs={{0,2},{2,0},{1,3},{3,1},{4,6},{6,4},{5,7},{7,5},{8,10},{10,8},{9,1... | collective-permute-start | bytes 626696 | tf_op jit(solution)/shard_map/ppermute | solution.py:132
  48.8 18.7 %collective-permute-start.33 = (bf16[48,2176]{1,0:T(8,128)(2,1)}, bf16[48,2176]{1,0:T(8,128)(2,1)S(1)}, u32[]{:S(2)}, u32[]{:S(2)}) collective-permute-start(bf16[48,2176]{1,0:T(8,128)(2,1)} %collective-permute-done.29.refs_11_), channel_id=1, source_target_pairs={{0,2},{2,0},{1,3},{3,1},{4,6},{6,4},{5,7},{7,5},{8,10},{10,8},{9,1... | collective-permute-start | bytes 626696 | tf_op jit(solution)/shard_map/ppermute | solution.py:132
  67.0 16.6 %collective-permute-start.16 = (bf16[192,2048]{1,0:T(8,128)(2,1)}, bf16[192,2048]{1,0:T(8,128)(2,1)S(1)}, u32[]{:S(2)}, u32[]{:S(2)}) collective-permute-start(bf16[192,2048]{1,0:T(8,128)(2,1)} %get-tuple-element.16), channel_id=1, source_target_pairs={{0,2},{2,0},{1,3},{3,1},{4,6},{6,4},{5,7},{7,5},{8,10},{10,8},{9,1... | collective-permute-start | bytes 2359304 | tf_op jit(solution)/shard_map/ppermute | solution.py:132
  67.0 53.7 %collective-permute-start.15 = (bf16[192,2048]{1,0:T(8,128)(2,1)S(1)}, bf16[192,2048]{1,0:T(8,128)(2,1)S(1)}, u32[]{:S(2)}, u32[]{:S(2)}) collective-permute-start(bf16[192,2048]{1,0:T(8,128)(2,1)S(1)} %get-tuple-element.14), channel_id=1, source_target_pairs={{0,2},{2,0},{1,3},{3,1},{4,6},{6,4},{5,7},{7,5},{8,10},{10,8},{9,1... | collective-permute-start | bytes 2359304 | tf_op jit(solution)/shard_map/ppermute | solution.py:132
  84.0 38.7 %collective-permute-start.41 = (bf16[48,2048]{1,0:T(8,128)(2,1)S(1)}, bf16[48,2048]{1,0:T(8,128)(2,1)S(1)}, u32[]{:S(2)}, u32[]{:S(2)}) collective-permute-start(bf16[48,2048]{1,0:T(8,128)(2,1)S(1)} %get-tuple-element.33), channel_id=1, source_target_pairs={{0,1},{1,0},{2,3},{3,2},{4,5},{5,4},{6,7},{7,6},{8,9},{9,8},{10,11... | collective-permute-start | bytes 589832 | tf_op jit(solution)/shard_map/ppermute | solution.py:131
  84.4 48.7 %collective-permute-start.17 = (bf16[48,2048]{1,0:T(8,128)(2,1)S(1)}, bf16[48,2048]{1,0:T(8,128)(2,1)S(1)}, u32[]{:S(2)}, u32[]{:S(2)}) collective-permute-start(bf16[48,2048]{1,0:T(8,128)(2,1)S(1)} %get-tuple-element.32), channel_id=1, source_target_pairs={{0,1},{1,0},{2,3},{3,2},{4,5},{5,4},{6,7},{7,6},{8,9},{9,8},{10,11... | collective-permute-start | bytes 589832 | tf_op jit(solution)/shard_map/ppermute | solution.py:131
  87.1 13.1 %collective-permute-start.36 = (bf16[48,2048]{1,0:T(8,128)(2,1)S(1)}, bf16[48,2048]{1,0:T(8,128)(2,1)S(1)}, u32[]{:S(2)}, u32[]{:S(2)}) collective-permute-start(bf16[48,2048]{1,0:T(8,128)(2,1)S(1)} %get-tuple-element.34), channel_id=1, source_target_pairs={{0,1},{1,0},{2,3},{3,2},{4,5},{5,4},{6,7},{7,6},{8,9},{9,8},{10,11... | collective-permute-start | bytes 589832 | tf_op jit(solution)/shard_map/ppermute | solution.py:131
  87.6 16.0 %collective-permute-start.42 = (bf16[48,2048]{1,0:T(8,128)(2,1)S(1)}, bf16[48,2048]{1,0:T(8,128)(2,1)S(1)}, u32[]{:S(2)}, u32[]{:S(2)}) collective-permute-start(bf16[48,2048]{1,0:T(8,128)(2,1)S(1)} %get-tuple-element.36), channel_id=1, source_target_pairs={{0,1},{1,0},{2,3},{3,2},{4,5},{5,4},{6,7},{7,6},{8,9},{9,8},{10,11... | collective-permute-start | bytes 589832 | tf_op jit(solution)/shard_map/ppermute | solution.py:131
  100.3 12.1 %collective-permute-start.45 = (bf16[2,48,2048]{2,1,0:T(8,128)(2,1)S(1)}, bf16[2,48,2048]{2,1,0:T(8,128)(2,1)S(1)}, u32[]{:S(2)}, u32[]{:S(2)}) collective-permute-start(bf16[2,48,2048]{2,1,0:T(8,128)(2,1)S(1)} %pad_maximum_fusion.1), channel_id=1, source_target_pairs={{0,4},{4,0},{1,5},{5,1},{2,6},{6,2},{3,7},{7,3},{8,12},{12,8},{9,1... | collective-permute-start | bytes 1179656 | tf_op jit(solution)/shard_map/ppermute | solution.py:130
  103.6 16.6 %collective-permute-start.38 = (bf16[2,48,2048]{2,1,0:T(8,128)(2,1)S(1)}, bf16[2,48,2048]{2,1,0:T(8,128)(2,1)S(1)}, u32[]{:S(2)}, u32[]{:S(2)}) collective-permute-start(bf16[2,48,2048]{2,1,0:T(8,128)(2,1)S(1)} %pad_maximum_fusion), channel_id=1, source_target_pairs={{0,4},{4,0},{1,5},{5,1},{2,6},{6,2},{3,7},{7,3},{8,12},{12,8},{9,1... | collective-permute-start | bytes 1179656 | tf_op jit(solution)/shard_map/ppermute | solution.py:130
  112.3 12.1 %collective-permute-start.43 = (bf16[48,2048]{1,0:T(8,128)(2,1)S(1)}, bf16[48,2048]{1,0:T(8,128)(2,1)S(1)}, u32[]{:S(2)}, u32[]{:S(2)}) collective-permute-start(bf16[48,2048]{1,0:T(8,128)(2,1)S(1)} %get-tuple-element.22), channel_id=1, source_target_pairs={{0,4},{4,0},{1,5},{5,1},{2,6},{6,2},{3,7},{7,3},{8,12},{12,8},{9,1... | collective-permute-start | bytes 589832 | tf_op jit(solution)/shard_map/ppermute | solution.py:130
  122.7 10.5 %collective-permute-start.37 = (bf16[48,2048]{1,0:T(8,128)(2,1)S(1)}, bf16[48,2048]{1,0:T(8,128)(2,1)S(1)}, u32[]{:S(2)}, u32[]{:S(2)}) collective-permute-start(bf16[48,2048]{1,0:T(8,128)(2,1)S(1)} %get-tuple-element.21), channel_id=1, source_target_pairs={{0,4},{4,0},{1,5},{5,1},{2,6},{6,2},{3,7},{7,3},{8,12},{12,8},{9,1... | collective-permute-start | bytes 589832 | tf_op jit(solution)/shard_map/ppermute | solution.py:130
  128.4 8.9 %collective-permute-start.40 = (bf16[48,2048]{1,0:T(8,128)(2,1)S(1)}, bf16[48,2048]{1,0:T(8,128)(2,1)S(1)}, u32[]{:S(2)}, u32[]{:S(2)}) collective-permute-start(bf16[48,2048]{1,0:T(8,128)(2,1)S(1)} %get-tuple-element.23), channel_id=1, source_target_pairs={{0,24},{8,0},{16,8},{24,16},{1,25},{9,1},{17,9},{25,17},{2,26},{10... | collective-permute-start | bytes 589832 | tf_op jit(solution)/shard_map/ppermute | solution.py:133
  132.5 12.2 %collective-permute-start.44 = (bf16[48,2048]{1,0:T(8,128)(2,1)S(1)}, bf16[48,2048]{1,0:T(8,128)(2,1)S(1)}, u32[]{:S(2)}, u32[]{:S(2)}) collective-permute-start(bf16[48,2048]{1,0:T(8,128)(2,1)S(1)} %get-tuple-element.25), channel_id=1, source_target_pairs={{0,16},{8,24},{16,0},{24,8},{1,17},{9,25},{17,1},{25,9},{2,18},{10... | collective-permute-start | bytes 589832 | tf_op jit(solution)/shard_map/ppermute | solution.py:133
  132.5 12.2 %collective-permute-start.47 = (bf16[48,2048]{1,0:T(8,128)(2,1)S(1)}, bf16[48,2048]{1,0:T(8,128)(2,1)S(1)}, u32[]{:S(2)}, u32[]{:S(2)}) collective-permute-start(bf16[48,2048]{1,0:T(8,128)(2,1)S(1)} %get-tuple-element.24), channel_id=1, source_target_pairs={{0,8},{8,16},{16,24},{24,0},{1,9},{9,17},{17,25},{25,1},{2,10},{10... | collective-permute-start | bytes 589832 | tf_op jit(solution)/shard_map/ppermute | solution.py:133
  (22 other events, 116.4 us)

commit v2 on v0

v2 whole, which is shorter than its diff:
```python
import functools

import jax
import jax.numpy as jnp
from jax import lax
from jax.experimental import pallas as pl
from jax.experimental.pallas import tpu as pltpu
from jax.sharding import Mesh, PartitionSpec as P

BF = jnp.bfloat16
F32 = jnp.float32
NT = (((1,), (1,)), ((), ()))


UNITS = 8


def ffn_kernel(layout, cols, *refs):
    sc, refs = refs[0], refs[1:]
    pieces, (wg, wu, wd) = refs[:8], refs[8:11]
    outs, (x_s, h_s, w_s) = refs[11:15], refs[15:]
    rows = x_s.shape[0] // UNITS
    ff, d = wg.shape
    fb, nb = 256, 512
    mine = pl.multiple_of(sc[0] * cols, 128)
    other = pl.multiple_of((1 - sc[0]) * cols, 128)
    lane = lax.broadcasted_iota(jnp.int32, (rows, 128), 1)
    chosen = (lane == sc[1]) | (lane == sc[1] + 64)
    for b, (p, i, q, j) in enumerate(layout):
        r = pl.ds(b * rows, rows)
        x_s[r, pl.ds(mine, cols)] = pieces[p][i * rows : (i + 1) * rows, :cols]
        x_s[r, pl.ds(other, cols)] = pieces[q][j * rows : (j + 1) * rows, :cols]
        tail = pieces[p][i * rows : (i + 1) * rows, cols:].astype(F32)
        w_s[r, :] = jnp.broadcast_to(jnp.sum(jnp.where(chosen, tail, 0.0), axis=1, keepdims=True), (rows, 128))
    for f in range(0, ff, fb):
        x = x_s[...]
        g = lax.dot_general(x, wg[pl.ds(f, fb), :], NT, preferred_element_type=F32)
        u = lax.dot_general(x, wu[pl.ds(f, fb), :], NT, preferred_element_type=F32)
        h_s[:, pl.ds(f, fb)] = (g / (1.0 + jnp.exp(-g)) * u * w_s[:, :1]).astype(BF)
    for n in range(0, 2 * cols, nb):
        far = n >= cols
        off = n - cols if far else n
        at = pl.multiple_of((other if far else mine) + off, 128)
        o = jnp.dot(h_s[...], wd[:, pl.ds(at, nb)], preferred_element_type=F32).astype(BF)
        for b in range(UNITS):
            core, plane, side = b // 4, b // 2 % 2, b % 2
            sends, unit = (side, int(far)) if plane == 0 else (int(far), side)
            out = outs[(0 if sends else 2) + core]
            k = (plane * 2 + unit) * rows
            out[k : k + rows, off : off + nb] = o[b * rows : (b + 1) * rows]


def ffn(sc, pieces, layout, cols, wg, wu, wd):
    ff, d = wg.shape
    rows = pieces[0].shape[0] // 2
    total = UNITS * rows
    vmem = pl.BlockSpec(memory_space=pltpu.VMEM)
    return pl.pallas_call(
        functools.partial(ffn_kernel, layout, cols),
        in_specs=[pl.BlockSpec(memory_space=pltpu.SMEM)] + [vmem] * 11,
        out_specs=[vmem] * 4,
        out_shape=[pltpu.VMEM((4 * rows, cols), BF)] * 4,
        scratch_shapes=[
            pltpu.VMEM((total, d), BF),
            pltpu.VMEM((total, ff), BF),
            pltpu.VMEM((total, 128), F32),
        ],
        compiler_params=pltpu.CompilerParams(vmem_limit_bytes=16 << 20),
        cost_estimate=pl.CostEstimate(
            flops=6 * total * ff * d, bytes_accessed=4 * total * d, transcendentals=total * ff
        ),
        name="ffn",
    )(sc, *pieces, wg, wu, wd)


def dense_weights(expert_ids, combine_weights, experts):
    hits = expert_ids[:, :, None] == jnp.arange(experts, dtype=jnp.int32)
    return jnp.sum(jnp.where(hits, combine_weights[:, :, None], 0.0), axis=1)


def on_device(tokens, expert_ids, combine_weights, gate_proj, up_proj, down_proj):
    held, cols = tokens.shape
    nz, nx = lax.axis_size("z"), lax.axis_size("x")
    experts = nz * nx * 2
    z, x, c, y = (lax.axis_index(a) for a in ("z", "x", "c", "y"))
    sc = jnp.stack([y, (z * nx + x) * 2 + c]).astype(jnp.int32)
    weights = (gate_proj[0], up_proj[0], down_proj[0])

    swap = [(0, 1), (1, 0)]
    px = lambda a: lax.ppermute(a, "x", swap)
    py = lambda a: lax.ppermute(a, "y", swap)
    pc = lambda a: lax.ppermute(a, "c", swap)
    pz = lambda a, k: lax.ppermute(a, "z", [(i, i ^ k) for i in range(nz)])

    w = dense_weights(expert_ids, combine_weights, experts)
    hi = w.astype(BF)
    lo = (w - hi.astype(F32)).astype(BF)
    pad = jnp.zeros((held, 64 - experts), BF)
    t0 = jnp.concatenate([tokens, hi, pad, lo, pad], axis=1)

    t1, t3 = pz(t0, 1), pz(t0, 3)
    t2 = pz(t3, 1)

    def gather(a, b):
        ma, mb = jnp.concatenate([a, py(a)]), jnp.concatenate([b, px(b)])
        na, nb = px(ma), py(mb)
        return [ma, na, mb, nb, pc(ma), pc(na), pc(mb), pc(nb)]

    layout = []
    for core in (0, 4):
        layout += [(core, 0, core, 1), (core + 1, 0, core + 1, 1)]
        layout += [(core + 2, 0, core + 3, 0), (core + 2, 1, core + 3, 1)]

    def scatter(parts):
        send, send_c, keep, keep_c = parts
        s = (send.astype(F32) + pc(send_c).astype(F32)).astype(BF)
        k = (keep.astype(F32) + pc(keep_c).astype(F32)).reshape(4, held, cols)
        ra = px(s[: 2 * held]).astype(F32).reshape(2, held, cols)
        rb = py(s[2 * held :]).astype(F32).reshape(2, held, cols)
        back_a = py((k[1] + ra[1]).astype(BF)).astype(F32)
        back_b = px((k[3] + rb[1]).astype(BF)).astype(F32)
        return k[0] + ra[0] + back_a, k[2] + rb[0] + back_b

    first = ffn(sc, gather(t0, t1), layout, cols, *weights)
    last = ffn(sc, gather(t3, t2), layout, cols, *weights)
    u0, u1 = scatter(first)
    u3, u2 = scatter(last)
    total = u0 + pz(u1.astype(BF), 1).astype(F32)
    total = total + pz(u3.astype(BF), 3).astype(F32) + pz(u2.astype(BF), 2).astype(F32)
    return total.astype(BF)


def on_device_any(tokens, expert_ids, combine_weights, gate_proj, up_proj, down_proj):
    groups = lax.axis_size("exp")
    held, cols = tokens.shape
    local = gate_proj.shape[0]
    w = lax.all_gather(dense_weights(expert_ids, combine_weights, groups * local), "exp", axis=0, tiled=True)
    rows = lax.all_gather(lax.all_gather(tokens, "ten", axis=1, tiled=True), "exp", axis=0, tiled=True)
    total = jnp.zeros((rows.shape[0], rows.shape[1]), F32)
    for j in range(local):
        g = lax.dot_general(rows, gate_proj[j], NT, preferred_element_type=F32)
        u = lax.dot_general(rows, up_proj[j], NT, preferred_element_type=F32)
        mine = jnp.take(w, lax.axis_index("exp") * local + j, axis=1)[:, None]
        h = (jax.nn.silu(g) * u * mine).astype(BF)
        total = total + jnp.dot(h, down_proj[j], preferred_element_type=F32)
    part = lax.psum_scatter(total.astype(BF), "exp", scatter_dimension=0, tiled=True)
    return lax.psum_scatter(part, "ten", scatter_dimension=1, tiled=True).astype(BF)


def solution(mesh):
    sizes = (mesh.shape["exp"], mesh.shape["ten"])
    if sizes == (16, 2):
        mesh = Mesh(mesh.devices.reshape(4, 2, 2, 2), ("z", "x", "c", "y"))
        exp, ten, body = ("z", "x", "c"), "y", on_device
    else:
        exp, ten, body = "exp", "ten", on_device_any
    return jax.shard_map(
        body,
        mesh=mesh,
        in_specs=(
            P(exp, ten),
            P(exp, None),
            P(exp, None),
            P(exp, ten, None),
            P(exp, ten, None),
            P(exp, ten, None),
        ),
        out_specs=P(exp, ten),
        check_vma=False,
    )
```

time: 281 us -> 126 us (0.45)
  the two profiles are of different devices: /device:TPU:11 before, /device:TPU:0 now
where the time goes in v2:
time: 126 us
  waiting for transfers between devices  58.6 us (47%)
  starting transfers between devices  34.1 us (27%)
  Pallas kernels  18.3 us (15%)
  local copies, waits for them, and re-layouts  11.6 us (9%)
  other arithmetic  3.19 us (3%)
    ppermute x8, waiting for transfers between devices, on_device(): px = lambda a: lax.ppermute(a, 'x', swap)  31.8 us
    pallas_call x2, Pallas kernels, ffn(): pl.pallas_call(functools.partial(ffn_kernel, layout, cols), in_specs=[pl....  18.3 us
    ppermute x6, waiting for transfers between devices, on_device(): pz = lambda a, k: lax.ppermute(a, 'z', [(i, i ^ k) for i in range(nz)])  16.7 us
    ppermute x8, starting transfers between devices, on_device(): px = lambda a: lax.ppermute(a, 'x', swap)  11.6 us
    ppermute x6, starting transfers between devices, on_device(): pz = lambda a, k: lax.ppermute(a, 'z', [(i, i ^ k) for i in range(nz)])  11.4 us
    unnamed x19, local copies, waits for them, and re-layouts  10.2 us
    ppermute x8, waiting for transfers between devices, on_device(): py = lambda a: lax.ppermute(a, 'y', swap)  9.72 us
    ppermute x8, starting transfers between devices, on_device(): py = lambda a: lax.ppermute(a, 'y', swap)  8.91 us
  transfers between devices with their start and end apart: 34, of which 15 were waited for; matrix products, arithmetic and copies ran while one was open for 1% of the time, Pallas kernels for 15%

profile of v2, /device:TPU:0, one launch (start us, length us, event | category | flops | bytes accessed | tf_op | source)
XLA Modules:
  0.0 126.0 jit_solution(15911384621505948609)
XLA Ops:
  2.0 3.0 %collective-permute-start = (bf16[48,2176]{1,0:T(8,128)(2,1)S(1)}, bf16[48,2176]{1,0:T(8,128)(2,1)S(1)}, u32[]{:S(2)}, u32[]{:S(2)}) collective-permute-start(bf16[48,2176]{1,0:T(8,128)(2,1)S(1)} %concatenate.15), channel_id=1, source_target_pairs={{0,1},{1,0},{2,3},{3,2},{4,5},{5,4},{6,7},{7,6},{8,9},{9,8},{10,11... | collective-permute-start | bytes 626696 | tf_op jit(solution)/shard_map/ppermute | solution.py:91
  5.0 1.6 %collective-permute-start.2 = (bf16[48,2176]{1,0:T(8,128)(2,1)S(1)}, bf16[48,2176]{1,0:T(8,128)(2,1)S(1)}, u32[]{:S(2)}, u32[]{:S(2)}) collective-permute-start(bf16[48,2176]{1,0:T(8,128)(2,1)S(1)} %concatenate.15), channel_id=1, source_target_pairs={{0,8},{8,0},{16,24},{24,16},{1,9},{9,1},{17,25},{25,17},{2,10},{10... | collective-permute-start | bytes 626696 | tf_op jit(solution)/shard_map/ppermute | solution.py:93
  6.6 2.5 %collective-permute-start.16 = (bf16[48,2176]{1,0:T(8,128)(2,1)S(1)}, bf16[48,2176]{1,0:T(8,128)(2,1)S(1)}, u32[]{:S(2)}, u32[]{:S(2)}) collective-permute-start(bf16[48,2176]{1,0:T(8,128)(2,1)S(1)} %concatenate.15), channel_id=1, source_target_pairs={{0,24},{8,16},{16,8},{24,0},{1,25},{9,17},{17,9},{25,1},{2,26},{10... | collective-permute-start | bytes 626696 | tf_op jit(solution)/shard_map/ppermute | solution.py:93
  10.2 1.8 %collective-permute-start.1 = (bf16[96,2176]{1,0:T(8,128)(2,1)S(1)}, bf16[96,2176]{1,0:T(8,128)(2,1)S(1)}, u32[]{:S(2)}, u32[]{:S(2)}) collective-permute-start(bf16[96,2176]{1,0:T(8,128)(2,1)S(1)} %pad_maximum_fusion.refs_1_), channel_id=1, source_target_pairs={{0,4},{4,0},{1,5},{5,1},{2,6},{6,2},{3,7},{7,3},{8,12},{12,8},{9,1... | collective-permute-start | bytes 1253384 | tf_op jit(solution)/shard_map/ppermute | solution.py:90
  12.2 1.5 %collective-permute-start.3 = (bf16[48,2176]{1,0:T(8,128)(2,1)S(1)}, bf16[48,2176]{1,0:T(8,128)(2,1)S(1)}, u32[]{:S(2)}, u32[]{:S(2)}) collective-permute-start(bf16[48,2176]{1,0:T(8,128)(2,1)S(1)} %collective-permute-done.2), channel_id=1, source_target_pairs={{0,4},{4,0},{1,5},{5,1},{2,6},{6,2},{3,7},{7,3},{8,12},{12,8},{9,1... | collective-permute-start | bytes 626696 | tf_op jit(solution)/shard_map/ppermute | solution.py:90
  13.7 4.5 %collective-permute-done.16 = bf16[48,2176]{1,0:T(8,128)(2,1)S(1)} collective-permute-done((bf16[48,2176]{1,0:T(8,128)(2,1)S(1)}, bf16[48,2176]{1,0:T(8,128)(2,1)S(1)}, u32[]{:S(2)}, u32[]{:S(2)}) %collective-permute-start.16) | collective-permute-done | bytes 208928 | tf_op jit(solution)/shard_map/ppermute | solution.py:93
  19.3 6.2 %collective-permute-done.3 = bf16[48,2176]{1,0:T(8,128)(2,1)S(1)} collective-permute-done((bf16[48,2176]{1,0:T(8,128)(2,1)S(1)}, bf16[48,2176]{1,0:T(8,128)(2,1)S(1)}, u32[]{:S(2)}, u32[]{:S(2)}) %collective-permute-start.3) | collective-permute-done | bytes 208928 | tf_op jit(solution)/shard_map/ppermute | solution.py:90
  25.6 1.5 %collective-permute-start.4 = (bf16[96,2176]{1,0:T(8,128)(2,1)S(1)}, bf16[96,2176]{1,0:T(8,128)(2,1)S(1)}, u32[]{:S(2)}, u32[]{:S(2)}) collective-permute-start(bf16[96,2176]{1,0:T(8,128)(2,1)S(1)} %constant_dynamic-update-slice_fusion.refs_3_), channel_id=1, source_target_pairs={{0,1},{1,0},{2,3},{3,2},{4,5},{5,4},{6,7},{7,6},{8,9},{9,8},{10,11... | collective-permute-start | bytes 1253384 | tf_op jit(solution)/shard_map/ppermute | solution.py:91
  27.1 1.6 %collective-permute-start.20 = (bf16[48,2176]{1,0:T(8,128)(2,1)S(1)}, bf16[48,2176]{1,0:T(8,128)(2,1)S(1)}, u32[]{:S(2)}, u32[]{:S(2)}) collective-permute-start(bf16[48,2176]{1,0:T(8,128)(2,1)S(1)} %collective-permute-done.19), channel_id=1, source_target_pairs={{0,4},{4,0},{1,5},{5,1},{2,6},{6,2},{3,7},{7,3},{8,12},{12,8},{9,1... | collective-permute-start | bytes 626696 | tf_op jit(solution)/shard_map/ppermute | solution.py:90
  29.3 5.8 %collective-permute-done.20 = bf16[48,2176]{1,0:T(8,128)(2,1)S(1)} collective-permute-done((bf16[48,2176]{1,0:T(8,128)(2,1)S(1)}, bf16[48,2176]{1,0:T(8,128)(2,1)S(1)}, u32[]{:S(2)}, u32[]{:S(2)}) %collective-permute-start.20) | collective-permute-done | bytes 208928 | tf_op jit(solution)/shard_map/ppermute | solution.py:90
  37.2 6.6 %collective-permute-done.18.refs_2_ = bf16[96,2176]{1,0:T(8,128)(2,1)} collective-permute-done((bf16[96,2176]{1,0:T(8,128)(2,1)S(1)}, bf16[96,2176]{1,0:T(8,128)(2,1)}, u32[]{:S(2)}, u32[]{:S(2)}) %collective-permute-start.18) | collective-permute-done | bytes 417824 | tf_op jit(solution)/shard_map/ppermute | solution.py:90
  44.3 3.1 %collective-permute-done.21.refs_4_ = bf16[96,2176]{1,0:T(8,128)(2,1)} collective-permute-done((bf16[96,2176]{1,0:T(8,128)(2,1)S(1)}, bf16[96,2176]{1,0:T(8,128)(2,1)}, u32[]{:S(2)}, u32[]{:S(2)}) %collective-permute-start.21) | collective-permute-done | bytes 417824 | tf_op jit(solution)/shard_map/ppermute | solution.py:91
  47.4 2.8 %copy-done = bf16[1,768,4096]{2,1,0:T(8,128)(2,1)S(1)} copy-done((bf16[1,768,4096]{2,1,0:T(8,128)(2,1)S(1)}, bf16[1,768,4096]{2,1,0:T(8,128)(2,1)}, u32[]{:S(2)}) %copy-start) | copy-done | bytes 6291480
  50.2 2.8 %copy-done.2 = bf16[1,768,4096]{2,1,0:T(8,128)(2,1)S(1)} copy-done((bf16[1,768,4096]{2,1,0:T(8,128)(2,1)S(1)}, bf16[1,768,4096]{2,1,0:T(8,128)(2,1)}, u32[]{:S(2)}) %copy-start.2) | copy-done | bytes 6291480
  53.0 2.8 %copy-done.4 = bf16[1,768,4096]{2,1,0:T(8,128)(2,1)S(1)} copy-done((bf16[1,768,4096]{2,1,0:T(8,128)(2,1)S(1)}, bf16[1,768,4096]{2,1,0:T(8,128)(2,1)}, u32[]{:S(2)}) %copy-start.4) | copy-done | bytes 6291480
  56.8 9.2 %ffn.2 = (bf16[192,2048]{1,0:T(8,128)(2,1)S(1)}, bf16[192,2048]{1,0:T(8,128)(2,1)S(1)}, bf16[192,2048]{1,0:T(8,128)(2,1)S(1)}, bf16[192,2048]{1,0:T(8,128)(2,1)S(1)}) custom-call(s32[2]{0:T(128)S(1)} %pad_add_fusion.refs_0_, bf16[96,2176]{1,0:T(8,128)(2,1)S(1)} %pad_maximum_fusion.refs_1_, bf16[96,2176]{1,0:T(8,128)(2,1)S(1)} %collective-permute-done.1.refs_2_, ...), custom_call_target="tpu_custom_call" | custom-call | flops 7247757312 | bytes 6291456 | tf_op jit(solution)/shard_map/ffn/pallas_call | solution.py:58
  66.7 9.1 %ffn.3 = (bf16[192,2048]{1,0:T(8,128)(2,1)S(1)}, bf16[192,2048]{1,0:T(8,128)(2,1)S(1)}, bf16[192,2048]{1,0:T(8,128)(2,1)S(1)}, bf16[192,2048]{1,0:T(8,128)(2,1)S(1)}) custom-call(s32[2]{0:T(128)S(1)} %pad_add_fusion.refs_0_, bf16[96,2176]{1,0:T(8,128)(2,1)S(1)} %constant_dynamic-update-slice_fusion.2.refs_1_, ...), custom_call_target="tpu_custom_call" | custom-call | flops 7247757312 | bytes 6291456 | tf_op jit(solution)/shard_map/ffn/pallas_call | solution.py:58
  76.8 1.6 %collective-permute-start.11 = (bf16[96,2048]{1,0:T(8,128)(2,1)S(1)}, bf16[96,2048]{1,0:T(8,128)(2,1)S(1)}, u32[]{:S(2)}, u32[]{:S(2)}) collective-permute-start(bf16[96,2048]{1,0:T(8,128)(2,1)S(1)} %get-tuple-element.26), channel_id=1, source_target_pairs={{0,4},{4,0},{1,5},{5,1},{2,6},{6,2},{3,7},{7,3},{8,12},{12,8},{9,1... | collective-permute-start | bytes 1179656 | tf_op jit(solution)/shard_map/ppermute | solution.py:90
  79.7 1.6 %collective-permute-start.28 = (bf16[96,2048]{1,0:T(8,128)(2,1)S(1)}, bf16[96,2048]{1,0:T(8,128)(2,1)S(1)}, u32[]{:S(2)}, u32[]{:S(2)}) collective-permute-start(bf16[96,2048]{1,0:T(8,128)(2,1)S(1)} %get-tuple-element.27), channel_id=1, source_target_pairs={{0,4},{4,0},{1,5},{5,1},{2,6},{6,2},{3,7},{7,3},{8,12},{12,8},{9,1... | collective-permute-start | bytes 1179656 | tf_op jit(solution)/shard_map/ppermute | solution.py:90
  82.0 6.7 %collective-permute-done.11 = bf16[96,2048]{1,0:T(8,128)(2,1)S(1)} collective-permute-done((bf16[96,2048]{1,0:T(8,128)(2,1)S(1)}, bf16[96,2048]{1,0:T(8,128)(2,1)S(1)}, u32[]{:S(2)}, u32[]{:S(2)}) %collective-permute-start.11) | collective-permute-done | bytes 393248 | tf_op jit(solution)/shard_map/ppermute | solution.py:90
  88.8 1.5 %collective-permute-done.13 = bf16[96,2048]{1,0:T(8,128)(2,1)S(1)} collective-permute-done((bf16[96,2048]{1,0:T(8,128)(2,1)S(1)}, bf16[96,2048]{1,0:T(8,128)(2,1)S(1)}, u32[]{:S(2)}, u32[]{:S(2)}) %collective-permute-start.13) | collective-permute-done | bytes 393248 | tf_op jit(solution)/shard_map/ppermute | solution.py:91
  90.3 6.4 %collective-permute-done.28 = bf16[96,2048]{1,0:T(8,128)(2,1)S(1)} collective-permute-done((bf16[96,2048]{1,0:T(8,128)(2,1)S(1)}, bf16[96,2048]{1,0:T(8,128)(2,1)S(1)}, u32[]{:S(2)}, u32[]{:S(2)}) %collective-permute-start.28) | collective-permute-done | bytes 393248 | tf_op jit(solution)/shard_map/ppermute | solution.py:90
  97.6 1.5 %collective-permute-start.14 = (bf16[48,2048]{1,0:T(8,128)(2,1)S(1)}, bf16[48,2048]{1,0:T(8,128)(2,1)S(1)}, u32[]{:S(2)}, u32[]{:S(2)}) collective-permute-start(bf16[48,2048]{1,0:T(8,128)(2,1)S(1)} %get-tuple-element.22), channel_id=1, source_target_pairs={{0,4},{4,0},{1,5},{5,1},{2,6},{6,2},{3,7},{7,3},{8,12},{12,8},{9,1... | collective-permute-start | bytes 589832 | tf_op jit(solution)/shard_map/ppermute | solution.py:90
  99.0 1.5 %collective-permute-start.12 = (bf16[48,2048]{1,0:T(8,128)(2,1)S(1)}, bf16[48,2048]{1,0:T(8,128)(2,1)S(1)}, u32[]{:S(2)}, u32[]{:S(2)}) collective-permute-start(bf16[48,2048]{1,0:T(8,128)(2,1)S(1)} %get-tuple-element.21), channel_id=1, source_target_pairs={{0,1},{1,0},{2,3},{3,2},{4,5},{5,4},{6,7},{7,6},{8,9},{9,8},{10,11... | collective-permute-start | bytes 589832 | tf_op jit(solution)/shard_map/ppermute | solution.py:91
  100.6 4.1 %collective-permute-done.29 = bf16[48,2048]{1,0:T(8,128)(2,1)S(1)} collective-permute-done((bf16[48,2048]{1,0:T(8,128)(2,1)S(1)}, bf16[48,2048]{1,0:T(8,128)(2,1)S(1)}, u32[]{:S(2)}, u32[]{:S(2)}) %collective-permute-start.29) | collective-permute-done | bytes 196640 | tf_op jit(solution)/shard_map/ppermute | solution.py:91
  104.8 1.6 %collective-permute-start.32 = (bf16[48,2048]{1,0:T(8,128)(2,1)S(1)}, bf16[48,2048]{1,0:T(8,128)(2,1)S(1)}, u32[]{:S(2)}, u32[]{:S(2)}) collective-permute-start(bf16[48,2048]{1,0:T(8,128)(2,1)S(1)} %get-tuple-element.24), channel_id=1, source_target_pairs={{0,4},{4,0},{1,5},{5,1},{2,6},{6,2},{3,7},{7,3},{8,12},{12,8},{9,1... | collective-permute-start | bytes 589832 | tf_op jit(solution)/shard_map/ppermute | solution.py:90
  106.4 1.6 %collective-permute-start.15 = (bf16[48,2048]{1,0:T(8,128)(2,1)S(1)}, bf16[48,2048]{1,0:T(8,128)(2,1)S(1)}, u32[]{:S(2)}, u32[]{:S(2)}) collective-permute-start(bf16[48,2048]{1,0:T(8,128)(2,1)S(1)} %fusion.8), channel_id=1, source_target_pairs={{0,8},{8,0},{16,24},{24,16},{1,9},{9,1},{17,25},{25,17},{2,10},{10... | collective-permute-start | bytes 589832 | tf_op jit(solution)/shard_map/ppermute | solution.py:93
  108.1 2.5 %collective-permute-start.30 = (bf16[48,2048]{1,0:T(8,128)(2,1)S(1)}, bf16[48,2048]{1,0:T(8,128)(2,1)S(1)}, u32[]{:S(2)}, u32[]{:S(2)}) collective-permute-start(bf16[48,2048]{1,0:T(8,128)(2,1)S(1)} %get-tuple-element.23), channel_id=1, source_target_pairs={{0,24},{8,16},{16,8},{24,0},{1,25},{9,17},{17,9},{25,1},{2,26},{10... | collective-permute-start | bytes 589832 | tf_op jit(solution)/shard_map/ppermute | solution.py:93
  110.6 2.7 %collective-permute-start.33 = (bf16[48,2048]{1,0:T(8,128)(2,1)S(1)}, bf16[48,2048]{1,0:T(8,128)(2,1)S(1)}, u32[]{:S(2)}, u32[]{:S(2)}) collective-permute-start(bf16[48,2048]{1,0:T(8,128)(2,1)S(1)} %fusion.2), channel_id=1, source_target_pairs={{0,16},{8,24},{16,0},{24,8},{1,17},{9,25},{17,1},{25,9},{2,18},{10... | collective-permute-start | bytes 589832 | tf_op jit(solution)/shard_map/ppermute | solution.py:93
  113.3 1.7 %collective-permute-done.15 = bf16[48,2048]{1,0:T(8,128)(2,1)S(1)} collective-permute-done((bf16[48,2048]{1,0:T(8,128)(2,1)S(1)}, bf16[48,2048]{1,0:T(8,128)(2,1)S(1)}, u32[]{:S(2)}, u32[]{:S(2)}) %collective-permute-start.15) | collective-permute-done | bytes 196640 | tf_op jit(solution)/shard_map/ppermute | solution.py:93
  115.0 3.9 %collective-permute-done.30 = bf16[48,2048]{1,0:T(8,128)(2,1)S(1)} collective-permute-done((bf16[48,2048]{1,0:T(8,128)(2,1)S(1)}, bf16[48,2048]{1,0:T(8,128)(2,1)S(1)}, u32[]{:S(2)}, u32[]{:S(2)}) %collective-permute-start.30) | collective-permute-done | bytes 196640 | tf_op jit(solution)/shard_map/ppermute | solution.py:93
  118.8 6.4 %collective-permute-done.33 = bf16[48,2048]{1,0:T(8,128)(2,1)S(1)} collective-permute-done((bf16[48,2048]{1,0:T(8,128)(2,1)S(1)}, bf16[48,2048]{1,0:T(8,128)(2,1)S(1)}, u32[]{:S(2)}, u32[]{:S(2)}) %collective-permute-start.33) | collective-permute-done | bytes 196640 | tf_op jit(solution)/shard_map/ppermute | solution.py:93
  (85 shorter events, 14.4 us)
Async XLA Ops:
  2.0 8.2 %collective-permute-start = (bf16[48,2176]{1,0:T(8,128)(2,1)S(1)}, bf16[48,2176]{1,0:T(8,128)(2,1)S(1)}, u32[]{:S(2)}, u32[]{:S(2)}) collective-permute-start(bf16[48,2176]{1,0:T(8,128)(2,1)S(1)} %concatenate.15), channel_id=1, source_target_pairs={{0,1},{1,0},{2,3},{3,2},{4,5},{5,4},{6,7},{7,6},{8,9},{9,8},{10,11... | collective-permute-start | bytes 626696 | tf_op jit(solution)/shard_map/ppermute | solution.py:91
  5.0 7.2 %collective-permute-start.2 = (bf16[48,2176]{1,0:T(8,128)(2,1)S(1)}, bf16[48,2176]{1,0:T(8,128)(2,1)S(1)}, u32[]{:S(2)}, u32[]{:S(2)}) collective-permute-start(bf16[48,2176]{1,0:T(8,128)(2,1)S(1)} %concatenate.15), channel_id=1, source_target_pairs={{0,8},{8,0},{16,24},{24,16},{1,9},{9,1},{17,25},{25,17},{2,10},{10... | collective-permute-start | bytes 626696 | tf_op jit(solution)/shard_map/ppermute | solution.py:93
  6.6 11.7 %collective-permute-start.16 = (bf16[48,2176]{1,0:T(8,128)(2,1)S(1)}, bf16[48,2176]{1,0:T(8,128)(2,1)S(1)}, u32[]{:S(2)}, u32[]{:S(2)}) collective-permute-start(bf16[48,2176]{1,0:T(8,128)(2,1)S(1)} %concatenate.15), channel_id=1, source_target_pairs={{0,24},{8,16},{16,8},{24,0},{1,25},{9,17},{17,9},{25,1},{2,26},{10... | collective-permute-start | bytes 626696 | tf_op jit(solution)/shard_map/ppermute | solution.py:93
  10.2 18.5 %collective-permute-start.1 = (bf16[96,2176]{1,0:T(8,128)(2,1)S(1)}, bf16[96,2176]{1,0:T(8,128)(2,1)S(1)}, u32[]{:S(2)}, u32[]{:S(2)}) collective-permute-start(bf16[96,2176]{1,0:T(8,128)(2,1)S(1)} %pad_maximum_fusion.refs_1_), channel_id=1, source_target_pairs={{0,4},{4,0},{1,5},{5,1},{2,6},{6,2},{3,7},{7,3},{8,12},{12,8},{9,1... | collective-permute-start | bytes 1253384 | tf_op jit(solution)/shard_map/ppermute | solution.py:90
  12.0 23.2 %collective-permute-start.5 = (bf16[96,2176]{1,0:T(8,128)(2,1)S(1)}, bf16[96,2176]{1,0:T(8,128)(2,1)S(1)}, u32[]{:S(2)}, u32[]{:S(2)}) collective-permute-start(bf16[96,2176]{1,0:T(8,128)(2,1)S(1)} %pad_maximum_fusion.refs_1_), channel_id=1, source_target_pairs={{0,2},{2,0},{1,3},{3,1},{4,6},{6,4},{5,7},{7,5},{8,10},{10,8},{9,1... | collective-permute-start | bytes 1253384 | tf_op jit(solution)/shard_map/ppermute | solution.py:92
  12.2 13.4 %collective-permute-start.3 = (bf16[48,2176]{1,0:T(8,128)(2,1)S(1)}, bf16[48,2176]{1,0:T(8,128)(2,1)S(1)}, u32[]{:S(2)}, u32[]{:S(2)}) collective-permute-start(bf16[48,2176]{1,0:T(8,128)(2,1)S(1)} %collective-permute-done.2), channel_id=1, source_target_pairs={{0,4},{4,0},{1,5},{5,1},{2,6},{6,2},{3,7},{7,3},{8,12},{12,8},{9,1... | collective-permute-start | bytes 626696 | tf_op jit(solution)/shard_map/ppermute | solution.py:90
  18.2 8.9 %collective-permute-start.19 = (bf16[48,2176]{1,0:T(8,128)(2,1)S(1)}, bf16[48,2176]{1,0:T(8,128)(2,1)S(1)}, u32[]{:S(2)}, u32[]{:S(2)}) collective-permute-start(bf16[48,2176]{1,0:T(8,128)(2,1)S(1)} %collective-permute-done.16), channel_id=1, source_target_pairs={{0,8},{8,0},{16,24},{24,16},{1,9},{9,1},{17,25},{25,17},{2,10},{10... | collective-permute-start | bytes 626696 | tf_op jit(solution)/shard_map/ppermute | solution.py:93
  18.8 8.3 %collective-permute-start.17 = (bf16[48,2176]{1,0:T(8,128)(2,1)S(1)}, bf16[48,2176]{1,0:T(8,128)(2,1)S(1)}, u32[]{:S(2)}, u32[]{:S(2)}) collective-permute-start(bf16[48,2176]{1,0:T(8,128)(2,1)S(1)} %collective-permute-done.16), channel_id=1, source_target_pairs={{0,1},{1,0},{2,3},{3,2},{4,5},{5,4},{6,7},{7,6},{8,9},{9,8},{10,11... | collective-permute-start | bytes 626696 | tf_op jit(solution)/shard_map/ppermute | solution.py:91
  25.6 10.3 %collective-permute-start.4 = (bf16[96,2176]{1,0:T(8,128)(2,1)S(1)}, bf16[96,2176]{1,0:T(8,128)(2,1)S(1)}, u32[]{:S(2)}, u32[]{:S(2)}) collective-permute-start(bf16[96,2176]{1,0:T(8,128)(2,1)S(1)} %constant_dynamic-update-slice_fusion.refs_3_), channel_id=1, source_target_pairs={{0,1},{1,0},{2,3},{3,2},{4,5},{5,4},{6,7},{7,6},{8,9},{9,8},{10,11... | collective-permute-start | bytes 1253384 | tf_op jit(solution)/shard_map/ppermute | solution.py:91
  27.1 9.8 %collective-permute-start.7 = (bf16[96,2176]{1,0:T(8,128)(2,1)S(1)}, bf16[96,2176]{1,0:T(8,128)(2,1)}, u32[]{:S(2)}, u32[]{:S(2)}) collective-permute-start(bf16[96,2176]{1,0:T(8,128)(2,1)S(1)} %constant_dynamic-update-slice_fusion.refs_3_), channel_id=1, source_target_pairs={{0,2},{2,0},{1,3},{3,1},{4,6},{6,4},{5,7},{7,5},{8,10},{10,8},{9,1... | collective-permute-start | bytes 1253384 | tf_op jit(solution)/shard_map/ppermute | solution.py:92
  27.1 8.0 %collective-permute-start.20 = (bf16[48,2176]{1,0:T(8,128)(2,1)S(1)}, bf16[48,2176]{1,0:T(8,128)(2,1)S(1)}, u32[]{:S(2)}, u32[]{:S(2)}) collective-permute-start(bf16[48,2176]{1,0:T(8,128)(2,1)S(1)} %collective-permute-done.19), channel_id=1, source_target_pairs={{0,4},{4,0},{1,5},{5,1},{2,6},{6,2},{3,7},{7,3},{8,12},{12,8},{9,1... | collective-permute-start | bytes 626696 | tf_op jit(solution)/shard_map/ppermute | solution.py:90
  28.7 15.1 %collective-permute-start.18 = (bf16[96,2176]{1,0:T(8,128)(2,1)S(1)}, bf16[96,2176]{1,0:T(8,128)(2,1)}, u32[]{:S(2)}, u32[]{:S(2)}) collective-permute-start(bf16[96,2176]{1,0:T(8,128)(2,1)S(1)} %constant_dynamic-update-slice_fusion.2.refs_1_), channel_id=1, source_target_pairs={{0,4},{4,0},{1,5},{5,1},{2,6},{6,2},{3,7},{7,3},{8,12},{12,8},{9,1... | collective-permute-start | bytes 1253384 | tf_op jit(solution)/shard_map/ppermute | solution.py:90
  35.1 8.7 %collective-permute-start.6 = (bf16[96,2176]{1,0:T(8,128)(2,1)S(1)}, bf16[96,2176]{1,0:T(8,128)(2,1)}, u32[]{:S(2)}, u32[]{:S(2)}) collective-permute-start(bf16[96,2176]{1,0:T(8,128)(2,1)S(1)} %collective-permute-done.1.refs_2_), channel_id=1, source_target_pairs={{0,2},{2,0},{1,3},{3,1},{4,6},{6,4},{5,7},{7,5},{8,10},{10,8},{9,1... | collective-permute-start | bytes 1253384 | tf_op jit(solution)/shard_map/ppermute | solution.py:92
  35.2 12.2 %collective-permute-start.21 = (bf16[96,2176]{1,0:T(8,128)(2,1)S(1)}, bf16[96,2176]{1,0:T(8,128)(2,1)}, u32[]{:S(2)}, u32[]{:S(2)}) collective-permute-start(bf16[96,2176]{1,0:T(8,128)(2,1)S(1)} %constant_dynamic-update-slice_fusion.4.refs_3_), channel_id=1, source_target_pairs={{0,1},{1,0},{2,3},{3,2},{4,5},{5,4},{6,7},{7,6},{8,9},{9,8},{10,11... | collective-permute-start | bytes 1253384 | tf_op jit(solution)/shard_map/ppermute | solution.py:91
  35.8 11.6 %collective-permute-start.8 = (bf16[96,2176]{1,0:T(8,128)(2,1)S(1)}, bf16[96,2176]{1,0:T(8,128)(2,1)}, u32[]{:S(2)}, u32[]{:S(2)}) collective-permute-start(bf16[96,2176]{1,0:T(8,128)(2,1)S(1)} %collective-permute-done.4.refs_4_), channel_id=1, source_target_pairs={{0,2},{2,0},{1,3},{3,1},{4,6},{6,4},{5,7},{7,5},{8,10},{10,8},{9,1... | collective-permute-start | bytes 1253384 | tf_op jit(solution)/shard_map/ppermute | solution.py:92
  36.9 29.6 %collective-permute-start.22 = (bf16[96,2176]{1,0:T(8,128)(2,1)S(1)}, bf16[96,2176]{1,0:T(8,128)(2,1)S(1)}, u32[]{:S(2)}, u32[]{:S(2)}) collective-permute-start(bf16[96,2176]{1,0:T(8,128)(2,1)S(1)} %constant_dynamic-update-slice_fusion.2.refs_1_), channel_id=1, source_target_pairs={{0,2},{2,0},{1,3},{3,1},{4,6},{6,4},{5,7},{7,5},{8,10},{10,8},{9,1... | collective-permute-start | bytes 1253384 | tf_op jit(solution)/shard_map/ppermute | solution.py:92
  43.8 22.8 %collective-permute-start.24 = (bf16[96,2176]{1,0:T(8,128)(2,1)S(1)}, bf16[96,2176]{1,0:T(8,128)(2,1)S(1)}, u32[]{:S(2)}, u32[]{:S(2)}) collective-permute-start(bf16[96,2176]{1,0:T(8,128)(2,1)S(1)} %constant_dynamic-update-slice_fusion.4.refs_3_), channel_id=1, source_target_pairs={{0,2},{2,0},{1,3},{3,1},{4,6},{6,4},{5,7},{7,5},{8,10},{10,8},{9,1... | collective-permute-start | bytes 1253384 | tf_op jit(solution)/shard_map/ppermute | solution.py:92
  43.8 22.8 %collective-permute-start.23 = (bf16[96,2176]{1,0:T(8,128)(2,1)}, bf16[96,2176]{1,0:T(8,128)(2,1)S(1)}, u32[]{:S(2)}, u32[]{:S(2)}) collective-permute-start(bf16[96,2176]{1,0:T(8,128)(2,1)} %collective-permute-done.18.refs_2_), channel_id=1, source_target_pairs={{0,2},{2,0},{1,3},{3,1},{4,6},{6,4},{5,7},{7,5},{8,10},{10,8},{9,1... | collective-permute-start | bytes 1253384 | tf_op jit(solution)/shard_map/ppermute | solution.py:92
  47.4 19.3 %collective-permute-start.25 = (bf16[96,2176]{1,0:T(8,128)(2,1)}, bf16[96,2176]{1,0:T(8,128)(2,1)S(1)}, u32[]{:S(2)}, u32[]{:S(2)}) collective-permute-start(bf16[96,2176]{1,0:T(8,128)(2,1)} %collective-permute-done.21.refs_4_), channel_id=1, source_target_pairs={{0,2},{2,0},{1,3},{3,1},{4,6},{6,4},{5,7},{7,5},{8,10},{10,8},{9,1... | collective-permute-start | bytes 1253384 | tf_op jit(solution)/shard_map/ppermute | solution.py:92
  66.0 10.4 %collective-permute-start.10 = (bf16[192,2048]{1,0:T(8,128)(2,1)S(1)}, bf16[192,2048]{1,0:T(8,128)(2,1)S(1)}, u32[]{:S(2)}, u32[]{:S(2)}) collective-permute-start(bf16[192,2048]{1,0:T(8,128)(2,1)S(1)} %get-tuple-element.16), channel_id=1, source_target_pairs={{0,2},{2,0},{1,3},{3,1},{4,6},{6,4},{5,7},{7,5},{8,10},{10,8},{9,1... | collective-permute-start | bytes 2359304 | tf_op jit(solution)/shard_map/ppermute | solution.py:92
  66.6 12.3 %collective-permute-start.9 = (bf16[192,2048]{1,0:T(8,128)(2,1)S(1)}, bf16[192,2048]{1,0:T(8,128)(2,1)S(1)}, u32[]{:S(2)}, u32[]{:S(2)}) collective-permute-start(bf16[192,2048]{1,0:T(8,128)(2,1)S(1)} %get-tuple-element.14), channel_id=1, source_target_pairs={{0,2},{2,0},{1,3},{3,1},{4,6},{6,4},{5,7},{7,5},{8,10},{10,8},{9,1... | collective-permute-start | bytes 2359304 | tf_op jit(solution)/shard_map/ppermute | solution.py:92
  75.8 6.0 %collective-permute-start.26 = (bf16[192,2048]{1,0:T(8,128)(2,1)S(1)}, bf16[192,2048]{1,0:T(8,128)(2,1)S(1)}, u32[]{:S(2)}, u32[]{:S(2)}) collective-permute-start(bf16[192,2048]{1,0:T(8,128)(2,1)S(1)} %get-tuple-element.18), channel_id=1, source_target_pairs={{0,2},{2,0},{1,3},{3,1},{4,6},{6,4},{5,7},{7,5},{8,10},{10,8},{9,1... | collective-permute-start | bytes 2359304 | tf_op jit(solution)/shard_map/ppermute | solution.py:92
  76.8 12.0 %collective-permute-start.11 = (bf16[96,2048]{1,0:T(8,128)(2,1)S(1)}, bf16[96,2048]{1,0:T(8,128)(2,1)S(1)}, u32[]{:S(2)}, u32[]{:S(2)}) collective-permute-start(bf16[96,2048]{1,0:T(8,128)(2,1)S(1)} %get-tuple-element.26), channel_id=1, source_target_pairs={{0,4},{4,0},{1,5},{5,1},{2,6},{6,2},{3,7},{7,3},{8,12},{12,8},{9,1... | collective-permute-start | bytes 1179656 | tf_op jit(solution)/shard_map/ppermute | solution.py:90
  78.3 12.0 %collective-permute-start.13 = (bf16[96,2048]{1,0:T(8,128)(2,1)S(1)}, bf16[96,2048]{1,0:T(8,128)(2,1)S(1)}, u32[]{:S(2)}, u32[]{:S(2)}) collective-permute-start(bf16[96,2048]{1,0:T(8,128)(2,1)S(1)} %get-tuple-element.25), channel_id=1, source_target_pairs={{0,1},{1,0},{2,3},{3,2},{4,5},{5,4},{6,7},{7,6},{8,9},{9,8},{10,11... | collective-permute-start | bytes 1179656 | tf_op jit(solution)/shard_map/ppermute | solution.py:91
  79.7 17.0 %collective-permute-start.28 = (bf16[96,2048]{1,0:T(8,128)(2,1)S(1)}, bf16[96,2048]{1,0:T(8,128)(2,1)S(1)}, u32[]{:S(2)}, u32[]{:S(2)}) collective-permute-start(bf16[96,2048]{1,0:T(8,128)(2,1)S(1)} %get-tuple-element.27), channel_id=1, source_target_pairs={{0,4},{4,0},{1,5},{5,1},{2,6},{6,2},{3,7},{7,3},{8,12},{12,8},{9,1... | collective-permute-start | bytes 1179656 | tf_op jit(solution)/shard_map/ppermute | solution.py:90
  81.3 19.3 %collective-permute-start.31 = (bf16[96,2048]{1,0:T(8,128)(2,1)S(1)}, bf16[96,2048]{1,0:T(8,128)(2,1)S(1)}, u32[]{:S(2)}, u32[]{:S(2)}) collective-permute-start(bf16[96,2048]{1,0:T(8,128)(2,1)S(1)} %get-tuple-element.28), channel_id=1, source_target_pairs={{0,1},{1,0},{2,3},{3,2},{4,5},{5,4},{6,7},{7,6},{8,9},{9,8},{10,11... | collective-permute-start | bytes 1179656 | tf_op jit(solution)/shard_map/ppermute | solution.py:91
  96.8 7.9 %collective-permute-start.29 = (bf16[48,2048]{1,0:T(8,128)(2,1)S(1)}, bf16[48,2048]{1,0:T(8,128)(2,1)S(1)}, u32[]{:S(2)}, u32[]{:S(2)}) collective-permute-start(bf16[48,2048]{1,0:T(8,128)(2,1)S(1)} %fusion.3), channel_id=1, source_target_pairs={{0,1},{1,0},{2,3},{3,2},{4,5},{5,4},{6,7},{7,6},{8,9},{9,8},{10,11... | collective-permute-start | bytes 589832 | tf_op jit(solution)/shard_map/ppermute | solution.py:91
  97.6 8.8 %collective-permute-start.14 = (bf16[48,2048]{1,0:T(8,128)(2,1)S(1)}, bf16[48,2048]{1,0:T(8,128)(2,1)S(1)}, u32[]{:S(2)}, u32[]{:S(2)}) collective-permute-start(bf16[48,2048]{1,0:T(8,128)(2,1)S(1)} %get-tuple-element.22), channel_id=1, source_target_pairs={{0,4},{4,0},{1,5},{5,1},{2,6},{6,2},{3,7},{7,3},{8,12},{12,8},{9,1... | collective-permute-start | bytes 589832 | tf_op jit(solution)/shard_map/ppermute | solution.py:90
  99.0 14.2 %collective-permute-start.12 = (bf16[48,2048]{1,0:T(8,128)(2,1)S(1)}, bf16[48,2048]{1,0:T(8,128)(2,1)S(1)}, u32[]{:S(2)}, u32[]{:S(2)}) collective-permute-start(bf16[48,2048]{1,0:T(8,128)(2,1)S(1)} %get-tuple-element.21), channel_id=1, source_target_pairs={{0,1},{1,0},{2,3},{3,2},{4,5},{5,4},{6,7},{7,6},{8,9},{9,8},{10,11... | collective-permute-start | bytes 589832 | tf_op jit(solution)/shard_map/ppermute | solution.py:91
  106.4 8.5 %collective-permute-start.15 = (bf16[48,2048]{1,0:T(8,128)(2,1)S(1)}, bf16[48,2048]{1,0:T(8,128)(2,1)S(1)}, u32[]{:S(2)}, u32[]{:S(2)}) collective-permute-start(bf16[48,2048]{1,0:T(8,128)(2,1)S(1)} %fusion.8), channel_id=1, source_target_pairs={{0,8},{8,0},{16,24},{24,16},{1,9},{9,1},{17,25},{25,17},{2,10},{10... | collective-permute-start | bytes 589832 | tf_op jit(solution)/shard_map/ppermute | solution.py:93
  108.1 10.8 %collective-permute-start.30 = (bf16[48,2048]{1,0:T(8,128)(2,1)S(1)}, bf16[48,2048]{1,0:T(8,128)(2,1)S(1)}, u32[]{:S(2)}, u32[]{:S(2)}) collective-permute-start(bf16[48,2048]{1,0:T(8,128)(2,1)S(1)} %get-tuple-element.23), channel_id=1, source_target_pairs={{0,24},{8,16},{16,8},{24,0},{1,25},{9,17},{17,9},{25,1},{2,26},{10... | collective-permute-start | bytes 589832 | tf_op jit(solution)/shard_map/ppermute | solution.py:93
  110.6 14.6 %collective-permute-start.33 = (bf16[48,2048]{1,0:T(8,128)(2,1)S(1)}, bf16[48,2048]{1,0:T(8,128)(2,1)S(1)}, u32[]{:S(2)}, u32[]{:S(2)}) collective-permute-start(bf16[48,2048]{1,0:T(8,128)(2,1)S(1)} %fusion.2), channel_id=1, source_target_pairs={{0,16},{8,24},{16,0},{24,8},{1,17},{9,25},{17,1},{25,9},{2,18},{10... | collective-permute-start | bytes 589832 | tf_op jit(solution)/shard_map/ppermute | solution.py:93
  (10 other events, 48.6 us)

commit v3 on v2

--- a/solution.py
+++ b/solution.py
@@ -12,16 +12,33 @@
 NT = (((1,), (1,)), ((), ()))
 
 
+STEPS = 3
 UNITS = 8
 
 
-def ffn_kernel(layout, cols, *refs):
+def ffn_kernel(layout, cols, fresh, waits, *refs):
+    refs = refs[waits:]
     sc, refs = refs[0], refs[1:]
-    pieces, (wg, wu, wd) = refs[:8], refs[8:11]
-    outs, (x_s, h_s, w_s) = refs[11:15], refs[15:]
+    pieces, given, outs, refs = refs[:8], refs[8:11], refs[11:15], refs[15:]
+    held = given
+    if fresh:
+        held, refs = refs[:3], refs[3:]
+    wg, wu, wd = held
+    x_s, h_s, w_s = refs[:3]
     rows = x_s.shape[0] // UNITS
     ff, d = wg.shape
-    fb, nb = 256, 512
+    fb, nb = ff // STEPS, 512
+
+    def stream(k, step):
+        part = pl.ds(step * fb, fb)
+        return pltpu.make_async_copy(given[k].at[part], held[k].at[part], refs[3].at[k * STEPS + step])
+
+    if fresh:
+        for step in range(STEPS):
+            stream(0, step).start()
+            stream(1, step).start()
+        for step in range(STEPS):
+            stream(2, step).start()
     mine = pl.multiple_of(sc[0] * cols, 128)
     other = pl.multiple_of((1 - sc[0]) * cols, 128)
     lane = lax.broadcasted_iota(jnp.int32, (rows, 128), 1)
@@ -32,45 +49,59 @@
         x_s[r, pl.ds(other, cols)] = pieces[q][j * rows : (j + 1) * rows, :cols]
         tail = pieces[p][i * rows : (i + 1) * rows, cols:].astype(F32)
         w_s[r, :] = jnp.broadcast_to(jnp.sum(jnp.where(chosen, tail, 0.0), axis=1, keepdims=True), (rows, 128))
-    for f in range(0, ff, fb):
+    for step in range(STEPS):
+        f = step * fb
+        if fresh:
+            stream(0, step).wait()
+            stream(1, step).wait()
         x = x_s[...]
         g = lax.dot_general(x, wg[pl.ds(f, fb), :], NT, preferred_element_type=F32)
         u = lax.dot_general(x, wu[pl.ds(f, fb), :], NT, preferred_element_type=F32)
         h_s[:, pl.ds(f, fb)] = (g / (1.0 + jnp.exp(-g)) * u * w_s[:, :1]).astype(BF)
+    if fresh:
+        for step in range(STEPS):
+            stream(2, step).wait()
     for n in range(0, 2 * cols, nb):
-        far = n >= cols
+        far = int(n >= cols)
         off = n - cols if far else n
         at = pl.multiple_of((other if far else mine) + off, 128)
         o = jnp.dot(h_s[...], wd[:, pl.ds(at, nb)], preferred_element_type=F32).astype(BF)
         for b in range(UNITS):
             core, plane, side = b // 4, b // 2 % 2, b % 2
-            sends, unit = (side, int(far)) if plane == 0 else (int(far), side)
-            out = outs[(0 if sends else 2) + core]
-            k = (plane * 2 + unit) * rows
-            out[k : k + rows, off : off + nb] = o[b * rows : (b + 1) * rows]
-
-
-def ffn(sc, pieces, layout, cols, wg, wu, wd):
-    ff, d = wg.shape
-    rows = pieces[0].shape[0] // 2
-    total = UNITS * rows
+            if side and far:
+                group, unit = 0, plane
+            elif side != far:
+                group, unit = (0, 2 + plane) if side != plane else (2, plane)
+            else:
+                group, unit = 2, 2 + plane
+            k = unit * rows
+            outs[group + core][k : k + rows, off : off + nb] = o[b * rows : (b + 1) * rows]
+
+
+def ffn(sc, pieces, layout, cols, weights, fresh, first_of_all):
+    ff, d = weights[0].shape
+    total = len(layout) * pieces[1].shape[0]
     vmem = pl.BlockSpec(memory_space=pltpu.VMEM)
+    out = [pltpu.VMEM((total // 2, cols), BF)] * 4
+    scratch = [pltpu.VMEM((total, d), BF), pltpu.VMEM((total, ff), BF), pltpu.VMEM((total, 128), F32)]
+    if fresh:
+        out += [pltpu.VMEM(a.shape, BF) for a in weights]
+        scratch.append(pltpu.SemaphoreType.DMA((3 * STEPS,)))
     return pl.pallas_call(
-        functools.partial(ffn_kernel, layout, cols),
-        in_specs=[pl.BlockSpec(memory_space=pltpu.SMEM)] + [vmem] * 11,
-        out_specs=[vmem] * 4,
-        out_shape=[pltpu.VMEM((4 * rows, cols), BF)] * 4,
-        scratch_shapes=[
-            pltpu.VMEM((total, d), BF),
-            pltpu.VMEM((total, ff), BF),
-            pltpu.VMEM((total, 128), F32),
-        ],
-        compiler_params=pltpu.CompilerParams(vmem_limit_bytes=16 << 20),
+        functools.partial(ffn_kernel, layout, cols, fresh, len(first_of_all)),
+        in_specs=[pl.BlockSpec(memory_space=pl.ANY)] * len(first_of_all)
+        + [pl.BlockSpec(memory_space=pltpu.SMEM)]
+        + [vmem] * 8
+        + [pl.BlockSpec(memory_space=pltpu.HBM) if fresh else vmem] * 3,
+        out_specs=[vmem] * len(out),
+        out_shape=out,
+        scratch_shapes=scratch,
+        compiler_params=pltpu.CompilerParams(vmem_limit_bytes=(36 if fresh else 8) << 20),
         cost_estimate=pl.CostEstimate(
-            flops=6 * total * ff * d, bytes_accessed=4 * total * d, transcendentals=total * ff
+            flops=6 * total * ff * d, bytes_accessed=6 * ff * d + 4 * total * d, transcendentals=total * ff
         ),
         name="ffn",
-    )(sc, *pieces, wg, wu, wd)
+    )(*first_of_all, sc, *pieces, *weights)
 
 
 def dense_weights(expert_ids, combine_weights, experts):
@@ -102,31 +133,37 @@
     t2 = pz(t3, 1)
 
     def gather(a, b):
-        ma, mb = jnp.concatenate([a, py(a)]), jnp.concatenate([b, px(b)])
-        na, nb = px(ma), py(mb)
-        return [ma, na, mb, nb, pc(ma), pc(na), pc(mb), pc(nb)]
+        xa, yb, ya, xb = px(a), py(b), py(a), px(b)
+        da, db = py(xa), px(yb)
+        return [jnp.concatenate([a, xa, ya]), da, jnp.concatenate([b, xb, yb]), db]
 
     layout = []
     for core in (0, 4):
-        layout += [(core, 0, core, 1), (core + 1, 0, core + 1, 1)]
-        layout += [(core + 2, 0, core + 3, 0), (core + 2, 1, core + 3, 1)]
-
-    def scatter(parts):
+        for plane in (core, core + 2):
+            layout += [(plane, 0, plane, 2), (plane, 1, plane + 1, 0)]
+
+    def core_sum(parts):
         send, send_c, keep, keep_c = parts
-        s = (send.astype(F32) + pc(send_c).astype(F32)).astype(BF)
+        s = (send.astype(F32) + pc(send_c).astype(F32)).astype(BF).reshape(4, held, cols)
         k = (keep.astype(F32) + pc(keep_c).astype(F32)).reshape(4, held, cols)
-        ra = px(s[: 2 * held]).astype(F32).reshape(2, held, cols)
-        rb = py(s[2 * held :]).astype(F32).reshape(2, held, cols)
-        back_a = py((k[1] + ra[1]).astype(BF)).astype(F32)
-        back_b = px((k[3] + rb[1]).astype(BF)).astype(F32)
-        return k[0] + ra[0] + back_a, k[2] + rb[0] + back_b
-
-    first = ffn(sc, gather(t0, t1), layout, cols, *weights)
-    last = ffn(sc, gather(t3, t2), layout, cols, *weights)
-    u0, u1 = scatter(first)
-    u3, u2 = scatter(last)
-    total = u0 + pz(u1.astype(BF), 1).astype(F32)
-    total = total + pz(u3.astype(BF), 3).astype(F32) + pz(u2.astype(BF), 2).astype(F32)
+        return s, k
+
+    def scatter(s, k):
+        ra, rb, qa, qb = px(s[0]), py(s[1]), px(s[2]), py(s[3])
+        back_a = py((k[0] + ra.astype(F32)).astype(BF)).astype(F32)
+        back_b = px((k[1] + rb.astype(F32)).astype(BF)).astype(F32)
+        return k[2] + qa.astype(F32) + back_a, k[3] + qb.astype(F32) + back_b
+
+    near, far = gather(t0, t1), gather(t3, t2)
+    near_c = [pc(a) for a in near]
+    far_c = [pc(a) for a in far]
+    *first, wg, wu, wd = ffn(sc, far + far_c, layout, cols, weights, True, near_c)
+    s, k = core_sum(first)
+    last = ffn(sc, near + near_c, layout, cols, (wg, wu, wd), False, [s])
+    u3, u2 = scatter(s, k)
+    u0, u1 = scatter(*core_sum(last))
+    total = u0 + pz(u3.astype(BF), 3).astype(F32) + pz(u2.astype(BF), 2).astype(F32)
+    total = total + pz(u1.astype(BF), 1).astype(F32)
     return total.astype(BF)
 
 

time: 126 us -> 115 us (0.913)
  waiting for transfers between devices: 58.6 us -> 47.9 us
  local copies, waits for them, and re-layouts: 11.6 us -> 6.42 us
  Pallas kernels: 18.3 us -> 21 us
  starting transfers between devices: 34.1 us -> 36 us
    ppermute x8 -> x12, waiting for transfers between devices: 31.8 us -> 14.2 us  [on_device(): px = lambda a: lax.ppermute(a, 'x', swap)]
    ppermute x8 -> x12, starting transfers between devices: 8.91 us -> 16.4 us  [on_device(): py = lambda a: lax.ppermute(a, 'y', swap)]
    ppermute x8 -> x12, waiting for transfers between devices: 9.72 us -> 16.9 us  [on_device(): py = lambda a: lax.ppermute(a, 'y', swap)]
    unnamed x19 -> x28, local copies, waits for them, and re-layouts: 10.2 us -> 3.66 us
    ppermute x6, waiting for transfers between devices: 16.7 us -> 12.2 us  [on_device(): pz = lambda a, k: lax.ppermute(a, 'z', [(i, i ^ k) for i in range(nz)])]
    ppermute x12, waiting for transfers between devices: 0.33 us -> 4.69 us  [on_device(): pc = lambda a: lax.ppermute(a, 'c', swap)]
    ppermute x6, starting transfers between devices: 11.4 us -> 7.22 us  [on_device(): pz = lambda a, k: lax.ppermute(a, 'z', [(i, i ^ k) for i in range(nz)])]
    pallas_call x2, Pallas kernels: 18.3 us -> 21 us  [ffn(): pl.pallas_call(functools.partial(ffn_kernel, layout, cols, fresh, len(fir...]
  transfers between devices with their start and end apart: 34 -> 42, of which waited for: 15 -> 19; matrix products, arithmetic and copies ran while one was open for 1% -> 6% of each run, Pallas kernels for 15% -> 7%
where the time goes in v3:
time: 115 us
  waiting for transfers between devices  47.9 us (42%)
  starting transfers between devices  36 us (31%)
  Pallas kernels  21 us (18%)
  local copies, waits for them, and re-layouts  6.42 us (6%)
  other arithmetic  3.57 us (3%)
    pallas_call x2, Pallas kernels, ffn(): pl.pallas_call(functools.partial(ffn_kernel, layout, cols, fresh, len(fir...  21 us
    ppermute x12, waiting for transfers between devices, on_device(): py = lambda a: lax.ppermute(a, 'y', swap)  16.9 us
    ppermute x12, starting transfers between devices, on_device(): py = lambda a: lax.ppermute(a, 'y', swap)  16.4 us
    ppermute x12, waiting for transfers between devices, on_device(): px = lambda a: lax.ppermute(a, 'x', swap)  14.2 us
    ppermute x6, waiting for transfers between devices, on_device(): pz = lambda a, k: lax.ppermute(a, 'z', [(i, i ^ k) for i in range(nz)])  12.2 us
    ppermute x12, starting transfers between devices, on_device(): px = lambda a: lax.ppermute(a, 'x', swap)  10.4 us
    ppermute x6, starting transfers between devices, on_device(): pz = lambda a, k: lax.ppermute(a, 'z', [(i, i ^ k) for i in range(nz)])  7.22 us
    ppermute x12, waiting for transfers between devices, on_device(): pc = lambda a: lax.ppermute(a, 'c', swap)  4.69 us
  transfers between devices with their start and end apart: 42, of which 19 were waited for; matrix products, arithmetic and copies ran while one was open for 6% of the time, Pallas kernels for 7%

profile of v3, /device:TPU:0, one launch (start us, length us, event | category | flops | bytes accessed | tf_op | source)
XLA Modules:
  0.0 115.2 jit_solution(6754732009581219831)
XLA Ops:
  2.0 3.0 %collective-permute-start.1 = (bf16[48,2176]{1,0:T(8,128)(2,1)S(1)}, bf16[48,2176]{1,0:T(8,128)(2,1)S(1)}, u32[]{:S(2)}, u32[]{:S(2)}) collective-permute-start(bf16[48,2176]{1,0:T(8,128)(2,1)S(1)} %concatenate.15), channel_id=1, source_target_pairs={{0,1},{1,0},{2,3},{3,2},{4,5},{5,4},{6,7},{7,6},{8,9},{9,8},{10,11... | collective-permute-start | bytes 626696 | tf_op jit(solution)/shard_map/ppermute | solution.py:122
  5.0 1.5 %collective-permute-start = (bf16[48,2176]{1,0:T(8,128)(2,1)S(1)}, bf16[48,2176]{1,0:T(8,128)(2,1)S(1)}, u32[]{:S(2)}, u32[]{:S(2)}) collective-permute-start(bf16[48,2176]{1,0:T(8,128)(2,1)S(1)} %concatenate.15), channel_id=1, source_target_pairs={{0,4},{4,0},{1,5},{5,1},{2,6},{6,2},{3,7},{7,3},{8,12},{12,8},{9,1... | collective-permute-start | bytes 626696 | tf_op jit(solution)/shard_map/ppermute | solution.py:121
  6.5 3.6 %collective-permute-start.11 = (bf16[48,2176]{1,0:T(8,128)(2,1)S(1)}, bf16[48,2176]{1,0:T(8,128)(2,1)S(1)}, u32[]{:S(2)}, u32[]{:S(2)}) collective-permute-start(bf16[48,2176]{1,0:T(8,128)(2,1)S(1)} %concatenate.15), channel_id=1, source_target_pairs={{0,24},{8,16},{16,8},{24,0},{1,25},{9,17},{17,9},{25,1},{2,26},{10... | collective-permute-start | bytes 626696 | tf_op jit(solution)/shard_map/ppermute | solution.py:124
  10.1 1.5 %collective-permute-done = bf16[48,2176]{1,0:T(8,128)(2,1)S(1)} collective-permute-done((bf16[48,2176]{1,0:T(8,128)(2,1)S(1)}, bf16[48,2176]{1,0:T(8,128)(2,1)S(1)}, u32[]{:S(2)}, u32[]{:S(2)}) %collective-permute-start) | collective-permute-done | bytes 208928 | tf_op jit(solution)/shard_map/ppermute | solution.py:121
  11.7 4.6 %collective-permute-done.11 = bf16[48,2176]{1,0:T(8,128)(2,1)S(1)} collective-permute-done((bf16[48,2176]{1,0:T(8,128)(2,1)S(1)}, bf16[48,2176]{1,0:T(8,128)(2,1)S(1)}, u32[]{:S(2)}, u32[]{:S(2)}) %collective-permute-start.11) | collective-permute-done | bytes 208928 | tf_op jit(solution)/shard_map/ppermute | solution.py:124
  16.4 2.5 %collective-permute-start.15 = (bf16[48,2176]{1,0:T(8,128)(2,1)S(1)}, bf16[48,2176]{1,0:T(8,128)(2,1)S(1)}, u32[]{:S(2)}, u32[]{:S(2)}) collective-permute-start(bf16[48,2176]{1,0:T(8,128)(2,1)S(1)} %collective-permute-done.11), channel_id=1, source_target_pairs={{0,8},{8,0},{16,24},{24,16},{1,9},{9,1},{17,25},{25,17},{2,10},{10... | collective-permute-start | bytes 626696 | tf_op jit(solution)/shard_map/ppermute | solution.py:124
  19.9 1.5 %collective-permute-start.7 = (bf16[48,2176]{1,0:T(8,128)(2,1)S(1)}, bf16[48,2176]{1,0:T(8,128)(2,1)S(1)}, u32[]{:S(2)}, u32[]{:S(2)}) collective-permute-start(bf16[48,2176]{1,0:T(8,128)(2,1)S(1)} %collective-permute-done.5), channel_id=1, source_target_pairs={{0,1},{1,0},{2,3},{3,2},{4,5},{5,4},{6,7},{7,6},{8,9},{9,8},{10,11... | collective-permute-start | bytes 626696 | tf_op jit(solution)/shard_map/ppermute | solution.py:122
  22.1 1.6 %collective-permute-done.15 = bf16[48,2176]{1,0:T(8,128)(2,1)S(1)} collective-permute-done((bf16[48,2176]{1,0:T(8,128)(2,1)S(1)}, bf16[48,2176]{1,0:T(8,128)(2,1)S(1)}, u32[]{:S(2)}, u32[]{:S(2)}) %collective-permute-start.15) | collective-permute-done | bytes 208928 | tf_op jit(solution)/shard_map/ppermute | solution.py:124
  25.0 4.7 %collective-permute-done.6 = bf16[48,2176]{1,0:T(8,128)(2,1)S(1)} collective-permute-done((bf16[48,2176]{1,0:T(8,128)(2,1)S(1)}, bf16[48,2176]{1,0:T(8,128)(2,1)S(1)}, u32[]{:S(2)}, u32[]{:S(2)}) %collective-permute-start.6) | collective-permute-done | bytes 208928 | tf_op jit(solution)/shard_map/ppermute | solution.py:121
  29.7 1.5 %collective-permute-start.3 = (bf16[48,2176]{1,0:T(8,128)(2,1)S(1)}, bf16[48,2176]{1,0:T(8,128)(2,1)S(1)}, u32[]{:S(2)}, u32[]{:S(2)}) collective-permute-start(bf16[48,2176]{1,0:T(8,128)(2,1)S(1)} %collective-permute-done), channel_id=1, source_target_pairs={{0,1},{1,0},{2,3},{3,2},{4,5},{5,4},{6,7},{7,6},{8,9},{9,8},{10,11... | collective-permute-start | bytes 626696 | tf_op jit(solution)/shard_map/ppermute | solution.py:122
  33.2 1.5 %collective-permute-start.14 = (bf16[48,2176]{1,0:T(8,128)(2,1)S(1)}, bf16[48,2176]{1,0:T(8,128)(2,1)S(1)}, u32[]{:S(2)}, u32[]{:S(2)}) collective-permute-start(bf16[48,2176]{1,0:T(8,128)(2,1)S(1)} %collective-permute-done.12), channel_id=1, source_target_pairs={{0,1},{1,0},{2,3},{3,2},{4,5},{5,4},{6,7},{7,6},{8,9},{9,8},{10,11... | collective-permute-start | bytes 626696 | tf_op jit(solution)/shard_map/ppermute | solution.py:122
  35.3 2.5 %collective-permute-done.3.refs_3_ = bf16[48,2176]{1,0:T(8,128)(2,1)S(1)} collective-permute-done((bf16[48,2176]{1,0:T(8,128)(2,1)S(1)}, bf16[48,2176]{1,0:T(8,128)(2,1)S(1)}, u32[]{:S(2)}, u32[]{:S(2)}) %collective-permute-start.3) | collective-permute-done | bytes 208928 | tf_op jit(solution)/shard_map/ppermute | solution.py:122
  38.3 3.8 %collective-permute-done.17 = bf16[48,2176]{1,0:T(8,128)(2,1)S(1)} collective-permute-done((bf16[48,2176]{1,0:T(8,128)(2,1)S(1)}, bf16[48,2176]{1,0:T(8,128)(2,1)S(1)}, u32[]{:S(2)}, u32[]{:S(2)}) %collective-permute-start.17) | collective-permute-done | bytes 208928 | tf_op jit(solution)/shard_map/ppermute | solution.py:122
  42.7 1.7 %collective-permute-done.14.refs_6_ = bf16[48,2176]{1,0:T(8,128)(2,1)S(1)} collective-permute-done((bf16[48,2176]{1,0:T(8,128)(2,1)S(1)}, bf16[48,2176]{1,0:T(8,128)(2,1)S(1)}, u32[]{:S(2)}, u32[]{:S(2)}) %collective-permute-start.14) | collective-permute-done | bytes 208928 | tf_op jit(solution)/shard_map/ppermute | solution.py:122
  46.4 3.5 %collective-permute-done.18.refs_8_ = bf16[48,2176]{1,0:T(8,128)(2,1)} collective-permute-done((bf16[48,2176]{1,0:T(8,128)(2,1)S(1)}, bf16[48,2176]{1,0:T(8,128)(2,1)}, u32[]{:S(2)}, u32[]{:S(2)}) %collective-permute-start.18) | collective-permute-done | bytes 208928 | tf_op jit(solution)/shard_map/ppermute | solution.py:121
  50.4 1.8 %collective-permute-done.10.refs_3_.refs_9_ = bf16[48,2176]{1,0:T(8,128)(2,1)S(1)} collective-permute-done((bf16[48,2176]{1,0:T(8,128)(2,1)S(1)}, bf16[48,2176]{1,0:T(8,128)(2,1)S(1)}, u32[]{:S(2)}, u32[]{:S(2)}) %collective-permute-start.10) | collective-permute-done | bytes 208928 | tf_op jit(solution)/shard_map/ppermute | solution.py:123
  54.8 12.5 %ffn.2 = (bf16[192,2048]{1,0:T(8,128)(2,1)S(1)}, bf16[192,2048]{1,0:T(8,128)(2,1)S(1)}, bf16[192,2048]{1,0:T(8,128)(2,1)S(1)}, bf16[192,2048]{1,0:T(8,128)(2,1)S...) custom-call(bf16[144,2176]{1,0:T(8,128)(2,1)} %copy-done, ...), custom_call_target="tpu_custom_call" | custom-call | flops 7247757312 | bytes 25165824 | tf_op jit(solution)/shard_map/ffn/pallas_call | solution.py:90
  67.9 1.8 %collective-permute-done.23 = bf16[192,2048]{1,0:T(8,128)(2,1)S(1)} collective-permute-done((bf16[192,2048]{1,0:T(8,128)(2,1)S(1)}, bf16[192,2048]{1,0:T(8,128)(2,1)S(1)}, u32[]{:S(2)}, u32[]{:S(2)}) %collective-permute-start.23) | collective-permute-done | bytes 786464 | tf_op jit(solution)/shard_map/ppermute | solution.py:123
  70.7 1.6 %collective-permute-start.35 = (bf16[48,2048]{1,0:T(8,128)(2,1)S(1)}, bf16[48,2048]{1,0:T(8,128)(2,1)S(1)}, u32[]{:S(2)}, u32[]{:S(2)}) collective-permute-start(bf16[48,2048]{1,0:T(8,128)(2,1)S(1)} %get-tuple-element.36), channel_id=1, source_target_pairs={{0,1},{1,0},{2,3},{3,2},{4,5},{5,4},{6,7},{7,6},{8,9},{9,8},{10,11... | collective-permute-start | bytes 589832 | tf_op jit(solution)/shard_map/ppermute | solution.py:122
  72.3 1.5 %collective-permute-start.31 = (bf16[48,2048]{1,0:T(8,128)(2,1)S(1)}, bf16[48,2048]{1,0:T(8,128)(2,1)S(1)}, u32[]{:S(2)}, u32[]{:S(2)}) collective-permute-start(bf16[48,2048]{1,0:T(8,128)(2,1)S(1)} %get-tuple-element.38), channel_id=1, source_target_pairs={{0,4},{4,0},{1,5},{5,1},{2,6},{6,2},{3,7},{7,3},{8,12},{12,8},{9,1... | collective-permute-start | bytes 589832 | tf_op jit(solution)/shard_map/ppermute | solution.py:121
  73.8 8.5 %ffn.3 = (bf16[192,2048]{1,0:T(8,128)(2,1)S(1)}, bf16[192,2048]{1,0:T(8,128)(2,1)S(1)}, bf16[192,2048]{1,0:T(8,128)(2,1)S(1)}, bf16[192,2048]{1,0:T(8,128)(2,1)S(1)}) custom-call(bf16[4,48,2048]{2,1,0:T(8,128)(2,1)S(1)} %bitcast.6, s32[2]{0:T(128)S(1)} %copy-done.8, bf16[144,2176]{1,0:T(8,128)(2,1)S(1)} %pad_maximum_fusion.refs_2_, ...), custom_call_target="tpu_custom_call" | custom-call | flops 7247757312 | bytes 25165824 | tf_op jit(solution)/shard_map/ffn/pallas_call | solution.py:90
  83.1 1.6 %collective-permute-start.34 = (bf16[48,2048]{1,0:T(8,128)(2,1)S(1)}, bf16[48,2048]{1,0:T(8,128)(2,1)S(1)}, u32[]{:S(2)}, u32[]{:S(2)}) collective-permute-start(bf16[48,2048]{1,0:T(8,128)(2,1)S(1)} %get-tuple-element.37), channel_id=1, source_target_pairs={{0,1},{1,0},{2,3},{3,2},{4,5},{5,4},{6,7},{7,6},{8,9},{9,8},{10,11... | collective-permute-start | bytes 589832 | tf_op jit(solution)/shard_map/ppermute | solution.py:122
  84.8 5.7 %collective-permute-done.32 = bf16[48,2048]{1,0:T(8,128)(2,1)S(1)} collective-permute-done((bf16[48,2048]{1,0:T(8,128)(2,1)S(1)}, bf16[48,2048]{1,0:T(8,128)(2,1)S(1)}, u32[]{:S(2)}, u32[]{:S(2)}) %collective-permute-start.32) | collective-permute-done | bytes 196640 | tf_op jit(solution)/shard_map/ppermute | solution.py:122
  91.9 1.8 %collective-permute-start.39 = (bf16[48,2048]{1,0:T(8,128)(2,1)S(1)}, bf16[48,2048]{1,0:T(8,128)(2,1)S(1)}, u32[]{:S(2)}, u32[]{:S(2)}) collective-permute-start(bf16[48,2048]{1,0:T(8,128)(2,1)S(1)} %get-tuple-element.32), channel_id=1, source_target_pairs={{0,1},{1,0},{2,3},{3,2},{4,5},{5,4},{6,7},{7,6},{8,9},{9,8},{10,11... | collective-permute-start | bytes 589832 | tf_op jit(solution)/shard_map/ppermute | solution.py:122
  93.8 1.5 %collective-permute-start.27 = (bf16[48,2048]{1,0:T(8,128)(2,1)S(1)}, bf16[48,2048]{1,0:T(8,128)(2,1)S(1)}, u32[]{:S(2)}, u32[]{:S(2)}) collective-permute-start(bf16[48,2048]{1,0:T(8,128)(2,1)S(1)} %get-tuple-element.34), channel_id=1, source_target_pairs={{0,4},{4,0},{1,5},{5,1},{2,6},{6,2},{3,7},{7,3},{8,12},{12,8},{9,1... | collective-permute-start | bytes 589832 | tf_op jit(solution)/shard_map/ppermute | solution.py:121
  95.5 3.0 %collective-permute-done.39 = bf16[48,2048]{1,0:T(8,128)(2,1)S(1)} collective-permute-done((bf16[48,2048]{1,0:T(8,128)(2,1)S(1)}, bf16[48,2048]{1,0:T(8,128)(2,1)S(1)}, u32[]{:S(2)}, u32[]{:S(2)}) %collective-permute-start.39) | collective-permute-done | bytes 196640 | tf_op jit(solution)/shard_map/ppermute | solution.py:122
  99.4 1.7 %collective-permute-done.27 = bf16[48,2048]{1,0:T(8,128)(2,1)S(1)} collective-permute-done((bf16[48,2048]{1,0:T(8,128)(2,1)S(1)}, bf16[48,2048]{1,0:T(8,128)(2,1)S(1)}, u32[]{:S(2)}, u32[]{:S(2)}) %collective-permute-start.27) | collective-permute-done | bytes 196640 | tf_op jit(solution)/shard_map/ppermute | solution.py:121
  102.4 1.5 %collective-permute-start.26 = (bf16[48,2048]{1,0:T(8,128)(2,1)S(1)}, bf16[48,2048]{1,0:T(8,128)(2,1)S(1)}, u32[]{:S(2)}, u32[]{:S(2)}) collective-permute-start(bf16[48,2048]{1,0:T(8,128)(2,1)S(1)} %get-tuple-element.31), channel_id=1, source_target_pairs={{0,4},{4,0},{1,5},{5,1},{2,6},{6,2},{3,7},{7,3},{8,12},{12,8},{9,1... | collective-permute-start | bytes 589832 | tf_op jit(solution)/shard_map/ppermute | solution.py:121
  104.1 1.3 %collective-permute-start.28 = (bf16[48,2048]{1,0:T(8,128)(2,1)S(1)}, bf16[48,2048]{1,0:T(8,128)(2,1)S(1)}, u32[]{:S(2)}, u32[]{:S(2)}) collective-permute-start(bf16[48,2048]{1,0:T(8,128)(2,1)S(1)} %get-tuple-element.27), channel_id=1, source_target_pairs={{0,1},{1,0},{2,3},{3,2},{4,5},{5,4},{6,7},{7,6},{8,9},{9,8},{10,11... | collective-permute-start | bytes 589832 | tf_op jit(solution)/shard_map/ppermute | solution.py:122
  105.4 2.9 %collective-permute-done.40 = bf16[48,2048]{1,0:T(8,128)(2,1)S(1)} collective-permute-done((bf16[48,2048]{1,0:T(8,128)(2,1)S(1)}, bf16[48,2048]{1,0:T(8,128)(2,1)S(1)}, u32[]{:S(2)}, u32[]{:S(2)}) %collective-permute-start.40) | collective-permute-done | bytes 196640 | tf_op jit(solution)/shard_map/ppermute | solution.py:121
  108.4 3.8 %collective-permute-done.37 = bf16[48,2048]{1,0:T(8,128)(2,1)S(1)} collective-permute-done((bf16[48,2048]{1,0:T(8,128)(2,1)S(1)}, bf16[48,2048]{1,0:T(8,128)(2,1)S(1)}, u32[]{:S(2)}, u32[]{:S(2)}) %collective-permute-start.37) | collective-permute-done | bytes 196640 | tf_op jit(solution)/shard_map/ppermute | solution.py:124
  112.3 2.1 %collective-permute-done.41 = bf16[48,2048]{1,0:T(8,128)(2,1)S(1)} collective-permute-done((bf16[48,2048]{1,0:T(8,128)(2,1)S(1)}, bf16[48,2048]{1,0:T(8,128)(2,1)S(1)}, u32[]{:S(2)}, u32[]{:S(2)}) %collective-permute-start.41) | collective-permute-done | bytes 196640 | tf_op jit(solution)/shard_map/ppermute | solution.py:124
  (106 shorter events, 21.5 us)
Async XLA Ops:
  2.0 8.2 %collective-permute-start.1 = (bf16[48,2176]{1,0:T(8,128)(2,1)S(1)}, bf16[48,2176]{1,0:T(8,128)(2,1)S(1)}, u32[]{:S(2)}, u32[]{:S(2)}) collective-permute-start(bf16[48,2176]{1,0:T(8,128)(2,1)S(1)} %concatenate.15), channel_id=1, source_target_pairs={{0,1},{1,0},{2,3},{3,2},{4,5},{5,4},{6,7},{7,6},{8,9},{9,8},{10,11... | collective-permute-start | bytes 626696 | tf_op jit(solution)/shard_map/ppermute | solution.py:122
  5.0 6.6 %collective-permute-start = (bf16[48,2176]{1,0:T(8,128)(2,1)S(1)}, bf16[48,2176]{1,0:T(8,128)(2,1)S(1)}, u32[]{:S(2)}, u32[]{:S(2)}) collective-permute-start(bf16[48,2176]{1,0:T(8,128)(2,1)S(1)} %concatenate.15), channel_id=1, source_target_pairs={{0,4},{4,0},{1,5},{5,1},{2,6},{6,2},{3,7},{7,3},{8,12},{12,8},{9,1... | collective-permute-start | bytes 626696 | tf_op jit(solution)/shard_map/ppermute | solution.py:121
  6.5 9.9 %collective-permute-start.11 = (bf16[48,2176]{1,0:T(8,128)(2,1)S(1)}, bf16[48,2176]{1,0:T(8,128)(2,1)S(1)}, u32[]{:S(2)}, u32[]{:S(2)}) collective-permute-start(bf16[48,2176]{1,0:T(8,128)(2,1)S(1)} %concatenate.15), channel_id=1, source_target_pairs={{0,24},{8,16},{16,8},{24,0},{1,25},{9,17},{17,9},{25,1},{2,26},{10... | collective-permute-start | bytes 626696 | tf_op jit(solution)/shard_map/ppermute | solution.py:124
  10.1 9.8 %collective-permute-start.5 = (bf16[48,2176]{1,0:T(8,128)(2,1)S(1)}, bf16[48,2176]{1,0:T(8,128)(2,1)S(1)}, u32[]{:S(2)}, u32[]{:S(2)}) collective-permute-start(bf16[48,2176]{1,0:T(8,128)(2,1)S(1)} %concatenate.15), channel_id=1, source_target_pairs={{0,8},{8,0},{16,24},{24,16},{1,9},{9,1},{17,25},{25,17},{2,10},{10... | collective-permute-start | bytes 626696 | tf_op jit(solution)/shard_map/ppermute | solution.py:124
  11.7 41.3 %collective-permute-start.2 = (bf16[144,2176]{1,0:T(8,128)(2,1)S(1)}, bf16[144,2176]{1,0:T(8,128)(2,1)S(1)}, u32[]{:S(2)}, u32[]{:S(2)}) collective-permute-start(bf16[144,2176]{1,0:T(8,128)(2,1)S(1)} %pad_maximum_fusion.refs_2_), channel_id=1, source_target_pairs={{0,2},{2,0},{1,3},{3,1},{4,6},{6,4},{5,7},{7,5},{8,10},{10,8},{9,1... | collective-permute-start | bytes 1880072 | tf_op jit(solution)/shard_map/ppermute | solution.py:123
  16.4 7.4 %collective-permute-start.15 = (bf16[48,2176]{1,0:T(8,128)(2,1)S(1)}, bf16[48,2176]{1,0:T(8,128)(2,1)S(1)}, u32[]{:S(2)}, u32[]{:S(2)}) collective-permute-start(bf16[48,2176]{1,0:T(8,128)(2,1)S(1)} %collective-permute-done.11), channel_id=1, source_target_pairs={{0,8},{8,0},{16,24},{24,16},{1,9},{9,1},{17,25},{25,17},{2,10},{10... | collective-permute-start | bytes 626696 | tf_op jit(solution)/shard_map/ppermute | solution.py:124
  18.9 14.3 %collective-permute-start.13 = (bf16[48,2176]{1,0:T(8,128)(2,1)S(1)}, bf16[48,2176]{1,0:T(8,128)(2,1)S(1)}, u32[]{:S(2)}, u32[]{:S(2)}) collective-permute-start(bf16[48,2176]{1,0:T(8,128)(2,1)S(1)} %collective-permute-done.11), channel_id=1, source_target_pairs={{0,1},{1,0},{2,3},{3,2},{4,5},{5,4},{6,7},{7,6},{8,9},{9,8},{10,11... | collective-permute-start | bytes 626696 | tf_op jit(solution)/shard_map/ppermute | solution.py:122
  19.4 12.5 %collective-permute-start.12 = (bf16[48,2176]{1,0:T(8,128)(2,1)S(1)}, bf16[48,2176]{1,0:T(8,128)(2,1)S(1)}, u32[]{:S(2)}, u32[]{:S(2)}) collective-permute-start(bf16[48,2176]{1,0:T(8,128)(2,1)S(1)} %collective-permute-done.11), channel_id=1, source_target_pairs={{0,4},{4,0},{1,5},{5,1},{2,6},{6,2},{3,7},{7,3},{8,12},{12,8},{9,1... | collective-permute-start | bytes 626696 | tf_op jit(solution)/shard_map/ppermute | solution.py:121
  19.9 11.3 %collective-permute-start.7 = (bf16[48,2176]{1,0:T(8,128)(2,1)S(1)}, bf16[48,2176]{1,0:T(8,128)(2,1)S(1)}, u32[]{:S(2)}, u32[]{:S(2)}) collective-permute-start(bf16[48,2176]{1,0:T(8,128)(2,1)S(1)} %collective-permute-done.5), channel_id=1, source_target_pairs={{0,1},{1,0},{2,3},{3,2},{4,5},{5,4},{6,7},{7,6},{8,9},{9,8},{10,11... | collective-permute-start | bytes 626696 | tf_op jit(solution)/shard_map/ppermute | solution.py:122
  29.7 8.1 %collective-permute-start.3 = (bf16[48,2176]{1,0:T(8,128)(2,1)S(1)}, bf16[48,2176]{1,0:T(8,128)(2,1)S(1)}, u32[]{:S(2)}, u32[]{:S(2)}) collective-permute-start(bf16[48,2176]{1,0:T(8,128)(2,1)S(1)} %collective-permute-done), channel_id=1, source_target_pairs={{0,1},{1,0},{2,3},{3,2},{4,5},{5,4},{6,7},{7,6},{8,9},{9,8},{10,11... | collective-permute-start | bytes 626696 | tf_op jit(solution)/shard_map/ppermute | solution.py:122
  31.2 11.0 %collective-permute-start.17 = (bf16[48,2176]{1,0:T(8,128)(2,1)S(1)}, bf16[48,2176]{1,0:T(8,128)(2,1)S(1)}, u32[]{:S(2)}, u32[]{:S(2)}) collective-permute-start(bf16[48,2176]{1,0:T(8,128)(2,1)S(1)} %collective-permute-done.15), channel_id=1, source_target_pairs={{0,1},{1,0},{2,3},{3,2},{4,5},{5,4},{6,7},{7,6},{8,9},{9,8},{10,11... | collective-permute-start | bytes 626696 | tf_op jit(solution)/shard_map/ppermute | solution.py:122
  31.9 10.3 %collective-permute-start.16 = (bf16[48,2176]{1,0:T(8,128)(2,1)S(1)}, bf16[48,2176]{1,0:T(8,128)(2,1)S(1)}, u32[]{:S(2)}, u32[]{:S(2)}) collective-permute-start(bf16[48,2176]{1,0:T(8,128)(2,1)S(1)} %collective-permute-done.15), channel_id=1, source_target_pairs={{0,4},{4,0},{1,5},{5,1},{2,6},{6,2},{3,7},{7,3},{8,12},{12,8},{9,1... | collective-permute-start | bytes 626696 | tf_op jit(solution)/shard_map/ppermute | solution.py:121
  33.2 11.2 %collective-permute-start.14 = (bf16[48,2176]{1,0:T(8,128)(2,1)S(1)}, bf16[48,2176]{1,0:T(8,128)(2,1)S(1)}, u32[]{:S(2)}, u32[]{:S(2)}) collective-permute-start(bf16[48,2176]{1,0:T(8,128)(2,1)S(1)} %collective-permute-done.12), channel_id=1, source_target_pairs={{0,1},{1,0},{2,3},{3,2},{4,5},{5,4},{6,7},{7,6},{8,9},{9,8},{10,11... | collective-permute-start | bytes 626696 | tf_op jit(solution)/shard_map/ppermute | solution.py:122
  37.8 8.1 %collective-permute-start.9 = (bf16[48,2176]{1,0:T(8,128)(2,1)S(1)}, bf16[48,2176]{1,0:T(8,128)(2,1)S(1)}, u32[]{:S(2)}, u32[]{:S(2)}) collective-permute-start(bf16[48,2176]{1,0:T(8,128)(2,1)S(1)} %collective-permute-done.7), channel_id=1, source_target_pairs={{0,4},{4,0},{1,5},{5,1},{2,6},{6,2},{3,7},{7,3},{8,12},{12,8},{9,1... | collective-permute-start | bytes 626696 | tf_op jit(solution)/shard_map/ppermute | solution.py:121
  42.2 7.7 %collective-permute-start.18 = (bf16[48,2176]{1,0:T(8,128)(2,1)S(1)}, bf16[48,2176]{1,0:T(8,128)(2,1)}, u32[]{:S(2)}, u32[]{:S(2)}) collective-permute-start(bf16[48,2176]{1,0:T(8,128)(2,1)S(1)} %collective-permute-done.17), channel_id=1, source_target_pairs={{0,4},{4,0},{1,5},{5,1},{2,6},{6,2},{3,7},{7,3},{8,12},{12,8},{9,1... | collective-permute-start | bytes 626696 | tf_op jit(solution)/shard_map/ppermute | solution.py:121
  45.9 8.2 %collective-permute-start.19 = (bf16[144,2176]{1,0:T(8,128)(2,1)}, bf16[144,2176]{1,0:T(8,128)(2,1)}, u32[]{:S(2)}, u32[]{:S(2)}) collective-permute-start(bf16[144,2176]{1,0:T(8,128)(2,1)} %constant_dynamic-update-slice_fusion.3.refs_5_), channel_id=1, source_target_pairs={{0,2},{2,0},{1,3},{3,1},{4,6},{6,4},{5,7},{7,5},{8,10},{10,8},{9,1... | collective-permute-start | bytes 1880072 | tf_op jit(solution)/shard_map/ppermute | solution.py:123
  46.3 7.7 %collective-permute-start.8 = (bf16[144,2176]{1,0:T(8,128)(2,1)S(1)}, bf16[144,2176]{1,0:T(8,128)(2,1)S(1)}, u32[]{:S(2)}, u32[]{:S(2)}) collective-permute-start(bf16[144,2176]{1,0:T(8,128)(2,1)S(1)} %constant_dynamic-update-slice_fusion.refs_4_), channel_id=1, source_target_pairs={{0,2},{2,0},{1,3},{3,1},{4,6},{6,4},{5,7},{7,5},{8,10},{10,8},{9,1... | collective-permute-start | bytes 1880072 | tf_op jit(solution)/shard_map/ppermute | solution.py:123
  67.5 14.8 %collective-permute-start.29 = (bf16[192,2048]{1,0:T(8,128)(2,1)S(1)}, bf16[192,2048]{1,0:T(8,128)(2,1)S(1)}, u32[]{:S(2)}, u32[]{:S(2)}) collective-permute-start(bf16[192,2048]{1,0:T(8,128)(2,1)S(1)} %get-tuple-element.26), channel_id=1, source_target_pairs={{0,2},{2,0},{1,3},{3,1},{4,6},{6,4},{5,7},{7,5},{8,10},{10,8},{9,1... | collective-permute-start | bytes 2359304 | tf_op jit(solution)/shard_map/ppermute | solution.py:123
  70.1 14.7 %collective-permute-start.30 = (bf16[48,2048]{1,0:T(8,128)(2,1)S(1)}, bf16[48,2048]{1,0:T(8,128)(2,1)S(1)}, u32[]{:S(2)}, u32[]{:S(2)}) collective-permute-start(bf16[48,2048]{1,0:T(8,128)(2,1)S(1)} %get-tuple-element.35), channel_id=1, source_target_pairs={{0,4},{4,0},{1,5},{5,1},{2,6},{6,2},{3,7},{7,3},{8,12},{12,8},{9,1... | collective-permute-start | bytes 589832 | tf_op jit(solution)/shard_map/ppermute | solution.py:121
  70.7 14.1 %collective-permute-start.35 = (bf16[48,2048]{1,0:T(8,128)(2,1)S(1)}, bf16[48,2048]{1,0:T(8,128)(2,1)S(1)}, u32[]{:S(2)}, u32[]{:S(2)}) collective-permute-start(bf16[48,2048]{1,0:T(8,128)(2,1)S(1)} %get-tuple-element.36), channel_id=1, source_target_pairs={{0,1},{1,0},{2,3},{3,2},{4,5},{5,4},{6,7},{7,6},{8,9},{9,8},{10,11... | collective-permute-start | bytes 589832 | tf_op jit(solution)/shard_map/ppermute | solution.py:122
  72.3 10.3 %collective-permute-start.31 = (bf16[48,2048]{1,0:T(8,128)(2,1)S(1)}, bf16[48,2048]{1,0:T(8,128)(2,1)S(1)}, u32[]{:S(2)}, u32[]{:S(2)}) collective-permute-start(bf16[48,2048]{1,0:T(8,128)(2,1)S(1)} %get-tuple-element.38), channel_id=1, source_target_pairs={{0,4},{4,0},{1,5},{5,1},{2,6},{6,2},{3,7},{7,3},{8,12},{12,8},{9,1... | collective-permute-start | bytes 589832 | tf_op jit(solution)/shard_map/ppermute | solution.py:121
  82.3 9.3 %collective-permute-start.25 = (bf16[192,2048]{1,0:T(8,128)(2,1)S(1)}, bf16[192,2048]{1,0:T(8,128)(2,1)S(1)}, u32[]{:S(2)}, u32[]{:S(2)}) collective-permute-start(bf16[192,2048]{1,0:T(8,128)(2,1)S(1)} %get-tuple-element.24), channel_id=1, source_target_pairs={{0,2},{2,0},{1,3},{3,1},{4,6},{6,4},{5,7},{7,5},{8,10},{10,8},{9,1... | collective-permute-start | bytes 2359304 | tf_op jit(solution)/shard_map/ppermute | solution.py:123
  82.7 7.8 %collective-permute-start.32 = (bf16[48,2048]{1,0:T(8,128)(2,1)S(1)}, bf16[48,2048]{1,0:T(8,128)(2,1)S(1)}, u32[]{:S(2)}, u32[]{:S(2)}) collective-permute-start(bf16[48,2048]{1,0:T(8,128)(2,1)S(1)} %fusion.6), channel_id=1, source_target_pairs={{0,1},{1,0},{2,3},{3,2},{4,5},{5,4},{6,7},{7,6},{8,9},{9,8},{10,11... | collective-permute-start | bytes 589832 | tf_op jit(solution)/shard_map/ppermute | solution.py:122
  83.1 18.7 %collective-permute-start.34 = (bf16[48,2048]{1,0:T(8,128)(2,1)S(1)}, bf16[48,2048]{1,0:T(8,128)(2,1)S(1)}, u32[]{:S(2)}, u32[]{:S(2)}) collective-permute-start(bf16[48,2048]{1,0:T(8,128)(2,1)S(1)} %get-tuple-element.37), channel_id=1, source_target_pairs={{0,1},{1,0},{2,3},{3,2},{4,5},{5,4},{6,7},{7,6},{8,9},{9,8},{10,11... | collective-permute-start | bytes 589832 | tf_op jit(solution)/shard_map/ppermute | solution.py:122
  84.7 9.0 %collective-permute-start.24 = (bf16[192,2048]{1,0:T(8,128)(2,1)S(1)}, bf16[192,2048]{1,0:T(8,128)(2,1)S(1)}, u32[]{:S(2)}, u32[]{:S(2)}) collective-permute-start(bf16[192,2048]{1,0:T(8,128)(2,1)S(1)} %get-tuple-element.22), channel_id=1, source_target_pairs={{0,2},{2,0},{1,3},{3,1},{4,6},{6,4},{5,7},{7,5},{8,10},{10,8},{9,1... | collective-permute-start | bytes 2359304 | tf_op jit(solution)/shard_map/ppermute | solution.py:123
  90.5 17.9 %collective-permute-start.33 = (bf16[48,2048]{1,0:T(8,128)(2,1)S(1)}, bf16[48,2048]{1,0:T(8,128)(2,1)S(1)}, u32[]{:S(2)}, u32[]{:S(2)}) collective-permute-start(bf16[48,2048]{1,0:T(8,128)(2,1)S(1)} %get-tuple-element.29), channel_id=1, source_target_pairs={{0,24},{8,16},{16,8},{24,0},{1,25},{9,17},{17,9},{25,1},{2,26},{10... | collective-permute-start | bytes 589832 | tf_op jit(solution)/shard_map/ppermute | solution.py:124
  91.1 10.7 %collective-permute-start.36 = (bf16[48,2048]{1,0:T(8,128)(2,1)S(1)}, bf16[48,2048]{1,0:T(8,128)(2,1)S(1)}, u32[]{:S(2)}, u32[]{:S(2)}) collective-permute-start(bf16[48,2048]{1,0:T(8,128)(2,1)S(1)} %get-tuple-element.30), channel_id=1, source_target_pairs={{0,4},{4,0},{1,5},{5,1},{2,6},{6,2},{3,7},{7,3},{8,12},{12,8},{9,1... | collective-permute-start | bytes 589832 | tf_op jit(solution)/shard_map/ppermute | solution.py:121
  93.8 7.4 %collective-permute-start.27 = (bf16[48,2048]{1,0:T(8,128)(2,1)S(1)}, bf16[48,2048]{1,0:T(8,128)(2,1)S(1)}, u32[]{:S(2)}, u32[]{:S(2)}) collective-permute-start(bf16[48,2048]{1,0:T(8,128)(2,1)S(1)} %get-tuple-element.34), channel_id=1, source_target_pairs={{0,4},{4,0},{1,5},{5,1},{2,6},{6,2},{3,7},{7,3},{8,12},{12,8},{9,1... | collective-permute-start | bytes 589832 | tf_op jit(solution)/shard_map/ppermute | solution.py:121
  101.2 7.1 %collective-permute-start.40 = (bf16[48,2048]{1,0:T(8,128)(2,1)S(1)}, bf16[48,2048]{1,0:T(8,128)(2,1)S(1)}, u32[]{:S(2)}, u32[]{:S(2)}) collective-permute-start(bf16[48,2048]{1,0:T(8,128)(2,1)S(1)} %get-tuple-element.28), channel_id=1, source_target_pairs={{0,4},{4,0},{1,5},{5,1},{2,6},{6,2},{3,7},{7,3},{8,12},{12,8},{9,1... | collective-permute-start | bytes 589832 | tf_op jit(solution)/shard_map/ppermute | solution.py:121
  101.9 10.4 %collective-permute-start.37 = (bf16[48,2048]{1,0:T(8,128)(2,1)S(1)}, bf16[48,2048]{1,0:T(8,128)(2,1)S(1)}, u32[]{:S(2)}, u32[]{:S(2)}) collective-permute-start(bf16[48,2048]{1,0:T(8,128)(2,1)S(1)} %fusion.5), channel_id=1, source_target_pairs={{0,16},{8,24},{16,0},{24,8},{1,17},{9,25},{17,1},{25,9},{2,18},{10... | collective-permute-start | bytes 589832 | tf_op jit(solution)/shard_map/ppermute | solution.py:124
  102.4 9.9 %collective-permute-start.26 = (bf16[48,2048]{1,0:T(8,128)(2,1)S(1)}, bf16[48,2048]{1,0:T(8,128)(2,1)S(1)}, u32[]{:S(2)}, u32[]{:S(2)}) collective-permute-start(bf16[48,2048]{1,0:T(8,128)(2,1)S(1)} %get-tuple-element.31), channel_id=1, source_target_pairs={{0,4},{4,0},{1,5},{5,1},{2,6},{6,2},{3,7},{7,3},{8,12},{12,8},{9,1... | collective-permute-start | bytes 589832 | tf_op jit(solution)/shard_map/ppermute | solution.py:121
  104.1 8.2 %collective-permute-start.28 = (bf16[48,2048]{1,0:T(8,128)(2,1)S(1)}, bf16[48,2048]{1,0:T(8,128)(2,1)S(1)}, u32[]{:S(2)}, u32[]{:S(2)}) collective-permute-start(bf16[48,2048]{1,0:T(8,128)(2,1)S(1)} %get-tuple-element.27), channel_id=1, source_target_pairs={{0,1},{1,0},{2,3},{3,2},{4,5},{5,4},{6,7},{7,6},{8,9},{9,8},{10,11... | collective-permute-start | bytes 589832 | tf_op jit(solution)/shard_map/ppermute | solution.py:122
  (21 other events, 88.2 us)

commit v4 on v3

--- a/solution.py
+++ b/solution.py
@@ -13,13 +13,14 @@
 
 
 STEPS = 3
+BLOCKS = 4
 UNITS = 8
 
 
-def ffn_kernel(layout, cols, fresh, waits, *refs):
+def ffn_kernel(layout, cols, fresh, waits, count, *refs):
     refs = refs[waits:]
     sc, refs = refs[0], refs[1:]
-    pieces, given, outs, refs = refs[:8], refs[8:11], refs[11:15], refs[15:]
+    pieces, given, outs, refs = refs[:count], refs[count : count + 3], refs[count + 3 : count + 7], refs[count + 7 :]
     held = given
     if fresh:
         held, refs = refs[:3], refs[3:]
@@ -67,20 +68,15 @@
         at = pl.multiple_of((other if far else mine) + off, 128)
         o = jnp.dot(h_s[...], wd[:, pl.ds(at, nb)], preferred_element_type=F32).astype(BF)
         for b in range(UNITS):
-            core, plane, side = b // 4, b // 2 % 2, b % 2
-            if side and far:
-                group, unit = 0, plane
-            elif side != far:
-                group, unit = (0, 2 + plane) if side != plane else (2, plane)
-            else:
-                group, unit = 2, 2 + plane
+            core, plane, side = b // BLOCKS, b // 2 % 2, b % 2
+            unit = 3 - 2 * side - far
             k = unit * rows
-            outs[group + core][k : k + rows, off : off + nb] = o[b * rows : (b + 1) * rows]
+            outs[2 * plane + core][k : k + rows, off : off + nb] = o[b * rows : (b + 1) * rows]
 
 
 def ffn(sc, pieces, layout, cols, weights, fresh, first_of_all):
     ff, d = weights[0].shape
-    total = len(layout) * pieces[1].shape[0]
+    total = len(layout) * (pieces[0].shape[0] // BLOCKS)
     vmem = pl.BlockSpec(memory_space=pltpu.VMEM)
     out = [pltpu.VMEM((total // 2, cols), BF)] * 4
     scratch = [pltpu.VMEM((total, d), BF), pltpu.VMEM((total, ff), BF), pltpu.VMEM((total, 128), F32)]
@@ -88,15 +84,15 @@
         out += [pltpu.VMEM(a.shape, BF) for a in weights]
         scratch.append(pltpu.SemaphoreType.DMA((3 * STEPS,)))
     return pl.pallas_call(
-        functools.partial(ffn_kernel, layout, cols, fresh, len(first_of_all)),
+        functools.partial(ffn_kernel, layout, cols, fresh, len(first_of_all), len(pieces)),
         in_specs=[pl.BlockSpec(memory_space=pl.ANY)] * len(first_of_all)
         + [pl.BlockSpec(memory_space=pltpu.SMEM)]
-        + [vmem] * 8
+        + [vmem] * len(pieces)
         + [pl.BlockSpec(memory_space=pltpu.HBM) if fresh else vmem] * 3,
         out_specs=[vmem] * len(out),
         out_shape=out,
         scratch_shapes=scratch,
-        compiler_params=pltpu.CompilerParams(vmem_limit_bytes=(36 if fresh else 8) << 20),
+        compiler_params=pltpu.CompilerParams(vmem_limit_bytes=(30 if fresh else 8) << 20),
         cost_estimate=pl.CostEstimate(
             flops=6 * total * ff * d, bytes_accessed=6 * ff * d + 4 * total * d, transcendentals=total * ff
         ),
@@ -121,6 +117,7 @@
     px = lambda a: lax.ppermute(a, "x", swap)
     py = lambda a: lax.ppermute(a, "y", swap)
     pc = lambda a: lax.ppermute(a, "c", swap)
+    pd = lambda a: lax.ppermute(a, ("x", "y"), [(i, 3 - i) for i in range(4)])
     pz = lambda a, k: lax.ppermute(a, "z", [(i, i ^ k) for i in range(nz)])
 
     w = dense_weights(expert_ids, combine_weights, experts)
@@ -129,41 +126,41 @@
     pad = jnp.zeros((held, 64 - experts), BF)
     t0 = jnp.concatenate([tokens, hi, pad, lo, pad], axis=1)
 
-    t1, t3 = pz(t0, 1), pz(t0, 3)
-    t2 = pz(t3, 1)
-
-    def gather(a, b):
-        xa, yb, ya, xb = px(a), py(b), py(a), px(b)
-        da, db = py(xa), px(yb)
-        return [jnp.concatenate([a, xa, ya]), da, jnp.concatenate([b, xb, yb]), db]
-
-    layout = []
-    for core in (0, 4):
-        for plane in (core, core + 2):
-            layout += [(plane, 0, plane, 2), (plane, 1, plane + 1, 0)]
-
-    def core_sum(parts):
-        send, send_c, keep, keep_c = parts
-        s = (send.astype(F32) + pc(send_c).astype(F32)).astype(BF).reshape(4, held, cols)
-        k = (keep.astype(F32) + pc(keep_c).astype(F32)).reshape(4, held, cols)
-        return s, k
-
-    def scatter(s, k):
-        ra, rb, qa, qb = px(s[0]), py(s[1]), px(s[2]), py(s[3])
-        back_a = py((k[0] + ra.astype(F32)).astype(BF)).astype(F32)
-        back_b = px((k[1] + rb.astype(F32)).astype(BF)).astype(F32)
-        return k[2] + qa.astype(F32) + back_a, k[3] + qb.astype(F32) + back_b
-
-    near, far = gather(t0, t1), gather(t3, t2)
-    near_c = [pc(a) for a in near]
-    far_c = [pc(a) for a in far]
-    *first, wg, wu, wd = ffn(sc, far + far_c, layout, cols, weights, True, near_c)
-    s, k = core_sum(first)
-    last = ffn(sc, near + near_c, layout, cols, (wg, wu, wd), False, [s])
-    u3, u2 = scatter(s, k)
-    u0, u1 = scatter(*core_sum(last))
-    total = u0 + pz(u3.astype(BF), 3).astype(F32) + pz(u2.astype(BF), 2).astype(F32)
-    total = total + pz(u1.astype(BF), 1).astype(F32)
+    t3, t1, x0, y0, d0 = pz(t0, 3), pz(t0, 1), px(t0), py(t0), pd(t0)
+    t2, x3, y3 = pz(t3, 1), px(t3), py(t3)
+    x3, t2, x0, y0, d0 = lax.optimization_barrier((x3, t2, x0, y0, d0))
+    rest0 = jnp.concatenate([y0, x0, d0])
+    d3, x2, y2, d2 = lax.optimization_barrier((py(x3), px(t2), py(t2), pd(t2)))
+    p0, p1, p2, p3 = (
+        jnp.concatenate(blocks)
+        for blocks in ([t0, rest0], [t1, pz(rest0, 1)], [t2, y2, x2, d2], [t3, y3, x3, d3])
+    )
+    layout = [(p, 2 * side, p, 2 * side + 1) for p in range(4) for side in range(2)]
+
+    def core_sum(mine, others):
+        return mine.astype(F32) + pc(others).astype(F32)
+
+    def plane_parts(s):
+        d, x, y, own = s.reshape(BLOCKS, held, cols)
+        return own, px(x), py(y), pd(d)
+
+    *first, wg, wu, wd = ffn(sc, [p3, p1, pc(p3), pc(p1)], layout, cols, weights, True, [])
+    s3, s1 = core_sum(*first[:2]).astype(BF), core_sum(*first[2:]).astype(BF)
+    last = ffn(sc, [p2, p0, pc(p2), pc(p0)], layout, cols, (wg, wu, wd), False, [s3, s1])
+    last = list(last)
+    d1, x1, y1, own1 = s1.reshape(BLOCKS, held, cols)
+    to1 = s1[: 2 * held]
+    held_back = lax.optimization_barrier((*last, own1, pz(to1, 1), py(y1), *plane_parts(s3)))
+    last, own1, back1, back_y, parts3 = held_back[:4], *held_back[4:7], held_back[7:]
+    back3 = pz(sum(p.astype(F32) for p in parts3).astype(BF), 3)
+    own1 = pz((own1.astype(F32) + back_y.astype(F32)).astype(BF), 1)
+    s2 = core_sum(*last[:2]).astype(BF)
+    parts2 = plane_parts(s2)
+    back2 = pz(sum(p.astype(F32) for p in parts2).astype(BF), 2)
+    s0 = core_sum(*last[2:])
+    s0 = s0 + jnp.concatenate([back1.astype(F32), jnp.zeros((2 * held, cols), F32)])
+    total = sum(p.astype(F32) for p in plane_parts(s0.astype(BF)))
+    total = total + own1.astype(F32) + back3.astype(F32) + back2.astype(F32)
     return total.astype(BF)
 
 

time: 115 us -> 105 us (0.913)
  waiting for transfers between devices: 47.9 us -> 35.4 us
  starting transfers between devices: 36 us -> 44 us
  local copies, waits for them, and re-layouts: 6.42 us -> 1.91 us
    ppermute x6 -> x8, starting transfers between devices: 7.22 us -> 17.1 us  [on_device(): pz = lambda a, k: lax.ppermute(a, 'z', [(i, i ^ k) for i in range(nz)])]
    ppermute x0 -> x5, starting transfers between devices: none -> 5.33 us  [on_device(): pd = lambda a: lax.ppermute(a, ('x', 'y'), [(i, 3 - i) for i in range(4)])]
    ppermute x12 -> x6, waiting for transfers between devices: 14.2 us -> 8.87 us  [on_device(): px = lambda a: lax.ppermute(a, 'x', swap)]
    ppermute x12 -> x8, starting transfers between devices: 16.4 us -> 11.3 us  [on_device(): py = lambda a: lax.ppermute(a, 'y', swap)]
    ppermute x12 -> x8, waiting for transfers between devices: 16.9 us -> 12.6 us  [on_device(): py = lambda a: lax.ppermute(a, 'y', swap)]
    ppermute x6 -> x8, waiting for transfers between devices: 12.2 us -> 8.62 us  [on_device(): pz = lambda a, k: lax.ppermute(a, 'z', [(i, i ^ k) for i in range(nz)])]
    unnamed x28 -> x19, local copies, waits for them, and re-layouts: 3.66 us -> 0.39 us
    ppermute x0 -> x5, waiting for transfers between devices: none -> 2.33 us  [on_device(): pd = lambda a: lax.ppermute(a, ('x', 'y'), [(i, 3 - i) for i in range(4)])]
  transfers between devices with their start and end apart: 42 -> 35, of which waited for: 19 -> 18; matrix products, arithmetic and copies ran while one was open for 6% -> 2% of each run, Pallas kernels for 7% -> 19%
where the time goes in v4:
time: 105 us
  starting transfers between devices  44 us (42%)
  waiting for transfers between devices  35.4 us (34%)
  Pallas kernels  20.2 us (19%)
  other arithmetic  3.19 us (3%)
  local copies, waits for them, and re-layouts  1.91 us (2%)
    pallas_call x2, Pallas kernels, ffn(): pl.pallas_call(functools.partial(ffn_kernel, layout, cols, fresh, len(fir...  20.2 us
    ppermute x8, starting transfers between devices, on_device(): pz = lambda a, k: lax.ppermute(a, 'z', [(i, i ^ k) for i in range(nz)])  17.1 us
    ppermute x8, waiting for transfers between devices, on_device(): py = lambda a: lax.ppermute(a, 'y', swap)  12.6 us
    ppermute x8, starting transfers between devices, on_device(): py = lambda a: lax.ppermute(a, 'y', swap)  11.3 us
    ppermute x6, waiting for transfers between devices, on_device(): px = lambda a: lax.ppermute(a, 'x', swap)  8.87 us
    ppermute x8, waiting for transfers between devices, on_device(): pz = lambda a, k: lax.ppermute(a, 'z', [(i, i ^ k) for i in range(nz)])  8.62 us
    ppermute x6, starting transfers between devices, on_device(): px = lambda a: lax.ppermute(a, 'x', swap)  8.33 us
    ppermute x5, starting transfers between devices, on_device(): pd = lambda a: lax.ppermute(a, ('x', 'y'), [(i, 3 - i) for i in range(4)])  5.33 us
  transfers between devices with their start and end apart: 35, of which 18 were waited for; matrix products, arithmetic and copies ran while one was open for 2% of the time, Pallas kernels for 19%

profile of v4, /device:TPU:0, one launch (start us, length us, event | category | flops | bytes accessed | tf_op | source)
XLA Modules:
  0.0 105.0 jit_solution(12666075118697892736)
XLA Ops:
  2.0 5.1 %collective-permute-start = (bf16[48,2176]{1,0:T(8,128)(2,1)S(1)}, bf16[48,2176]{1,0:T(8,128)(2,1)S(1)}, u32[]{:S(2)}, u32[]{:S(2)}) collective-permute-start(bf16[48,2176]{1,0:T(8,128)(2,1)S(1)} %concatenate.24), channel_id=1, source_target_pairs={{0,24},{8,16},{16,8},{24,0},{1,25},{9,17},{17,9},{25,1},{2,26},{10... | collective-permute-start | bytes 626696 | tf_op jit(solution)/shard_map/ppermute | solution.py:121
  7.1 1.5 %collective-permute-start.4 = (bf16[48,2176]{1,0:T(8,128)(2,1)S(1)}, bf16[48,2176]{1,0:T(8,128)(2,1)S(1)}, u32[]{:S(2)}, u32[]{:S(2)}) collective-permute-start(bf16[48,2176]{1,0:T(8,128)(2,1)S(1)} %concatenate.24), channel_id=1, source_target_pairs={{0,4},{4,0},{1,5},{5,1},{2,6},{6,2},{3,7},{7,3},{8,12},{12,8},{9,1... | collective-permute-start | bytes 626696 | tf_op jit(solution)/shard_map/ppermute | solution.py:117
  8.6 1.5 %collective-permute-start.5 = (bf16[48,2176]{1,0:T(8,128)(2,1)S(1)}, bf16[48,2176]{1,0:T(8,128)(2,1)S(1)}, u32[]{:S(2)}, u32[]{:S(2)}) collective-permute-start(bf16[48,2176]{1,0:T(8,128)(2,1)S(1)} %concatenate.24), channel_id=1, source_target_pairs={{0,1},{1,0},{2,3},{3,2},{4,5},{5,4},{6,7},{7,6},{8,9},{9,8},{10,11... | collective-permute-start | bytes 626696 | tf_op jit(solution)/shard_map/ppermute | solution.py:118
  10.6 2.5 %collective-permute-done = bf16[48,2176]{1,0:T(8,128)(2,1)S(1)} collective-permute-done((bf16[48,2176]{1,0:T(8,128)(2,1)S(1)}, bf16[48,2176]{1,0:T(8,128)(2,1)S(1)}, u32[]{:S(2)}, u32[]{:S(2)}) %collective-permute-start) | collective-permute-done | bytes 208928 | tf_op jit(solution)/shard_map/ppermute | solution.py:121
  13.1 1.7 %collective-permute-start.2 = (bf16[48,2176]{1,0:T(8,128)(2,1)S(1)}, bf16[48,2176]{1,0:T(8,128)(2,1)S(1)}, u32[]{:S(2)}, u32[]{:S(2)}) collective-permute-start(bf16[48,2176]{1,0:T(8,128)(2,1)S(1)} %collective-permute-done), channel_id=1, source_target_pairs={{0,4},{4,0},{1,5},{5,1},{2,6},{6,2},{3,7},{7,3},{8,12},{12,8},{9,1... | collective-permute-start | bytes 626696 | tf_op jit(solution)/shard_map/ppermute | solution.py:117
  14.8 2.1 %collective-permute-done.11 = bf16[48,2176]{1,0:T(8,128)(2,1)S(1)} collective-permute-done((bf16[48,2176]{1,0:T(8,128)(2,1)S(1)}, bf16[48,2176]{1,0:T(8,128)(2,1)S(1)}, u32[]{:S(2)}, u32[]{:S(2)}) %collective-permute-start.11) | collective-permute-done | bytes 208928 | tf_op jit(solution)/shard_map/ppermute | solution.py:121
  17.0 1.5 %collective-permute-start.3 = (bf16[48,2176]{1,0:T(8,128)(2,1)S(1)}, bf16[48,2176]{1,0:T(8,128)(2,1)S(1)}, u32[]{:S(2)}, u32[]{:S(2)}) collective-permute-start(bf16[48,2176]{1,0:T(8,128)(2,1)S(1)} %collective-permute-done), channel_id=1, source_target_pairs={{0,8},{8,0},{16,24},{24,16},{1,9},{9,1},{17,25},{25,17},{2,10},{10... | collective-permute-start | bytes 626696 | tf_op jit(solution)/shard_map/ppermute | solution.py:121
  18.5 1.6 %collective-permute-start.1 = (bf16[48,2176]{1,0:T(8,128)(2,1)S(1)}, bf16[48,2176]{1,0:T(8,128)(2,1)S(1)}, u32[]{:S(2)}, u32[]{:S(2)}) collective-permute-start(bf16[48,2176]{1,0:T(8,128)(2,1)S(1)} %collective-permute-done), channel_id=1, source_target_pairs={{0,1},{1,0},{2,3},{3,2},{4,5},{5,4},{6,7},{7,6},{8,9},{9,8},{10,11... | collective-permute-start | bytes 626696 | tf_op jit(solution)/shard_map/ppermute | solution.py:118
  20.6 2.1 %collective-permute-done.2 = bf16[48,2176]{1,0:T(8,128)(2,1)S(1)} collective-permute-done((bf16[48,2176]{1,0:T(8,128)(2,1)S(1)}, bf16[48,2176]{1,0:T(8,128)(2,1)S(1)}, u32[]{:S(2)}, u32[]{:S(2)}) %collective-permute-start.2) | collective-permute-done | bytes 208928 | tf_op jit(solution)/shard_map/ppermute | solution.py:117
  22.8 2.5 %collective-permute-start.10 = (bf16[48,2176]{1,0:T(8,128)(2,1)S(1)}, bf16[48,2176]{1,0:T(8,128)(2,1)S(1)}, u32[]{:S(2)}, u32[]{:S(2)}) collective-permute-start(bf16[48,2176]{1,0:T(8,128)(2,1)S(1)} %collective-permute-done.3), channel_id=1, source_target_pairs={{0,5},{1,4},{4,1},{5,0},{2,7},{3,6},{6,3},{7,2},{8,13},{9,12},{12,... | collective-permute-start | bytes 626696 | tf_op jit(solution)/shard_map/ppermute | solution.py:120
  26.4 1.8 %collective-permute-start.12 = (bf16[144,2176]{1,0:T(8,128)(2,1)S(1)}, bf16[144,2176]{1,0:T(8,128)(2,1)S(1)}, u32[]{:S(2)}, u32[]{:S(2)}) collective-permute-start(bf16[144,2176]{1,0:T(8,128)(2,1)S(1)} %pad_maximum_fusion.1), channel_id=1, source_target_pairs={{0,8},{8,0},{16,24},{24,16},{1,9},{9,1},{17,25},{25,17},{2,10},{10... | collective-permute-start | bytes 1880072 | tf_op jit(solution)/shard_map/ppermute | solution.py:121
  28.2 1.5 %collective-permute-start.7 = (bf16[48,2176]{1,0:T(8,128)(2,1)S(1)}, bf16[48,2176]{1,0:T(8,128)(2,1)S(1)}, u32[]{:S(2)}, u32[]{:S(2)}) collective-permute-start(bf16[48,2176]{1,0:T(8,128)(2,1)S(1)} %collective-permute-done.2), channel_id=1, source_target_pairs={{0,1},{1,0},{2,3},{3,2},{4,5},{5,4},{6,7},{7,6},{8,9},{9,8},{10,11... | collective-permute-start | bytes 626696 | tf_op jit(solution)/shard_map/ppermute | solution.py:118
  29.8 1.8 %collective-permute-done.10 = bf16[48,2176]{1,0:T(8,128)(2,1)S(1)} collective-permute-done((bf16[48,2176]{1,0:T(8,128)(2,1)S(1)}, bf16[48,2176]{1,0:T(8,128)(2,1)S(1)}, u32[]{:S(2)}, u32[]{:S(2)}) %collective-permute-start.10) | collective-permute-done | bytes 208928 | tf_op jit(solution)/shard_map/ppermute | solution.py:120
  31.6 2.3 %collective-permute-done.8 = bf16[48,2176]{1,0:T(8,128)(2,1)S(1)} collective-permute-done((bf16[48,2176]{1,0:T(8,128)(2,1)S(1)}, bf16[48,2176]{1,0:T(8,128)(2,1)S(1)}, u32[]{:S(2)}, u32[]{:S(2)}) %collective-permute-start.8) | collective-permute-done | bytes 208928 | tf_op jit(solution)/shard_map/ppermute | solution.py:117
  35.2 3.1 %collective-permute-done.7 = bf16[48,2176]{1,0:T(8,128)(2,1)S(1)} collective-permute-done((bf16[48,2176]{1,0:T(8,128)(2,1)S(1)}, bf16[48,2176]{1,0:T(8,128)(2,1)S(1)}, u32[]{:S(2)}, u32[]{:S(2)}) %collective-permute-start.7) | collective-permute-done | bytes 208928 | tf_op jit(solution)/shard_map/ppermute | solution.py:118
  38.4 1.8 %collective-permute-done.12 = bf16[144,2176]{1,0:T(8,128)(2,1)S(1)} collective-permute-done((bf16[144,2176]{1,0:T(8,128)(2,1)S(1)}, bf16[144,2176]{1,0:T(8,128)(2,1)S(1)}, u32[]{:S(2)}, u32[]{:S(2)}) %collective-permute-start.12) | collective-permute-done | bytes 626720 | tf_op jit(solution)/shard_map/ppermute | solution.py:121
  41.3 1.5 %collective-permute-done.14.refs_4_ = bf16[192,2176]{1,0:T(8,128)(2,1)} collective-permute-done((bf16[192,2176]{1,0:T(8,128)(2,1)S(1)}, bf16[192,2176]{1,0:T(8,128)(2,1)}, u32[]{:S(2)}, u32[]{:S(2)}) %collective-permute-start.14) | collective-permute-done | bytes 835616 | tf_op jit(solution)/shard_map/ppermute | solution.py:119
  42.8 11.7 %ffn.2 = (bf16[192,2048]{1,0:T(8,128)(2,1)S(1)}, bf16[192,2048]{1,0:T(8,128)(2,1)S(1)}, bf16[192,2048]{1,0:T(8,128)(2,1)S(1)}, bf16[192,2048]{1,0:T(8,128)(2,1)S...) custom-call(s32[2]{0:T(128)S(1)} %pad_add_fusion.refs_0_.refs_2_, ...), custom_call_target="tpu_custom_call" | custom-call | flops 7247757312 | bytes 25165824 | tf_op jit(solution)/shard_map/ffn/pallas_call | solution.py:86
  55.4 1.5 %collective-permute-done.16 = bf16[192,2048]{1,0:T(8,128)(2,1)S(1)} collective-permute-done((bf16[192,2048]{1,0:T(8,128)(2,1)S(1)}, bf16[192,2048]{1,0:T(8,128)(2,1)S(1)}, u32[]{:S(2)}, u32[]{:S(2)}) %collective-permute-start.16) | collective-permute-done | bytes 786464 | tf_op jit(solution)/shard_map/ppermute | solution.py:119
  58.6 1.6 %collective-permute-start.20 = (bf16[48,2048]{1,0:T(8,128)(2,1)S(1)}, bf16[48,2048]{1,0:T(8,128)(2,1)S(1)}, u32[]{:S(2)}, u32[]{:S(2)}) collective-permute-start(bf16[48,2048]{1,0:T(8,128)(2,1)S(1)} %get-tuple-element.77), channel_id=1, source_target_pairs={{0,1},{1,0},{2,3},{3,2},{4,5},{5,4},{6,7},{7,6},{8,9},{9,8},{10,11... | collective-permute-start | bytes 589832 | tf_op jit(solution)/shard_map/ppermute | solution.py:118
  60.5 1.6 %collective-permute-start.21 = (bf16[48,2048]{1,0:T(8,128)(2,1)S(1)}, bf16[48,2048]{1,0:T(8,128)(2,1)S(1)}, u32[]{:S(2)}, u32[]{:S(2)}) collective-permute-start(bf16[48,2048]{1,0:T(8,128)(2,1)S(1)} %get-tuple-element.75), channel_id=1, source_target_pairs={{0,4},{4,0},{1,5},{5,1},{2,6},{6,2},{3,7},{7,3},{8,12},{12,8},{9,1... | collective-permute-start | bytes 589832 | tf_op jit(solution)/shard_map/ppermute | solution.py:117
  62.6 1.5 %collective-permute-start.23 = (bf16[48,2048]{1,0:T(8,128)(2,1)S(1)}, bf16[48,2048]{1,0:T(8,128)(2,1)S(1)}, u32[]{:S(2)}, u32[]{:S(2)}) collective-permute-start(bf16[48,2048]{1,0:T(8,128)(2,1)S(1)} %get-tuple-element.73), channel_id=1, source_target_pairs={{0,5},{1,4},{4,1},{5,0},{2,7},{3,6},{6,3},{7,2},{8,13},{9,12},{12,... | collective-permute-start | bytes 589832 | tf_op jit(solution)/shard_map/ppermute | solution.py:120
  64.1 8.5 %ffn.3 = (bf16[192,2048]{1,0:T(8,128)(2,1)S(1)}, bf16[192,2048]{1,0:T(8,128)(2,1)S(1)}, bf16[192,2048]{1,0:T(8,128)(2,1)S(1)}, bf16[192,2048]{1,0:T(8,128)(2,1)S(1)}) custom-call(bf16[192,2048]{1,0:T(8,128)(2,1)S(1)} %add_convert_fusion.3.refs_0_, bf16[192,2048]{1,0:T(8,128)(2,1)S(1)} %add_convert_fusion.2.refs_1_, s32[2]{0:T(128)S(1)} %pad_add_fusion.refs_0_.refs_2_, ...), custom_call_target="tpu_custom_call" | custom-call | flops 7247757312 | bytes 25165824 | tf_op jit(solution)/shard_map/ffn/pallas_call | solution.py:86
  75.2 5.3 %collective-permute-start.29 = (bf16[48,2048]{1,0:T(8,128)(2,1)S(1)}, bf16[48,2048]{1,0:T(8,128)(2,1)S(1)}, u32[]{:S(2)}, u32[]{:S(2)}) collective-permute-start(bf16[48,2048]{1,0:T(8,128)(2,1)S(1)} %add_convert_fusion.6), channel_id=1, source_target_pairs={{0,24},{8,16},{16,8},{24,0},{1,25},{9,17},{17,9},{25,1},{2,26},{10... | collective-permute-start | bytes 589832 | tf_op jit(solution)/shard_map/ppermute | solution.py:121
  80.8 1.6 %collective-permute-start.31 = (bf16[48,2048]{1,0:T(8,128)(2,1)S(1)}, bf16[48,2048]{1,0:T(8,128)(2,1)S(1)}, u32[]{:S(2)}, u32[]{:S(2)}) collective-permute-start(bf16[48,2048]{1,0:T(8,128)(2,1)S(1)} %get-tuple-element.70), channel_id=1, source_target_pairs={{0,4},{4,0},{1,5},{5,1},{2,6},{6,2},{3,7},{7,3},{8,12},{12,8},{9,1... | collective-permute-start | bytes 589832 | tf_op jit(solution)/shard_map/ppermute | solution.py:117
  82.4 1.5 %collective-permute-start.32 = (bf16[48,2048]{1,0:T(8,128)(2,1)S(1)}, bf16[48,2048]{1,0:T(8,128)(2,1)S(1)}, u32[]{:S(2)}, u32[]{:S(2)}) collective-permute-start(bf16[48,2048]{1,0:T(8,128)(2,1)S(1)} %get-tuple-element.72), channel_id=1, source_target_pairs={{0,1},{1,0},{2,3},{3,2},{4,5},{5,4},{6,7},{7,6},{8,9},{9,8},{10,11... | collective-permute-start | bytes 589832 | tf_op jit(solution)/shard_map/ppermute | solution.py:118
  84.8 3.9 %collective-permute-done.31 = bf16[48,2048]{1,0:T(8,128)(2,1)S(1)} collective-permute-done((bf16[48,2048]{1,0:T(8,128)(2,1)S(1)}, bf16[48,2048]{1,0:T(8,128)(2,1)S(1)}, u32[]{:S(2)}, u32[]{:S(2)}) %collective-permute-start.31) | collective-permute-done | bytes 196640 | tf_op jit(solution)/shard_map/ppermute | solution.py:117
  88.7 1.5 %collective-permute-start.25 = (bf16[48,2048]{1,0:T(8,128)(2,1)S(1)}, bf16[48,2048]{1,0:T(8,128)(2,1)S(1)}, u32[]{:S(2)}, u32[]{:S(2)}) collective-permute-start(bf16[48,2048]{1,0:T(8,128)(2,1)S(1)} %get-tuple-element.67), channel_id=1, source_target_pairs={{0,4},{4,0},{1,5},{5,1},{2,6},{6,2},{3,7},{7,3},{8,12},{12,8},{9,1... | collective-permute-start | bytes 589832 | tf_op jit(solution)/shard_map/ppermute | solution.py:117
  90.2 2.1 %collective-permute-done.32 = bf16[48,2048]{1,0:T(8,128)(2,1)S(1)} collective-permute-done((bf16[48,2048]{1,0:T(8,128)(2,1)S(1)}, bf16[48,2048]{1,0:T(8,128)(2,1)S(1)}, u32[]{:S(2)}, u32[]{:S(2)}) %collective-permute-start.32) | collective-permute-done | bytes 196640 | tf_op jit(solution)/shard_map/ppermute | solution.py:118
  92.3 2.6 %collective-permute-start.26 = (bf16[48,2048]{1,0:T(8,128)(2,1)S(1)}, bf16[48,2048]{1,0:T(8,128)(2,1)S(1)}, u32[]{:S(2)}, u32[]{:S(2)}) collective-permute-start(bf16[48,2048]{1,0:T(8,128)(2,1)S(1)} %get-tuple-element.69), channel_id=1, source_target_pairs={{0,1},{1,0},{2,3},{3,2},{4,5},{5,4},{6,7},{7,6},{8,9},{9,8},{10,11... | collective-permute-start | bytes 589832 | tf_op jit(solution)/shard_map/ppermute | solution.py:118
  97.2 4.9 %collective-permute-done.26 = bf16[48,2048]{1,0:T(8,128)(2,1)S(1)} collective-permute-done((bf16[48,2048]{1,0:T(8,128)(2,1)S(1)}, bf16[48,2048]{1,0:T(8,128)(2,1)S(1)}, u32[]{:S(2)}, u32[]{:S(2)}) %collective-permute-start.26) | collective-permute-done | bytes 196640 | tf_op jit(solution)/shard_map/ppermute | solution.py:118
  102.1 2.0 %collective-permute-done.34 = bf16[48,2048]{1,0:T(8,128)(2,1)S(1)} collective-permute-done((bf16[48,2048]{1,0:T(8,128)(2,1)S(1)}, bf16[48,2048]{1,0:T(8,128)(2,1)S(1)}, u32[]{:S(2)}, u32[]{:S(2)}) %collective-permute-start.34) | collective-permute-done | bytes 196640 | tf_op jit(solution)/shard_map/ppermute | solution.py:121
  (85 shorter events, 17.0 us)
Async XLA Ops:
  2.0 11.1 %collective-permute-start = (bf16[48,2176]{1,0:T(8,128)(2,1)S(1)}, bf16[48,2176]{1,0:T(8,128)(2,1)S(1)}, u32[]{:S(2)}, u32[]{:S(2)}) collective-permute-start(bf16[48,2176]{1,0:T(8,128)(2,1)S(1)} %concatenate.24), channel_id=1, source_target_pairs={{0,24},{8,16},{16,8},{24,0},{1,25},{9,17},{17,9},{25,1},{2,26},{10... | collective-permute-start | bytes 626696 | tf_op jit(solution)/shard_map/ppermute | solution.py:121
  7.1 11.5 %collective-permute-start.4 = (bf16[48,2176]{1,0:T(8,128)(2,1)S(1)}, bf16[48,2176]{1,0:T(8,128)(2,1)S(1)}, u32[]{:S(2)}, u32[]{:S(2)}) collective-permute-start(bf16[48,2176]{1,0:T(8,128)(2,1)S(1)} %concatenate.24), channel_id=1, source_target_pairs={{0,4},{4,0},{1,5},{5,1},{2,6},{6,2},{3,7},{7,3},{8,12},{12,8},{9,1... | collective-permute-start | bytes 626696 | tf_op jit(solution)/shard_map/ppermute | solution.py:117
  8.6 11.6 %collective-permute-start.5 = (bf16[48,2176]{1,0:T(8,128)(2,1)S(1)}, bf16[48,2176]{1,0:T(8,128)(2,1)S(1)}, u32[]{:S(2)}, u32[]{:S(2)}) collective-permute-start(bf16[48,2176]{1,0:T(8,128)(2,1)S(1)} %concatenate.24), channel_id=1, source_target_pairs={{0,1},{1,0},{2,3},{3,2},{4,5},{5,4},{6,7},{7,6},{8,9},{9,8},{10,11... | collective-permute-start | bytes 626696 | tf_op jit(solution)/shard_map/ppermute | solution.py:118
  10.1 10.6 %collective-permute-start.6 = (bf16[48,2176]{1,0:T(8,128)(2,1)S(1)}, bf16[48,2176]{1,0:T(8,128)(2,1)S(1)}, u32[]{:S(2)}, u32[]{:S(2)}) collective-permute-start(bf16[48,2176]{1,0:T(8,128)(2,1)S(1)} %concatenate.24), channel_id=1, source_target_pairs={{0,5},{1,4},{4,1},{5,0},{2,7},{3,6},{6,3},{7,2},{8,13},{9,12},{12,... | collective-permute-start | bytes 626696 | tf_op jit(solution)/shard_map/ppermute | solution.py:120
  10.6 6.4 %collective-permute-start.11 = (bf16[48,2176]{1,0:T(8,128)(2,1)S(1)}, bf16[48,2176]{1,0:T(8,128)(2,1)S(1)}, u32[]{:S(2)}, u32[]{:S(2)}) collective-permute-start(bf16[48,2176]{1,0:T(8,128)(2,1)S(1)} %concatenate.24), channel_id=1, source_target_pairs={{0,8},{8,0},{16,24},{24,16},{1,9},{9,1},{17,25},{25,17},{2,10},{10... | collective-permute-start | bytes 626696 | tf_op jit(solution)/shard_map/ppermute | solution.py:121
  13.1 9.6 %collective-permute-start.2 = (bf16[48,2176]{1,0:T(8,128)(2,1)S(1)}, bf16[48,2176]{1,0:T(8,128)(2,1)S(1)}, u32[]{:S(2)}, u32[]{:S(2)}) collective-permute-start(bf16[48,2176]{1,0:T(8,128)(2,1)S(1)} %collective-permute-done), channel_id=1, source_target_pairs={{0,4},{4,0},{1,5},{5,1},{2,6},{6,2},{3,7},{7,3},{8,12},{12,8},{9,1... | collective-permute-start | bytes 626696 | tf_op jit(solution)/shard_map/ppermute | solution.py:117
  17.0 5.9 %collective-permute-start.3 = (bf16[48,2176]{1,0:T(8,128)(2,1)S(1)}, bf16[48,2176]{1,0:T(8,128)(2,1)S(1)}, u32[]{:S(2)}, u32[]{:S(2)}) collective-permute-start(bf16[48,2176]{1,0:T(8,128)(2,1)S(1)} %collective-permute-done), channel_id=1, source_target_pairs={{0,8},{8,0},{16,24},{24,16},{1,9},{9,1},{17,25},{25,17},{2,10},{10... | collective-permute-start | bytes 626696 | tf_op jit(solution)/shard_map/ppermute | solution.py:121
  18.5 9.7 %collective-permute-start.1 = (bf16[48,2176]{1,0:T(8,128)(2,1)S(1)}, bf16[48,2176]{1,0:T(8,128)(2,1)S(1)}, u32[]{:S(2)}, u32[]{:S(2)}) collective-permute-start(bf16[48,2176]{1,0:T(8,128)(2,1)S(1)} %collective-permute-done), channel_id=1, source_target_pairs={{0,1},{1,0},{2,3},{3,2},{4,5},{5,4},{6,7},{7,6},{8,9},{9,8},{10,11... | collective-permute-start | bytes 626696 | tf_op jit(solution)/shard_map/ppermute | solution.py:118
  22.8 8.7 %collective-permute-start.10 = (bf16[48,2176]{1,0:T(8,128)(2,1)S(1)}, bf16[48,2176]{1,0:T(8,128)(2,1)S(1)}, u32[]{:S(2)}, u32[]{:S(2)}) collective-permute-start(bf16[48,2176]{1,0:T(8,128)(2,1)S(1)} %collective-permute-done.3), channel_id=1, source_target_pairs={{0,5},{1,4},{4,1},{5,0},{2,7},{3,6},{6,3},{7,2},{8,13},{9,12},{12,... | collective-permute-start | bytes 626696 | tf_op jit(solution)/shard_map/ppermute | solution.py:120
  25.3 8.6 %collective-permute-start.8 = (bf16[48,2176]{1,0:T(8,128)(2,1)S(1)}, bf16[48,2176]{1,0:T(8,128)(2,1)S(1)}, u32[]{:S(2)}, u32[]{:S(2)}) collective-permute-start(bf16[48,2176]{1,0:T(8,128)(2,1)S(1)} %collective-permute-done.3), channel_id=1, source_target_pairs={{0,4},{4,0},{1,5},{5,1},{2,6},{6,2},{3,7},{7,3},{8,12},{12,8},{9,1... | collective-permute-start | bytes 626696 | tf_op jit(solution)/shard_map/ppermute | solution.py:117
  25.9 9.3 %collective-permute-start.9 = (bf16[48,2176]{1,0:T(8,128)(2,1)S(1)}, bf16[48,2176]{1,0:T(8,128)(2,1)S(1)}, u32[]{:S(2)}, u32[]{:S(2)}) collective-permute-start(bf16[48,2176]{1,0:T(8,128)(2,1)S(1)} %collective-permute-done.3), channel_id=1, source_target_pairs={{0,1},{1,0},{2,3},{3,2},{4,5},{5,4},{6,7},{7,6},{8,9},{9,8},{10,11... | collective-permute-start | bytes 626696 | tf_op jit(solution)/shard_map/ppermute | solution.py:118
  26.4 13.7 %collective-permute-start.12 = (bf16[144,2176]{1,0:T(8,128)(2,1)S(1)}, bf16[144,2176]{1,0:T(8,128)(2,1)S(1)}, u32[]{:S(2)}, u32[]{:S(2)}) collective-permute-start(bf16[144,2176]{1,0:T(8,128)(2,1)S(1)} %pad_maximum_fusion.1), channel_id=1, source_target_pairs={{0,8},{8,0},{16,24},{24,16},{1,9},{9,1},{17,25},{25,17},{2,10},{10... | collective-permute-start | bytes 1880072 | tf_op jit(solution)/shard_map/ppermute | solution.py:121
  28.2 10.1 %collective-permute-start.7 = (bf16[48,2176]{1,0:T(8,128)(2,1)S(1)}, bf16[48,2176]{1,0:T(8,128)(2,1)S(1)}, u32[]{:S(2)}, u32[]{:S(2)}) collective-permute-start(bf16[48,2176]{1,0:T(8,128)(2,1)S(1)} %collective-permute-done.2), channel_id=1, source_target_pairs={{0,1},{1,0},{2,3},{3,2},{4,5},{5,4},{6,7},{7,6},{8,9},{9,8},{10,11... | collective-permute-start | bytes 626696 | tf_op jit(solution)/shard_map/ppermute | solution.py:118
  40.5 21.6 %collective-permute-start.18 = (bf16[192,2176]{1,0:T(8,128)(2,1)S(1)}, bf16[192,2176]{1,0:T(8,128)(2,1)S(1)}, u32[]{:S(2)}, u32[]{:S(2)}) collective-permute-start(bf16[192,2176]{1,0:T(8,128)(2,1)S(1)} %pad_maximum_fusion.refs_4_), channel_id=1, source_target_pairs={{0,2},{2,0},{1,3},{3,1},{4,6},{6,4},{5,7},{7,5},{8,10},{10,8},{9,1... | collective-permute-start | bytes 2506760 | tf_op jit(solution)/shard_map/ppermute | solution.py:119
  54.8 7.8 %collective-permute-start.17 = (bf16[192,2176]{1,0:T(8,128)(2,1)S(1)}, bf16[192,2176]{1,0:T(8,128)(2,1)S(1)}, u32[]{:S(2)}, u32[]{:S(2)}) collective-permute-start(bf16[192,2176]{1,0:T(8,128)(2,1)S(1)} %constant_dynamic-update-slice_fusion.6.refs_3_), channel_id=1, source_target_pairs={{0,2},{2,0},{1,3},{3,1},{4,6},{6,4},{5,7},{7,5},{8,10},{10,8},{9,1... | collective-permute-start | bytes 2506760 | tf_op jit(solution)/shard_map/ppermute | solution.py:119
  55.2 4.9 %collective-permute-start.15 = (bf16[192,2048]{1,0:T(8,128)(2,1)S(1)}, bf16[192,2048]{1,0:T(8,128)(2,1)S(1)}, u32[]{:S(2)}, u32[]{:S(2)}) collective-permute-start(bf16[192,2048]{1,0:T(8,128)(2,1)S(1)} %get-tuple-element.43), channel_id=1, source_target_pairs={{0,2},{2,0},{1,3},{3,1},{4,6},{6,4},{5,7},{7,5},{8,10},{10,8},{9,1... | collective-permute-start | bytes 2359304 | tf_op jit(solution)/shard_map/ppermute | solution.py:119
  57.1 16.6 %collective-permute-start.19 = (bf16[96,2048]{1,0:T(8,128)(2,1)S(1)}, bf16[96,2048]{1,0:T(8,128)(2,1)S(1)}, u32[]{:S(2)}, u32[]{:S(2)}) collective-permute-start(bf16[96,2048]{1,0:T(8,128)(2,1)S(1)} %slice.18), channel_id=1, source_target_pairs={{0,8},{8,0},{16,24},{24,16},{1,9},{9,1},{17,25},{25,17},{2,10},{10... | collective-permute-start | bytes 1179656 | tf_op jit(solution)/shard_map/ppermute | solution.py:121
  58.6 14.0 %collective-permute-start.20 = (bf16[48,2048]{1,0:T(8,128)(2,1)S(1)}, bf16[48,2048]{1,0:T(8,128)(2,1)S(1)}, u32[]{:S(2)}, u32[]{:S(2)}) collective-permute-start(bf16[48,2048]{1,0:T(8,128)(2,1)S(1)} %get-tuple-element.77), channel_id=1, source_target_pairs={{0,1},{1,0},{2,3},{3,2},{4,5},{5,4},{6,7},{7,6},{8,9},{9,8},{10,11... | collective-permute-start | bytes 589832 | tf_op jit(solution)/shard_map/ppermute | solution.py:118
  60.5 12.1 %collective-permute-start.21 = (bf16[48,2048]{1,0:T(8,128)(2,1)S(1)}, bf16[48,2048]{1,0:T(8,128)(2,1)S(1)}, u32[]{:S(2)}, u32[]{:S(2)}) collective-permute-start(bf16[48,2048]{1,0:T(8,128)(2,1)S(1)} %get-tuple-element.75), channel_id=1, source_target_pairs={{0,4},{4,0},{1,5},{5,1},{2,6},{6,2},{3,7},{7,3},{8,12},{12,8},{9,1... | collective-permute-start | bytes 589832 | tf_op jit(solution)/shard_map/ppermute | solution.py:117
  62.1 11.7 %collective-permute-start.22 = (bf16[48,2048]{1,0:T(8,128)(2,1)S(1)}, bf16[48,2048]{1,0:T(8,128)(2,1)S(1)}, u32[]{:S(2)}, u32[]{:S(2)}) collective-permute-start(bf16[48,2048]{1,0:T(8,128)(2,1)S(1)} %get-tuple-element.74), channel_id=1, source_target_pairs={{0,1},{1,0},{2,3},{3,2},{4,5},{5,4},{6,7},{7,6},{8,9},{9,8},{10,11... | collective-permute-start | bytes 589832 | tf_op jit(solution)/shard_map/ppermute | solution.py:118
  62.6 11.1 %collective-permute-start.23 = (bf16[48,2048]{1,0:T(8,128)(2,1)S(1)}, bf16[48,2048]{1,0:T(8,128)(2,1)S(1)}, u32[]{:S(2)}, u32[]{:S(2)}) collective-permute-start(bf16[48,2048]{1,0:T(8,128)(2,1)S(1)} %get-tuple-element.73), channel_id=1, source_target_pairs={{0,5},{1,4},{4,1},{5,0},{2,7},{3,6},{6,3},{7,2},{8,13},{9,12},{12,... | collective-permute-start | bytes 589832 | tf_op jit(solution)/shard_map/ppermute | solution.py:120
  73.7 10.2 %collective-permute-start.24 = (bf16[192,2048]{1,0:T(8,128)(2,1)S(1)}, bf16[192,2048]{1,0:T(8,128)(2,1)S(1)}, u32[]{:S(2)}, u32[]{:S(2)}) collective-permute-start(bf16[192,2048]{1,0:T(8,128)(2,1)S(1)} %get-tuple-element.57), channel_id=1, source_target_pairs={{0,2},{2,0},{1,3},{3,1},{4,6},{6,4},{5,7},{7,5},{8,10},{10,8},{9,1... | collective-permute-start | bytes 2359304 | tf_op jit(solution)/shard_map/ppermute | solution.py:119
  73.7 6.8 %collective-permute-start.30 = (bf16[192,2048]{1,0:T(8,128)(2,1)S(1)}, bf16[192,2048]{1,0:T(8,128)(2,1)S(1)}, u32[]{:S(2)}, u32[]{:S(2)}) collective-permute-start(bf16[192,2048]{1,0:T(8,128)(2,1)S(1)} %get-tuple-element.66), channel_id=1, source_target_pairs={{0,2},{2,0},{1,3},{3,1},{4,6},{6,4},{5,7},{7,5},{8,10},{10,8},{9,1... | collective-permute-start | bytes 2359304 | tf_op jit(solution)/shard_map/ppermute | solution.py:119
  74.3 21.2 %collective-permute-start.28 = (bf16[48,2048]{1,0:T(8,128)(2,1)S(1)}, bf16[48,2048]{1,0:T(8,128)(2,1)S(1)}, u32[]{:S(2)}, u32[]{:S(2)}) collective-permute-start(bf16[48,2048]{1,0:T(8,128)(2,1)S(1)} %add_convert_fusion.7), channel_id=1, source_target_pairs={{0,8},{8,0},{16,24},{24,16},{1,9},{9,1},{17,25},{25,17},{2,10},{10... | collective-permute-start | bytes 589832 | tf_op jit(solution)/shard_map/ppermute | solution.py:121
  75.2 21.5 %collective-permute-start.29 = (bf16[48,2048]{1,0:T(8,128)(2,1)S(1)}, bf16[48,2048]{1,0:T(8,128)(2,1)S(1)}, u32[]{:S(2)}, u32[]{:S(2)}) collective-permute-start(bf16[48,2048]{1,0:T(8,128)(2,1)S(1)} %add_convert_fusion.6), channel_id=1, source_target_pairs={{0,24},{8,16},{16,8},{24,0},{1,25},{9,17},{17,9},{25,1},{2,26},{10... | collective-permute-start | bytes 589832 | tf_op jit(solution)/shard_map/ppermute | solution.py:121
  80.8 7.9 %collective-permute-start.31 = (bf16[48,2048]{1,0:T(8,128)(2,1)S(1)}, bf16[48,2048]{1,0:T(8,128)(2,1)S(1)}, u32[]{:S(2)}, u32[]{:S(2)}) collective-permute-start(bf16[48,2048]{1,0:T(8,128)(2,1)S(1)} %get-tuple-element.70), channel_id=1, source_target_pairs={{0,4},{4,0},{1,5},{5,1},{2,6},{6,2},{3,7},{7,3},{8,12},{12,8},{9,1... | collective-permute-start | bytes 589832 | tf_op jit(solution)/shard_map/ppermute | solution.py:117
  82.4 9.9 %collective-permute-start.32 = (bf16[48,2048]{1,0:T(8,128)(2,1)S(1)}, bf16[48,2048]{1,0:T(8,128)(2,1)S(1)}, u32[]{:S(2)}, u32[]{:S(2)}) collective-permute-start(bf16[48,2048]{1,0:T(8,128)(2,1)S(1)} %get-tuple-element.72), channel_id=1, source_target_pairs={{0,1},{1,0},{2,3},{3,2},{4,5},{5,4},{6,7},{7,6},{8,9},{9,8},{10,11... | collective-permute-start | bytes 589832 | tf_op jit(solution)/shard_map/ppermute | solution.py:118
  83.9 11.0 %collective-permute-start.33 = (bf16[48,2048]{1,0:T(8,128)(2,1)S(1)}, bf16[48,2048]{1,0:T(8,128)(2,1)S(1)}, u32[]{:S(2)}, u32[]{:S(2)}) collective-permute-start(bf16[48,2048]{1,0:T(8,128)(2,1)S(1)} %get-tuple-element.71), channel_id=1, source_target_pairs={{0,5},{1,4},{4,1},{5,0},{2,7},{3,6},{6,3},{7,2},{8,13},{9,12},{12,... | collective-permute-start | bytes 589832 | tf_op jit(solution)/shard_map/ppermute | solution.py:120
  88.7 8.5 %collective-permute-start.25 = (bf16[48,2048]{1,0:T(8,128)(2,1)S(1)}, bf16[48,2048]{1,0:T(8,128)(2,1)S(1)}, u32[]{:S(2)}, u32[]{:S(2)}) collective-permute-start(bf16[48,2048]{1,0:T(8,128)(2,1)S(1)} %get-tuple-element.67), channel_id=1, source_target_pairs={{0,4},{4,0},{1,5},{5,1},{2,6},{6,2},{3,7},{7,3},{8,12},{12,8},{9,1... | collective-permute-start | bytes 589832 | tf_op jit(solution)/shard_map/ppermute | solution.py:117
  92.3 9.8 %collective-permute-start.26 = (bf16[48,2048]{1,0:T(8,128)(2,1)S(1)}, bf16[48,2048]{1,0:T(8,128)(2,1)S(1)}, u32[]{:S(2)}, u32[]{:S(2)}) collective-permute-start(bf16[48,2048]{1,0:T(8,128)(2,1)S(1)} %get-tuple-element.69), channel_id=1, source_target_pairs={{0,1},{1,0},{2,3},{3,2},{4,5},{5,4},{6,7},{7,6},{8,9},{9,8},{10,11... | collective-permute-start | bytes 589832 | tf_op jit(solution)/shard_map/ppermute | solution.py:118
  95.0 7.2 %collective-permute-start.27 = (bf16[48,2048]{1,0:T(8,128)(2,1)S(1)}, bf16[48,2048]{1,0:T(8,128)(2,1)S(1)}, u32[]{:S(2)}, u32[]{:S(2)}) collective-permute-start(bf16[48,2048]{1,0:T(8,128)(2,1)S(1)} %get-tuple-element.68), channel_id=1, source_target_pairs={{0,5},{1,4},{4,1},{5,0},{2,7},{3,6},{6,3},{7,2},{8,13},{9,12},{12,... | collective-permute-start | bytes 589832 | tf_op jit(solution)/shard_map/ppermute | solution.py:120
  95.5 8.7 %collective-permute-start.34 = (bf16[48,2048]{1,0:T(8,128)(2,1)S(1)}, bf16[48,2048]{1,0:T(8,128)(2,1)S(1)}, u32[]{:S(2)}, u32[]{:S(2)}) collective-permute-start(bf16[48,2048]{1,0:T(8,128)(2,1)S(1)} %add_convert_fusion.5), channel_id=1, source_target_pairs={{0,16},{8,24},{16,0},{24,8},{1,17},{9,25},{17,1},{25,9},{2,18},{10... | collective-permute-start | bytes 589832 | tf_op jit(solution)/shard_map/ppermute | solution.py:121
  (9 other events, 55.6 us)

commit v5 on v4

--- a/solution.py
+++ b/solution.py
@@ -148,17 +148,16 @@
     s3, s1 = core_sum(*first[:2]).astype(BF), core_sum(*first[2:]).astype(BF)
     last = ffn(sc, [p2, p0, pc(p2), pc(p0)], layout, cols, (wg, wu, wd), False, [s3, s1])
     last = list(last)
-    d1, x1, y1, own1 = s1.reshape(BLOCKS, held, cols)
-    to1 = s1[: 2 * held]
-    held_back = lax.optimization_barrier((*last, own1, pz(to1, 1), py(y1), *plane_parts(s3)))
-    last, own1, back1, back_y, parts3 = held_back[:4], *held_back[4:7], held_back[7:]
+    cut = 3 * held
+    held_back = lax.optimization_barrier((*last, s1[cut:], pz(s1[:cut], 1), *plane_parts(s3)))
+    last, own1, back1, parts3 = held_back[:4], *held_back[4:6], held_back[6:]
     back3 = pz(sum(p.astype(F32) for p in parts3).astype(BF), 3)
-    own1 = pz((own1.astype(F32) + back_y.astype(F32)).astype(BF), 1)
+    own1 = pz(own1, 1)
     s2 = core_sum(*last[:2]).astype(BF)
     parts2 = plane_parts(s2)
     back2 = pz(sum(p.astype(F32) for p in parts2).astype(BF), 2)
     s0 = core_sum(*last[2:])
-    s0 = s0 + jnp.concatenate([back1.astype(F32), jnp.zeros((2 * held, cols), F32)])
+    s0 = s0 + jnp.concatenate([back1.astype(F32), jnp.zeros((held, cols), F32)])
     total = sum(p.astype(F32) for p in plane_parts(s0.astype(BF)))
     total = total + own1.astype(F32) + back3.astype(F32) + back2.astype(F32)
     return total.astype(BF)

time: 105 us -> 104 us (level)
  starting transfers between devices: 44 us -> 40.8 us
  waiting for transfers between devices: 35.4 us -> 37.3 us
    ppermute x8, waiting for transfers between devices: 8.62 us -> 10.3 us  [on_device(): pz = lambda a, k: lax.ppermute(a, 'z', [(i, i ^ k) for i in range(nz)])]
    ppermute x5, starting transfers between devices: 5.33 us -> 3.9 us  [on_device(): pd = lambda a: lax.ppermute(a, ('x', 'y'), [(i, 3 - i) for i in range(4)])]
    ppermute x8, starting transfers between devices: 17.1 us -> 15.9 us  [on_device(): pz = lambda a, k: lax.ppermute(a, 'z', [(i, i ^ k) for i in range(nz)])]
    ppermute x8 -> x7, starting transfers between devices: 11.3 us -> 10.6 us  [on_device(): py = lambda a: lax.ppermute(a, 'y', swap)]
    ppermute x8 -> x7, waiting for transfers between devices: 12.6 us -> 12.5 us  [on_device(): py = lambda a: lax.ppermute(a, 'y', swap)]
  transfers between devices with their start and end apart: 35 -> 34, of which waited for: 18 -> 18; matrix products, arithmetic and copies ran while one was open for 2% -> 2% of each run, Pallas kernels for 19% -> 20%
where the time goes in v5:
time: 104 us
  starting transfers between devices  40.8 us (39%)
  waiting for transfers between devices  37.3 us (36%)
  Pallas kernels  20.2 us (19%)
  other arithmetic  3.16 us (3%)
  local copies, waits for them, and re-layouts  1.92 us (2%)
    pallas_call x2, Pallas kernels, ffn(): pl.pallas_call(functools.partial(ffn_kernel, layout, cols, fresh, len(fir...  20.2 us
    ppermute x8, starting transfers between devices, on_device(): pz = lambda a, k: lax.ppermute(a, 'z', [(i, i ^ k) for i in range(nz)])  15.9 us
    ppermute x7, waiting for transfers between devices, on_device(): py = lambda a: lax.ppermute(a, 'y', swap)  12.5 us
    ppermute x7, starting transfers between devices, on_device(): py = lambda a: lax.ppermute(a, 'y', swap)  10.6 us
    ppermute x8, waiting for transfers between devices, on_device(): pz = lambda a, k: lax.ppermute(a, 'z', [(i, i ^ k) for i in range(nz)])  10.3 us
    ppermute x6, waiting for transfers between devices, on_device(): px = lambda a: lax.ppermute(a, 'x', swap)  9.21 us
    ppermute x6, starting transfers between devices, on_device(): px = lambda a: lax.ppermute(a, 'x', swap)  8.33 us
    ppermute x5, starting transfers between devices, on_device(): pd = lambda a: lax.ppermute(a, ('x', 'y'), [(i, 3 - i) for i in range(4)])  3.9 us
  transfers between devices with their start and end apart: 34, of which 18 were waited for; matrix products, arithmetic and copies ran while one was open for 2% of the time, Pallas kernels for 20%

profile of v5, /device:TPU:0, one launch (start us, length us, event | category | flops | bytes accessed | tf_op | source)
XLA Modules:
  0.0 103.6 jit_solution(6604054478250136072)
XLA Ops:
  2.0 5.1 %collective-permute-start = (bf16[48,2176]{1,0:T(8,128)(2,1)S(1)}, bf16[48,2176]{1,0:T(8,128)(2,1)S(1)}, u32[]{:S(2)}, u32[]{:S(2)}) collective-permute-start(bf16[48,2176]{1,0:T(8,128)(2,1)S(1)} %concatenate.24), channel_id=1, source_target_pairs={{0,24},{8,16},{16,8},{24,0},{1,25},{9,17},{17,9},{25,1},{2,26},{10... | collective-permute-start | bytes 626696 | tf_op jit(solution)/shard_map/ppermute | solution.py:121
  7.1 1.5 %collective-permute-start.4 = (bf16[48,2176]{1,0:T(8,128)(2,1)S(1)}, bf16[48,2176]{1,0:T(8,128)(2,1)S(1)}, u32[]{:S(2)}, u32[]{:S(2)}) collective-permute-start(bf16[48,2176]{1,0:T(8,128)(2,1)S(1)} %concatenate.24), channel_id=1, source_target_pairs={{0,4},{4,0},{1,5},{5,1},{2,6},{6,2},{3,7},{7,3},{8,12},{12,8},{9,1... | collective-permute-start | bytes 626696 | tf_op jit(solution)/shard_map/ppermute | solution.py:117
  8.6 1.5 %collective-permute-start.5 = (bf16[48,2176]{1,0:T(8,128)(2,1)S(1)}, bf16[48,2176]{1,0:T(8,128)(2,1)S(1)}, u32[]{:S(2)}, u32[]{:S(2)}) collective-permute-start(bf16[48,2176]{1,0:T(8,128)(2,1)S(1)} %concatenate.24), channel_id=1, source_target_pairs={{0,1},{1,0},{2,3},{3,2},{4,5},{5,4},{6,7},{7,6},{8,9},{9,8},{10,11... | collective-permute-start | bytes 626696 | tf_op jit(solution)/shard_map/ppermute | solution.py:118
  10.6 2.5 %collective-permute-done = bf16[48,2176]{1,0:T(8,128)(2,1)S(1)} collective-permute-done((bf16[48,2176]{1,0:T(8,128)(2,1)S(1)}, bf16[48,2176]{1,0:T(8,128)(2,1)S(1)}, u32[]{:S(2)}, u32[]{:S(2)}) %collective-permute-start) | collective-permute-done | bytes 208928 | tf_op jit(solution)/shard_map/ppermute | solution.py:121
  13.1 1.7 %collective-permute-start.2 = (bf16[48,2176]{1,0:T(8,128)(2,1)S(1)}, bf16[48,2176]{1,0:T(8,128)(2,1)S(1)}, u32[]{:S(2)}, u32[]{:S(2)}) collective-permute-start(bf16[48,2176]{1,0:T(8,128)(2,1)S(1)} %collective-permute-done), channel_id=1, source_target_pairs={{0,4},{4,0},{1,5},{5,1},{2,6},{6,2},{3,7},{7,3},{8,12},{12,8},{9,1... | collective-permute-start | bytes 626696 | tf_op jit(solution)/shard_map/ppermute | solution.py:117
  14.8 2.1 %collective-permute-done.11 = bf16[48,2176]{1,0:T(8,128)(2,1)S(1)} collective-permute-done((bf16[48,2176]{1,0:T(8,128)(2,1)S(1)}, bf16[48,2176]{1,0:T(8,128)(2,1)S(1)}, u32[]{:S(2)}, u32[]{:S(2)}) %collective-permute-start.11) | collective-permute-done | bytes 208928 | tf_op jit(solution)/shard_map/ppermute | solution.py:121
  17.0 1.5 %collective-permute-start.3 = (bf16[48,2176]{1,0:T(8,128)(2,1)S(1)}, bf16[48,2176]{1,0:T(8,128)(2,1)S(1)}, u32[]{:S(2)}, u32[]{:S(2)}) collective-permute-start(bf16[48,2176]{1,0:T(8,128)(2,1)S(1)} %collective-permute-done), channel_id=1, source_target_pairs={{0,8},{8,0},{16,24},{24,16},{1,9},{9,1},{17,25},{25,17},{2,10},{10... | collective-permute-start | bytes 626696 | tf_op jit(solution)/shard_map/ppermute | solution.py:121
  18.5 1.6 %collective-permute-start.1 = (bf16[48,2176]{1,0:T(8,128)(2,1)S(1)}, bf16[48,2176]{1,0:T(8,128)(2,1)S(1)}, u32[]{:S(2)}, u32[]{:S(2)}) collective-permute-start(bf16[48,2176]{1,0:T(8,128)(2,1)S(1)} %collective-permute-done), channel_id=1, source_target_pairs={{0,1},{1,0},{2,3},{3,2},{4,5},{5,4},{6,7},{7,6},{8,9},{9,8},{10,11... | collective-permute-start | bytes 626696 | tf_op jit(solution)/shard_map/ppermute | solution.py:118
  20.6 2.1 %collective-permute-done.2 = bf16[48,2176]{1,0:T(8,128)(2,1)S(1)} collective-permute-done((bf16[48,2176]{1,0:T(8,128)(2,1)S(1)}, bf16[48,2176]{1,0:T(8,128)(2,1)S(1)}, u32[]{:S(2)}, u32[]{:S(2)}) %collective-permute-start.2) | collective-permute-done | bytes 208928 | tf_op jit(solution)/shard_map/ppermute | solution.py:117
  22.8 2.5 %collective-permute-start.10 = (bf16[48,2176]{1,0:T(8,128)(2,1)S(1)}, bf16[48,2176]{1,0:T(8,128)(2,1)S(1)}, u32[]{:S(2)}, u32[]{:S(2)}) collective-permute-start(bf16[48,2176]{1,0:T(8,128)(2,1)S(1)} %collective-permute-done.3), channel_id=1, source_target_pairs={{0,5},{1,4},{4,1},{5,0},{2,7},{3,6},{6,3},{7,2},{8,13},{9,12},{12,... | collective-permute-start | bytes 626696 | tf_op jit(solution)/shard_map/ppermute | solution.py:120
  26.4 1.8 %collective-permute-start.12 = (bf16[144,2176]{1,0:T(8,128)(2,1)S(1)}, bf16[144,2176]{1,0:T(8,128)(2,1)S(1)}, u32[]{:S(2)}, u32[]{:S(2)}) collective-permute-start(bf16[144,2176]{1,0:T(8,128)(2,1)S(1)} %pad_maximum_fusion.1), channel_id=1, source_target_pairs={{0,8},{8,0},{16,24},{24,16},{1,9},{9,1},{17,25},{25,17},{2,10},{10... | collective-permute-start | bytes 1880072 | tf_op jit(solution)/shard_map/ppermute | solution.py:121
  28.2 1.5 %collective-permute-start.7 = (bf16[48,2176]{1,0:T(8,128)(2,1)S(1)}, bf16[48,2176]{1,0:T(8,128)(2,1)S(1)}, u32[]{:S(2)}, u32[]{:S(2)}) collective-permute-start(bf16[48,2176]{1,0:T(8,128)(2,1)S(1)} %collective-permute-done.2), channel_id=1, source_target_pairs={{0,1},{1,0},{2,3},{3,2},{4,5},{5,4},{6,7},{7,6},{8,9},{9,8},{10,11... | collective-permute-start | bytes 626696 | tf_op jit(solution)/shard_map/ppermute | solution.py:118
  29.8 1.8 %collective-permute-done.10 = bf16[48,2176]{1,0:T(8,128)(2,1)S(1)} collective-permute-done((bf16[48,2176]{1,0:T(8,128)(2,1)S(1)}, bf16[48,2176]{1,0:T(8,128)(2,1)S(1)}, u32[]{:S(2)}, u32[]{:S(2)}) %collective-permute-start.10) | collective-permute-done | bytes 208928 | tf_op jit(solution)/shard_map/ppermute | solution.py:120
  31.6 2.3 %collective-permute-done.8 = bf16[48,2176]{1,0:T(8,128)(2,1)S(1)} collective-permute-done((bf16[48,2176]{1,0:T(8,128)(2,1)S(1)}, bf16[48,2176]{1,0:T(8,128)(2,1)S(1)}, u32[]{:S(2)}, u32[]{:S(2)}) %collective-permute-start.8) | collective-permute-done | bytes 208928 | tf_op jit(solution)/shard_map/ppermute | solution.py:117
  35.2 3.1 %collective-permute-done.7 = bf16[48,2176]{1,0:T(8,128)(2,1)S(1)} collective-permute-done((bf16[48,2176]{1,0:T(8,128)(2,1)S(1)}, bf16[48,2176]{1,0:T(8,128)(2,1)S(1)}, u32[]{:S(2)}, u32[]{:S(2)}) %collective-permute-start.7) | collective-permute-done | bytes 208928 | tf_op jit(solution)/shard_map/ppermute | solution.py:118
  38.4 1.8 %collective-permute-done.12 = bf16[144,2176]{1,0:T(8,128)(2,1)S(1)} collective-permute-done((bf16[144,2176]{1,0:T(8,128)(2,1)S(1)}, bf16[144,2176]{1,0:T(8,128)(2,1)S(1)}, u32[]{:S(2)}, u32[]{:S(2)}) %collective-permute-start.12) | collective-permute-done | bytes 626720 | tf_op jit(solution)/shard_map/ppermute | solution.py:121
  41.3 1.5 %collective-permute-done.14.refs_4_ = bf16[192,2176]{1,0:T(8,128)(2,1)} collective-permute-done((bf16[192,2176]{1,0:T(8,128)(2,1)S(1)}, bf16[192,2176]{1,0:T(8,128)(2,1)}, u32[]{:S(2)}, u32[]{:S(2)}) %collective-permute-start.14) | collective-permute-done | bytes 835616 | tf_op jit(solution)/shard_map/ppermute | solution.py:119
  42.8 11.7 %ffn.2 = (bf16[192,2048]{1,0:T(8,128)(2,1)S(1)}, bf16[192,2048]{1,0:T(8,128)(2,1)S(1)}, bf16[192,2048]{1,0:T(8,128)(2,1)S(1)}, bf16[192,2048]{1,0:T(8,128)(2,1)S...) custom-call(s32[2]{0:T(128)S(1)} %pad_add_fusion.refs_0_.refs_2_, ...), custom_call_target="tpu_custom_call" | custom-call | flops 7247757312 | bytes 25165824 | tf_op jit(solution)/shard_map/ffn/pallas_call | solution.py:86
  55.4 1.4 %collective-permute-done.16 = bf16[192,2048]{1,0:T(8,128)(2,1)S(1)} collective-permute-done((bf16[192,2048]{1,0:T(8,128)(2,1)S(1)}, bf16[192,2048]{1,0:T(8,128)(2,1)S(1)}, u32[]{:S(2)}, u32[]{:S(2)}) %collective-permute-start.16) | collective-permute-done | bytes 786464 | tf_op jit(solution)/shard_map/ppermute | solution.py:119
  58.9 1.6 %collective-permute-start.20 = (bf16[48,2048]{1,0:T(8,128)(2,1)S(1)}, bf16[48,2048]{1,0:T(8,128)(2,1)S(1)}, u32[]{:S(2)}, u32[]{:S(2)}) collective-permute-start(bf16[48,2048]{1,0:T(8,128)(2,1)S(1)} %get-tuple-element.73), channel_id=1, source_target_pairs={{0,4},{4,0},{1,5},{5,1},{2,6},{6,2},{3,7},{7,3},{8,12},{12,8},{9,1... | collective-permute-start | bytes 589832 | tf_op jit(solution)/shard_map/ppermute | solution.py:117
  60.5 1.5 %collective-permute-start.21 = (bf16[48,2048]{1,0:T(8,128)(2,1)S(1)}, bf16[48,2048]{1,0:T(8,128)(2,1)S(1)}, u32[]{:S(2)}, u32[]{:S(2)}) collective-permute-start(bf16[48,2048]{1,0:T(8,128)(2,1)S(1)} %get-tuple-element.72), channel_id=1, source_target_pairs={{0,1},{1,0},{2,3},{3,2},{4,5},{5,4},{6,7},{7,6},{8,9},{9,8},{10,11... | collective-permute-start | bytes 589832 | tf_op jit(solution)/shard_map/ppermute | solution.py:118
  62.5 8.5 %ffn.3 = (bf16[192,2048]{1,0:T(8,128)(2,1)S(1)}, bf16[192,2048]{1,0:T(8,128)(2,1)S(1)}, bf16[192,2048]{1,0:T(8,128)(2,1)S(1)}, bf16[192,2048]{1,0:T(8,128)(2,1)S(1)}) custom-call(bf16[192,2048]{1,0:T(8,128)(2,1)S(1)} %add_convert_fusion.3.refs_0_, bf16[192,2048]{1,0:T(8,128)(2,1)S(1)} %add_convert_fusion.2.refs_1_, s32[2]{0:T(128)S(1)} %pad_add_fusion.refs_0_.refs_2_, ...), custom_call_target="tpu_custom_call" | custom-call | flops 7247757312 | bytes 25165824 | tf_op jit(solution)/shard_map/ffn/pallas_call | solution.py:86
  71.1 1.5 %collective-permute-done.19 = bf16[144,2048]{1,0:T(8,128)(2,1)S(1)} collective-permute-done((bf16[144,2048]{1,0:T(8,128)(2,1)S(1)}, bf16[144,2048]{1,0:T(8,128)(2,1)S(1)}, u32[]{:S(2)}, u32[]{:S(2)}) %collective-permute-start.19) | collective-permute-done | bytes 589856 | tf_op jit(solution)/shard_map/ppermute | solution.py:121
  73.2 5.3 %collective-permute-start.28 = (bf16[48,2048]{1,0:T(8,128)(2,1)S(1)}, bf16[48,2048]{1,0:T(8,128)(2,1)S(1)}, u32[]{:S(2)}, u32[]{:S(2)}) collective-permute-start(bf16[48,2048]{1,0:T(8,128)(2,1)S(1)} %add_convert_fusion.6), channel_id=1, source_target_pairs={{0,24},{8,16},{16,8},{24,0},{1,25},{9,17},{17,9},{25,1},{2,26},{10... | collective-permute-start | bytes 589832 | tf_op jit(solution)/shard_map/ppermute | solution.py:121
  78.9 1.6 %collective-permute-start.30 = (bf16[48,2048]{1,0:T(8,128)(2,1)S(1)}, bf16[48,2048]{1,0:T(8,128)(2,1)S(1)}, u32[]{:S(2)}, u32[]{:S(2)}) collective-permute-start(bf16[48,2048]{1,0:T(8,128)(2,1)S(1)} %get-tuple-element.68), channel_id=1, source_target_pairs={{0,4},{4,0},{1,5},{5,1},{2,6},{6,2},{3,7},{7,3},{8,12},{12,8},{9,1... | collective-permute-start | bytes 589832 | tf_op jit(solution)/shard_map/ppermute | solution.py:117
  80.4 1.5 %collective-permute-start.31 = (bf16[48,2048]{1,0:T(8,128)(2,1)S(1)}, bf16[48,2048]{1,0:T(8,128)(2,1)S(1)}, u32[]{:S(2)}, u32[]{:S(2)}) collective-permute-start(bf16[48,2048]{1,0:T(8,128)(2,1)S(1)} %get-tuple-element.70), channel_id=1, source_target_pairs={{0,1},{1,0},{2,3},{3,2},{4,5},{5,4},{6,7},{7,6},{8,9},{9,8},{10,11... | collective-permute-start | bytes 589832 | tf_op jit(solution)/shard_map/ppermute | solution.py:118
  82.9 3.9 %collective-permute-done.30 = bf16[48,2048]{1,0:T(8,128)(2,1)S(1)} collective-permute-done((bf16[48,2048]{1,0:T(8,128)(2,1)S(1)}, bf16[48,2048]{1,0:T(8,128)(2,1)S(1)}, u32[]{:S(2)}, u32[]{:S(2)}) %collective-permute-start.30) | collective-permute-done | bytes 196640 | tf_op jit(solution)/shard_map/ppermute | solution.py:117
  86.8 1.5 %collective-permute-start.24 = (bf16[48,2048]{1,0:T(8,128)(2,1)S(1)}, bf16[48,2048]{1,0:T(8,128)(2,1)S(1)}, u32[]{:S(2)}, u32[]{:S(2)}) collective-permute-start(bf16[48,2048]{1,0:T(8,128)(2,1)S(1)} %get-tuple-element.65), channel_id=1, source_target_pairs={{0,4},{4,0},{1,5},{5,1},{2,6},{6,2},{3,7},{7,3},{8,12},{12,8},{9,1... | collective-permute-start | bytes 589832 | tf_op jit(solution)/shard_map/ppermute | solution.py:117
  88.3 2.7 %collective-permute-done.31 = bf16[48,2048]{1,0:T(8,128)(2,1)S(1)} collective-permute-done((bf16[48,2048]{1,0:T(8,128)(2,1)S(1)}, bf16[48,2048]{1,0:T(8,128)(2,1)S(1)}, u32[]{:S(2)}, u32[]{:S(2)}) %collective-permute-start.31) | collective-permute-done | bytes 196640 | tf_op jit(solution)/shard_map/ppermute | solution.py:118
  90.9 2.5 %collective-permute-start.25 = (bf16[48,2048]{1,0:T(8,128)(2,1)S(1)}, bf16[48,2048]{1,0:T(8,128)(2,1)S(1)}, u32[]{:S(2)}, u32[]{:S(2)}) collective-permute-start(bf16[48,2048]{1,0:T(8,128)(2,1)S(1)} %get-tuple-element.67), channel_id=1, source_target_pairs={{0,1},{1,0},{2,3},{3,2},{4,5},{5,4},{6,7},{7,6},{8,9},{9,8},{10,11... | collective-permute-start | bytes 589832 | tf_op jit(solution)/shard_map/ppermute | solution.py:118
  95.2 5.4 %collective-permute-done.25 = bf16[48,2048]{1,0:T(8,128)(2,1)S(1)} collective-permute-done((bf16[48,2048]{1,0:T(8,128)(2,1)S(1)}, bf16[48,2048]{1,0:T(8,128)(2,1)S(1)}, u32[]{:S(2)}, u32[]{:S(2)}) %collective-permute-start.25) | collective-permute-done | bytes 196640 | tf_op jit(solution)/shard_map/ppermute | solution.py:118
  100.6 2.2 %collective-permute-done.33 = bf16[48,2048]{1,0:T(8,128)(2,1)S(1)} collective-permute-done((bf16[48,2048]{1,0:T(8,128)(2,1)S(1)}, bf16[48,2048]{1,0:T(8,128)(2,1)S(1)}, u32[]{:S(2)}, u32[]{:S(2)}) %collective-permute-start.33) | collective-permute-done | bytes 196640 | tf_op jit(solution)/shard_map/ppermute | solution.py:121
  (82 shorter events, 14.7 us)
Async XLA Ops:
  2.0 11.1 %collective-permute-start = (bf16[48,2176]{1,0:T(8,128)(2,1)S(1)}, bf16[48,2176]{1,0:T(8,128)(2,1)S(1)}, u32[]{:S(2)}, u32[]{:S(2)}) collective-permute-start(bf16[48,2176]{1,0:T(8,128)(2,1)S(1)} %concatenate.24), channel_id=1, source_target_pairs={{0,24},{8,16},{16,8},{24,0},{1,25},{9,17},{17,9},{25,1},{2,26},{10... | collective-permute-start | bytes 626696 | tf_op jit(solution)/shard_map/ppermute | solution.py:121
  7.1 11.5 %collective-permute-start.4 = (bf16[48,2176]{1,0:T(8,128)(2,1)S(1)}, bf16[48,2176]{1,0:T(8,128)(2,1)S(1)}, u32[]{:S(2)}, u32[]{:S(2)}) collective-permute-start(bf16[48,2176]{1,0:T(8,128)(2,1)S(1)} %concatenate.24), channel_id=1, source_target_pairs={{0,4},{4,0},{1,5},{5,1},{2,6},{6,2},{3,7},{7,3},{8,12},{12,8},{9,1... | collective-permute-start | bytes 626696 | tf_op jit(solution)/shard_map/ppermute | solution.py:117
  8.6 11.6 %collective-permute-start.5 = (bf16[48,2176]{1,0:T(8,128)(2,1)S(1)}, bf16[48,2176]{1,0:T(8,128)(2,1)S(1)}, u32[]{:S(2)}, u32[]{:S(2)}) collective-permute-start(bf16[48,2176]{1,0:T(8,128)(2,1)S(1)} %concatenate.24), channel_id=1, source_target_pairs={{0,1},{1,0},{2,3},{3,2},{4,5},{5,4},{6,7},{7,6},{8,9},{9,8},{10,11... | collective-permute-start | bytes 626696 | tf_op jit(solution)/shard_map/ppermute | solution.py:118
  10.1 10.6 %collective-permute-start.6 = (bf16[48,2176]{1,0:T(8,128)(2,1)S(1)}, bf16[48,2176]{1,0:T(8,128)(2,1)S(1)}, u32[]{:S(2)}, u32[]{:S(2)}) collective-permute-start(bf16[48,2176]{1,0:T(8,128)(2,1)S(1)} %concatenate.24), channel_id=1, source_target_pairs={{0,5},{1,4},{4,1},{5,0},{2,7},{3,6},{6,3},{7,2},{8,13},{9,12},{12,... | collective-permute-start | bytes 626696 | tf_op jit(solution)/shard_map/ppermute | solution.py:120
  10.6 6.4 %collective-permute-start.11 = (bf16[48,2176]{1,0:T(8,128)(2,1)S(1)}, bf16[48,2176]{1,0:T(8,128)(2,1)S(1)}, u32[]{:S(2)}, u32[]{:S(2)}) collective-permute-start(bf16[48,2176]{1,0:T(8,128)(2,1)S(1)} %concatenate.24), channel_id=1, source_target_pairs={{0,8},{8,0},{16,24},{24,16},{1,9},{9,1},{17,25},{25,17},{2,10},{10... | collective-permute-start | bytes 626696 | tf_op jit(solution)/shard_map/ppermute | solution.py:121
  13.1 9.6 %collective-permute-start.2 = (bf16[48,2176]{1,0:T(8,128)(2,1)S(1)}, bf16[48,2176]{1,0:T(8,128)(2,1)S(1)}, u32[]{:S(2)}, u32[]{:S(2)}) collective-permute-start(bf16[48,2176]{1,0:T(8,128)(2,1)S(1)} %collective-permute-done), channel_id=1, source_target_pairs={{0,4},{4,0},{1,5},{5,1},{2,6},{6,2},{3,7},{7,3},{8,12},{12,8},{9,1... | collective-permute-start | bytes 626696 | tf_op jit(solution)/shard_map/ppermute | solution.py:117
  17.0 5.9 %collective-permute-start.3 = (bf16[48,2176]{1,0:T(8,128)(2,1)S(1)}, bf16[48,2176]{1,0:T(8,128)(2,1)S(1)}, u32[]{:S(2)}, u32[]{:S(2)}) collective-permute-start(bf16[48,2176]{1,0:T(8,128)(2,1)S(1)} %collective-permute-done), channel_id=1, source_target_pairs={{0,8},{8,0},{16,24},{24,16},{1,9},{9,1},{17,25},{25,17},{2,10},{10... | collective-permute-start | bytes 626696 | tf_op jit(solution)/shard_map/ppermute | solution.py:121
  18.5 9.7 %collective-permute-start.1 = (bf16[48,2176]{1,0:T(8,128)(2,1)S(1)}, bf16[48,2176]{1,0:T(8,128)(2,1)S(1)}, u32[]{:S(2)}, u32[]{:S(2)}) collective-permute-start(bf16[48,2176]{1,0:T(8,128)(2,1)S(1)} %collective-permute-done), channel_id=1, source_target_pairs={{0,1},{1,0},{2,3},{3,2},{4,5},{5,4},{6,7},{7,6},{8,9},{9,8},{10,11... | collective-permute-start | bytes 626696 | tf_op jit(solution)/shard_map/ppermute | solution.py:118
  22.8 8.7 %collective-permute-start.10 = (bf16[48,2176]{1,0:T(8,128)(2,1)S(1)}, bf16[48,2176]{1,0:T(8,128)(2,1)S(1)}, u32[]{:S(2)}, u32[]{:S(2)}) collective-permute-start(bf16[48,2176]{1,0:T(8,128)(2,1)S(1)} %collective-permute-done.3), channel_id=1, source_target_pairs={{0,5},{1,4},{4,1},{5,0},{2,7},{3,6},{6,3},{7,2},{8,13},{9,12},{12,... | collective-permute-start | bytes 626696 | tf_op jit(solution)/shard_map/ppermute | solution.py:120
  25.3 8.6 %collective-permute-start.8 = (bf16[48,2176]{1,0:T(8,128)(2,1)S(1)}, bf16[48,2176]{1,0:T(8,128)(2,1)S(1)}, u32[]{:S(2)}, u32[]{:S(2)}) collective-permute-start(bf16[48,2176]{1,0:T(8,128)(2,1)S(1)} %collective-permute-done.3), channel_id=1, source_target_pairs={{0,4},{4,0},{1,5},{5,1},{2,6},{6,2},{3,7},{7,3},{8,12},{12,8},{9,1... | collective-permute-start | bytes 626696 | tf_op jit(solution)/shard_map/ppermute | solution.py:117
  25.9 9.3 %collective-permute-start.9 = (bf16[48,2176]{1,0:T(8,128)(2,1)S(1)}, bf16[48,2176]{1,0:T(8,128)(2,1)S(1)}, u32[]{:S(2)}, u32[]{:S(2)}) collective-permute-start(bf16[48,2176]{1,0:T(8,128)(2,1)S(1)} %collective-permute-done.3), channel_id=1, source_target_pairs={{0,1},{1,0},{2,3},{3,2},{4,5},{5,4},{6,7},{7,6},{8,9},{9,8},{10,11... | collective-permute-start | bytes 626696 | tf_op jit(solution)/shard_map/ppermute | solution.py:118
  26.4 13.7 %collective-permute-start.12 = (bf16[144,2176]{1,0:T(8,128)(2,1)S(1)}, bf16[144,2176]{1,0:T(8,128)(2,1)S(1)}, u32[]{:S(2)}, u32[]{:S(2)}) collective-permute-start(bf16[144,2176]{1,0:T(8,128)(2,1)S(1)} %pad_maximum_fusion.1), channel_id=1, source_target_pairs={{0,8},{8,0},{16,24},{24,16},{1,9},{9,1},{17,25},{25,17},{2,10},{10... | collective-permute-start | bytes 1880072 | tf_op jit(solution)/shard_map/ppermute | solution.py:121
  28.2 10.1 %collective-permute-start.7 = (bf16[48,2176]{1,0:T(8,128)(2,1)S(1)}, bf16[48,2176]{1,0:T(8,128)(2,1)S(1)}, u32[]{:S(2)}, u32[]{:S(2)}) collective-permute-start(bf16[48,2176]{1,0:T(8,128)(2,1)S(1)} %collective-permute-done.2), channel_id=1, source_target_pairs={{0,1},{1,0},{2,3},{3,2},{4,5},{5,4},{6,7},{7,6},{8,9},{9,8},{10,11... | collective-permute-start | bytes 626696 | tf_op jit(solution)/shard_map/ppermute | solution.py:118
  38.3 2.9 %collective-permute-start.13 = (bf16[192,2176]{1,0:T(8,128)(2,1)S(1)}, bf16[192,2176]{1,0:T(8,128)(2,1)S(1)}, u32[]{:S(2)}, u32[]{:S(2)}) collective-permute-start(bf16[192,2176]{1,0:T(8,128)(2,1)S(1)} %constant_dynamic-update-slice_fusion.refs_1_), channel_id=1, source_target_pairs={{0,2},{2,0},{1,3},{3,1},{4,6},{6,4},{5,7},{7,5},{8,10},{10,8},{9,1... | collective-permute-start | bytes 2506760 | tf_op jit(solution)/shard_map/ppermute | solution.py:119
  40.5 21.5 %collective-permute-start.18 = (bf16[192,2176]{1,0:T(8,128)(2,1)S(1)}, bf16[192,2176]{1,0:T(8,128)(2,1)S(1)}, u32[]{:S(2)}, u32[]{:S(2)}) collective-permute-start(bf16[192,2176]{1,0:T(8,128)(2,1)S(1)} %pad_maximum_fusion.refs_4_), channel_id=1, source_target_pairs={{0,2},{2,0},{1,3},{3,1},{4,6},{6,4},{5,7},{7,5},{8,10},{10,8},{9,1... | collective-permute-start | bytes 2506760 | tf_op jit(solution)/shard_map/ppermute | solution.py:119
  54.8 3.8 %collective-permute-start.15 = (bf16[192,2048]{1,0:T(8,128)(2,1)S(1)}, bf16[192,2048]{1,0:T(8,128)(2,1)S(1)}, u32[]{:S(2)}, u32[]{:S(2)}) collective-permute-start(bf16[192,2048]{1,0:T(8,128)(2,1)S(1)} %get-tuple-element.42), channel_id=1, source_target_pairs={{0,2},{2,0},{1,3},{3,1},{4,6},{6,4},{5,7},{7,5},{8,10},{10,8},{9,1... | collective-permute-start | bytes 2359304 | tf_op jit(solution)/shard_map/ppermute | solution.py:119
  55.2 7.3 %collective-permute-start.17 = (bf16[192,2176]{1,0:T(8,128)(2,1)S(1)}, bf16[192,2176]{1,0:T(8,128)(2,1)S(1)}, u32[]{:S(2)}, u32[]{:S(2)}) collective-permute-start(bf16[192,2176]{1,0:T(8,128)(2,1)S(1)} %constant_dynamic-update-slice_fusion.6.refs_3_), channel_id=1, source_target_pairs={{0,2},{2,0},{1,3},{3,1},{4,6},{6,4},{5,7},{7,5},{8,10},{10,8},{9,1... | collective-permute-start | bytes 2506760 | tf_op jit(solution)/shard_map/ppermute | solution.py:119
  57.2 15.4 %collective-permute-start.19 = (bf16[144,2048]{1,0:T(8,128)(2,1)S(1)}, bf16[144,2048]{1,0:T(8,128)(2,1)S(1)}, u32[]{:S(2)}, u32[]{:S(2)}) collective-permute-start(bf16[144,2048]{1,0:T(8,128)(2,1)S(1)} %slice.21), channel_id=1, source_target_pairs={{0,8},{8,0},{16,24},{24,16},{1,9},{9,1},{17,25},{25,17},{2,10},{10... | collective-permute-start | bytes 1769480 | tf_op jit(solution)/shard_map/ppermute | solution.py:121
  58.9 12.1 %collective-permute-start.20 = (bf16[48,2048]{1,0:T(8,128)(2,1)S(1)}, bf16[48,2048]{1,0:T(8,128)(2,1)S(1)}, u32[]{:S(2)}, u32[]{:S(2)}) collective-permute-start(bf16[48,2048]{1,0:T(8,128)(2,1)S(1)} %get-tuple-element.73), channel_id=1, source_target_pairs={{0,4},{4,0},{1,5},{5,1},{2,6},{6,2},{3,7},{7,3},{8,12},{12,8},{9,1... | collective-permute-start | bytes 589832 | tf_op jit(solution)/shard_map/ppermute | solution.py:117
  60.5 10.6 %collective-permute-start.21 = (bf16[48,2048]{1,0:T(8,128)(2,1)S(1)}, bf16[48,2048]{1,0:T(8,128)(2,1)S(1)}, u32[]{:S(2)}, u32[]{:S(2)}) collective-permute-start(bf16[48,2048]{1,0:T(8,128)(2,1)S(1)} %get-tuple-element.72), channel_id=1, source_target_pairs={{0,1},{1,0},{2,3},{3,2},{4,5},{5,4},{6,7},{7,6},{8,9},{9,8},{10,11... | collective-permute-start | bytes 589832 | tf_op jit(solution)/shard_map/ppermute | solution.py:118
  62.0 9.1 %collective-permute-start.22 = (bf16[48,2048]{1,0:T(8,128)(2,1)S(1)}, bf16[48,2048]{1,0:T(8,128)(2,1)S(1)}, u32[]{:S(2)}, u32[]{:S(2)}) collective-permute-start(bf16[48,2048]{1,0:T(8,128)(2,1)S(1)} %get-tuple-element.71), channel_id=1, source_target_pairs={{0,5},{1,4},{4,1},{5,0},{2,7},{3,6},{6,3},{7,2},{8,13},{9,12},{12,... | collective-permute-start | bytes 589832 | tf_op jit(solution)/shard_map/ppermute | solution.py:120
  72.6 6.0 %collective-permute-start.29 = (bf16[192,2048]{1,0:T(8,128)(2,1)S(1)}, bf16[192,2048]{1,0:T(8,128)(2,1)S(1)}, u32[]{:S(2)}, u32[]{:S(2)}) collective-permute-start(bf16[192,2048]{1,0:T(8,128)(2,1)S(1)} %get-tuple-element.64), channel_id=1, source_target_pairs={{0,2},{2,0},{1,3},{3,1},{4,6},{6,4},{5,7},{7,5},{8,10},{10,8},{9,1... | collective-permute-start | bytes 2359304 | tf_op jit(solution)/shard_map/ppermute | solution.py:119
  72.6 9.4 %collective-permute-start.23 = (bf16[192,2048]{1,0:T(8,128)(2,1)S(1)}, bf16[192,2048]{1,0:T(8,128)(2,1)S(1)}, u32[]{:S(2)}, u32[]{:S(2)}) collective-permute-start(bf16[192,2048]{1,0:T(8,128)(2,1)S(1)} %get-tuple-element.56), channel_id=1, source_target_pairs={{0,2},{2,0},{1,3},{3,1},{4,6},{6,4},{5,7},{7,5},{8,10},{10,8},{9,1... | collective-permute-start | bytes 2359304 | tf_op jit(solution)/shard_map/ppermute | solution.py:119
  73.2 20.3 %collective-permute-start.28 = (bf16[48,2048]{1,0:T(8,128)(2,1)S(1)}, bf16[48,2048]{1,0:T(8,128)(2,1)S(1)}, u32[]{:S(2)}, u32[]{:S(2)}) collective-permute-start(bf16[48,2048]{1,0:T(8,128)(2,1)S(1)} %add_convert_fusion.6), channel_id=1, source_target_pairs={{0,24},{8,16},{16,8},{24,0},{1,25},{9,17},{17,9},{25,1},{2,26},{10... | collective-permute-start | bytes 589832 | tf_op jit(solution)/shard_map/ppermute | solution.py:121
  78.6 15.7 %collective-permute-start.27 = (bf16[48,2048]{1,0:T(8,128)(2,1)S(1)}, bf16[48,2048]{1,0:T(8,128)(2,1)S(1)}, u32[]{:S(2)}, u32[]{:S(2)}) collective-permute-start(bf16[48,2048]{1,0:T(8,128)(2,1)S(1)} %slice.20), channel_id=1, source_target_pairs={{0,8},{8,0},{16,24},{24,16},{1,9},{9,1},{17,25},{25,17},{2,10},{10... | collective-permute-start | bytes 589832 | tf_op jit(solution)/shard_map/ppermute | solution.py:121
  78.9 7.9 %collective-permute-start.30 = (bf16[48,2048]{1,0:T(8,128)(2,1)S(1)}, bf16[48,2048]{1,0:T(8,128)(2,1)S(1)}, u32[]{:S(2)}, u32[]{:S(2)}) collective-permute-start(bf16[48,2048]{1,0:T(8,128)(2,1)S(1)} %get-tuple-element.68), channel_id=1, source_target_pairs={{0,4},{4,0},{1,5},{5,1},{2,6},{6,2},{3,7},{7,3},{8,12},{12,8},{9,1... | collective-permute-start | bytes 589832 | tf_op jit(solution)/shard_map/ppermute | solution.py:117
  80.4 10.5 %collective-permute-start.31 = (bf16[48,2048]{1,0:T(8,128)(2,1)S(1)}, bf16[48,2048]{1,0:T(8,128)(2,1)S(1)}, u32[]{:S(2)}, u32[]{:S(2)}) collective-permute-start(bf16[48,2048]{1,0:T(8,128)(2,1)S(1)} %get-tuple-element.70), channel_id=1, source_target_pairs={{0,1},{1,0},{2,3},{3,2},{4,5},{5,4},{6,7},{7,6},{8,9},{9,8},{10,11... | collective-permute-start | bytes 589832 | tf_op jit(solution)/shard_map/ppermute | solution.py:118
  82.0 11.4 %collective-permute-start.32 = (bf16[48,2048]{1,0:T(8,128)(2,1)S(1)}, bf16[48,2048]{1,0:T(8,128)(2,1)S(1)}, u32[]{:S(2)}, u32[]{:S(2)}) collective-permute-start(bf16[48,2048]{1,0:T(8,128)(2,1)S(1)} %get-tuple-element.69), channel_id=1, source_target_pairs={{0,5},{1,4},{4,1},{5,0},{2,7},{3,6},{6,3},{7,2},{8,13},{9,12},{12,... | collective-permute-start | bytes 589832 | tf_op jit(solution)/shard_map/ppermute | solution.py:120
  86.8 8.5 %collective-permute-start.24 = (bf16[48,2048]{1,0:T(8,128)(2,1)S(1)}, bf16[48,2048]{1,0:T(8,128)(2,1)S(1)}, u32[]{:S(2)}, u32[]{:S(2)}) collective-permute-start(bf16[48,2048]{1,0:T(8,128)(2,1)S(1)} %get-tuple-element.65), channel_id=1, source_target_pairs={{0,4},{4,0},{1,5},{5,1},{2,6},{6,2},{3,7},{7,3},{8,12},{12,8},{9,1... | collective-permute-start | bytes 589832 | tf_op jit(solution)/shard_map/ppermute | solution.py:117
  90.9 9.7 %collective-permute-start.25 = (bf16[48,2048]{1,0:T(8,128)(2,1)S(1)}, bf16[48,2048]{1,0:T(8,128)(2,1)S(1)}, u32[]{:S(2)}, u32[]{:S(2)}) collective-permute-start(bf16[48,2048]{1,0:T(8,128)(2,1)S(1)} %get-tuple-element.67), channel_id=1, source_target_pairs={{0,1},{1,0},{2,3},{3,2},{4,5},{5,4},{6,7},{7,6},{8,9},{9,8},{10,11... | collective-permute-start | bytes 589832 | tf_op jit(solution)/shard_map/ppermute | solution.py:118
  93.4 7.2 %collective-permute-start.26 = (bf16[48,2048]{1,0:T(8,128)(2,1)S(1)}, bf16[48,2048]{1,0:T(8,128)(2,1)S(1)}, u32[]{:S(2)}, u32[]{:S(2)}) collective-permute-start(bf16[48,2048]{1,0:T(8,128)(2,1)S(1)} %get-tuple-element.66), channel_id=1, source_target_pairs={{0,5},{1,4},{4,1},{5,0},{2,7},{3,6},{6,3},{7,2},{8,13},{9,12},{12,... | collective-permute-start | bytes 589832 | tf_op jit(solution)/shard_map/ppermute | solution.py:120
  93.5 9.2 %collective-permute-start.33 = (bf16[48,2048]{1,0:T(8,128)(2,1)S(1)}, bf16[48,2048]{1,0:T(8,128)(2,1)S(1)}, u32[]{:S(2)}, u32[]{:S(2)}) collective-permute-start(bf16[48,2048]{1,0:T(8,128)(2,1)S(1)} %add_convert_fusion.5), channel_id=1, source_target_pairs={{0,16},{8,24},{16,0},{24,8},{1,17},{9,25},{17,1},{25,9},{2,18},{10... | collective-permute-start | bytes 589832 | tf_op jit(solution)/shard_map/ppermute | solution.py:121
  (8 other events, 52.7 us)

commit v6 on v5

--- a/solution.py
+++ b/solution.py
@@ -130,7 +130,8 @@
     t2, x3, y3 = pz(t3, 1), px(t3), py(t3)
     x3, t2, x0, y0, d0 = lax.optimization_barrier((x3, t2, x0, y0, d0))
     rest0 = jnp.concatenate([y0, x0, d0])
-    d3, x2, y2, d2 = lax.optimization_barrier((py(x3), px(t2), py(t2), pd(t2)))
+    y2 = py(t2)
+    d3, x2, y2, d2 = lax.optimization_barrier((py(x3), px(t2), y2, px(y2)))
     p0, p1, p2, p3 = (
         jnp.concatenate(blocks)
         for blocks in ([t0, rest0], [t1, pz(rest0, 1)], [t2, y2, x2, d2], [t3, y3, x3, d3])

time: 104 us -> 104 us (level)
    ppermute x7, starting transfers between devices: 10.6 us -> 7.69 us  [on_device(): py = lambda a: lax.ppermute(a, 'y', swap)]
    ppermute x7, waiting for transfers between devices: 12.5 us -> 9.56 us  [on_device(): py = lambda a: lax.ppermute(a, 'y', swap)]
    ppermute x5 -> x4, starting transfers between devices: 3.9 us -> 6.78 us  [on_device(): pd = lambda a: lax.ppermute(a, ('x', 'y'), [(i, 3 - i) for i in range(4)])]
    ppermute x8, waiting for transfers between devices: 10.3 us -> 12.5 us  [on_device(): pz = lambda a, k: lax.ppermute(a, 'z', [(i, i ^ k) for i in range(nz)])]
    ppermute x6 -> x7, waiting for transfers between devices: 9.21 us -> 9.94 us  [on_device(): px = lambda a: lax.ppermute(a, 'x', swap)]
    ppermute x6 -> x7, starting transfers between devices: 8.33 us -> 7.98 us  [on_device(): px = lambda a: lax.ppermute(a, 'x', swap)]
    ppermute x5 -> x4, waiting for transfers between devices: 2.33 us -> 2.26 us  [on_device(): pd = lambda a: lax.ppermute(a, ('x', 'y'), [(i, 3 - i) for i in range(4)])]
where the time goes in v6:
time: 104 us; the launch traced here: 103 us
  starting transfers between devices  40 us (38%)
  waiting for transfers between devices  37.4 us (36%)
  Pallas kernels  20.3 us (20%)
  other arithmetic  3.16 us (3%)
  local copies, waits for them, and re-layouts  2.37 us (2%)
    pallas_call x2, Pallas kernels, ffn(): pl.pallas_call(functools.partial(ffn_kernel, layout, cols, fresh, len(fir...  20.3 us
    ppermute x8, starting transfers between devices, on_device(): pz = lambda a, k: lax.ppermute(a, 'z', [(i, i ^ k) for i in range(nz)])  15.5 us
    ppermute x8, waiting for transfers between devices, on_device(): pz = lambda a, k: lax.ppermute(a, 'z', [(i, i ^ k) for i in range(nz)])  12.5 us
    ppermute x7, waiting for transfers between devices, on_device(): px = lambda a: lax.ppermute(a, 'x', swap)  9.94 us
    ppermute x7, waiting for transfers between devices, on_device(): py = lambda a: lax.ppermute(a, 'y', swap)  9.56 us
    ppermute x7, starting transfers between devices, on_device(): px = lambda a: lax.ppermute(a, 'x', swap)  7.98 us
    ppermute x7, starting transfers between devices, on_device(): py = lambda a: lax.ppermute(a, 'y', swap)  7.69 us
    ppermute x4, starting transfers between devices, on_device(): pd = lambda a: lax.ppermute(a, ('x', 'y'), [(i, 3 - i) for i in range(4)])  6.78 us
  transfers between devices with their start and end apart: 34, of which 18 were waited for; matrix products, arithmetic and copies ran while one was open for 2% of the time, Pallas kernels for 20%

profile of v6, /device:TPU:0, one launch (start us, length us, event | category | flops | bytes accessed | tf_op | source)
XLA Modules:
  0.0 103.4 jit_solution(6123358276755708475)
XLA Ops:
  2.0 5.1 %collective-permute-start = (bf16[48,2176]{1,0:T(8,128)(2,1)S(1)}, bf16[48,2176]{1,0:T(8,128)(2,1)S(1)}, u32[]{:S(2)}, u32[]{:S(2)}) collective-permute-start(bf16[48,2176]{1,0:T(8,128)(2,1)S(1)} %concatenate.24), channel_id=1, source_target_pairs={{0,24},{8,16},{16,8},{24,0},{1,25},{9,17},{17,9},{25,1},{2,26},{10... | collective-permute-start | bytes 626696 | tf_op jit(solution)/shard_map/ppermute | solution.py:121
  7.1 1.5 %collective-permute-start.4 = (bf16[48,2176]{1,0:T(8,128)(2,1)S(1)}, bf16[48,2176]{1,0:T(8,128)(2,1)S(1)}, u32[]{:S(2)}, u32[]{:S(2)}) collective-permute-start(bf16[48,2176]{1,0:T(8,128)(2,1)S(1)} %concatenate.24), channel_id=1, source_target_pairs={{0,4},{4,0},{1,5},{5,1},{2,6},{6,2},{3,7},{7,3},{8,12},{12,8},{9,1... | collective-permute-start | bytes 626696 | tf_op jit(solution)/shard_map/ppermute | solution.py:117
  8.6 1.5 %collective-permute-start.5 = (bf16[48,2176]{1,0:T(8,128)(2,1)S(1)}, bf16[48,2176]{1,0:T(8,128)(2,1)S(1)}, u32[]{:S(2)}, u32[]{:S(2)}) collective-permute-start(bf16[48,2176]{1,0:T(8,128)(2,1)S(1)} %concatenate.24), channel_id=1, source_target_pairs={{0,1},{1,0},{2,3},{3,2},{4,5},{5,4},{6,7},{7,6},{8,9},{9,8},{10,11... | collective-permute-start | bytes 626696 | tf_op jit(solution)/shard_map/ppermute | solution.py:118
  10.6 2.5 %collective-permute-done = bf16[48,2176]{1,0:T(8,128)(2,1)S(1)} collective-permute-done((bf16[48,2176]{1,0:T(8,128)(2,1)S(1)}, bf16[48,2176]{1,0:T(8,128)(2,1)S(1)}, u32[]{:S(2)}, u32[]{:S(2)}) %collective-permute-start) | collective-permute-done | bytes 208928 | tf_op jit(solution)/shard_map/ppermute | solution.py:121
  13.1 1.7 %collective-permute-start.2 = (bf16[48,2176]{1,0:T(8,128)(2,1)S(1)}, bf16[48,2176]{1,0:T(8,128)(2,1)S(1)}, u32[]{:S(2)}, u32[]{:S(2)}) collective-permute-start(bf16[48,2176]{1,0:T(8,128)(2,1)S(1)} %collective-permute-done), channel_id=1, source_target_pairs={{0,4},{4,0},{1,5},{5,1},{2,6},{6,2},{3,7},{7,3},{8,12},{12,8},{9,1... | collective-permute-start | bytes 626696 | tf_op jit(solution)/shard_map/ppermute | solution.py:117
  14.8 2.1 %collective-permute-done.11 = bf16[48,2176]{1,0:T(8,128)(2,1)S(1)} collective-permute-done((bf16[48,2176]{1,0:T(8,128)(2,1)S(1)}, bf16[48,2176]{1,0:T(8,128)(2,1)S(1)}, u32[]{:S(2)}, u32[]{:S(2)}) %collective-permute-start.11) | collective-permute-done | bytes 208928 | tf_op jit(solution)/shard_map/ppermute | solution.py:121
  17.0 1.5 %collective-permute-start.3 = (bf16[48,2176]{1,0:T(8,128)(2,1)S(1)}, bf16[48,2176]{1,0:T(8,128)(2,1)S(1)}, u32[]{:S(2)}, u32[]{:S(2)}) collective-permute-start(bf16[48,2176]{1,0:T(8,128)(2,1)S(1)} %collective-permute-done), channel_id=1, source_target_pairs={{0,8},{8,0},{16,24},{24,16},{1,9},{9,1},{17,25},{25,17},{2,10},{10... | collective-permute-start | bytes 626696 | tf_op jit(solution)/shard_map/ppermute | solution.py:121
  18.5 1.6 %collective-permute-start.1 = (bf16[48,2176]{1,0:T(8,128)(2,1)S(1)}, bf16[48,2176]{1,0:T(8,128)(2,1)S(1)}, u32[]{:S(2)}, u32[]{:S(2)}) collective-permute-start(bf16[48,2176]{1,0:T(8,128)(2,1)S(1)} %collective-permute-done), channel_id=1, source_target_pairs={{0,1},{1,0},{2,3},{3,2},{4,5},{5,4},{6,7},{7,6},{8,9},{9,8},{10,11... | collective-permute-start | bytes 626696 | tf_op jit(solution)/shard_map/ppermute | solution.py:118
  20.6 2.1 %collective-permute-done.2 = bf16[48,2176]{1,0:T(8,128)(2,1)S(1)} collective-permute-done((bf16[48,2176]{1,0:T(8,128)(2,1)S(1)}, bf16[48,2176]{1,0:T(8,128)(2,1)S(1)}, u32[]{:S(2)}, u32[]{:S(2)}) %collective-permute-start.2) | collective-permute-done | bytes 208928 | tf_op jit(solution)/shard_map/ppermute | solution.py:117
  22.8 1.5 %collective-permute-start.9 = (bf16[48,2176]{1,0:T(8,128)(2,1)S(1)}, bf16[48,2176]{1,0:T(8,128)(2,1)S(1)}, u32[]{:S(2)}, u32[]{:S(2)}) collective-permute-start(bf16[48,2176]{1,0:T(8,128)(2,1)S(1)} %collective-permute-done.3), channel_id=1, source_target_pairs={{0,1},{1,0},{2,3},{3,2},{4,5},{5,4},{6,7},{7,6},{8,9},{9,8},{10,11... | collective-permute-start | bytes 626696 | tf_op jit(solution)/shard_map/ppermute | solution.py:118
  24.4 1.5 %collective-permute-start.8 = (bf16[48,2176]{1,0:T(8,128)(2,1)S(1)}, bf16[48,2176]{1,0:T(8,128)(2,1)S(1)}, u32[]{:S(2)}, u32[]{:S(2)}) collective-permute-start(bf16[48,2176]{1,0:T(8,128)(2,1)S(1)} %collective-permute-done.3), channel_id=1, source_target_pairs={{0,4},{4,0},{1,5},{5,1},{2,6},{6,2},{3,7},{7,3},{8,12},{12,8},{9,1... | collective-permute-start | bytes 626696 | tf_op jit(solution)/shard_map/ppermute | solution.py:117
  25.9 1.8 %collective-permute-start.12 = (bf16[144,2176]{1,0:T(8,128)(2,1)S(1)}, bf16[144,2176]{1,0:T(8,128)(2,1)S(1)}, u32[]{:S(2)}, u32[]{:S(2)}) collective-permute-start(bf16[144,2176]{1,0:T(8,128)(2,1)S(1)} %pad_maximum_fusion.1), channel_id=1, source_target_pairs={{0,8},{8,0},{16,24},{24,16},{1,9},{9,1},{17,25},{25,17},{2,10},{10... | collective-permute-start | bytes 1880072 | tf_op jit(solution)/shard_map/ppermute | solution.py:121
  28.2 2.6 %collective-permute-done.9 = bf16[48,2176]{1,0:T(8,128)(2,1)S(1)} collective-permute-done((bf16[48,2176]{1,0:T(8,128)(2,1)S(1)}, bf16[48,2176]{1,0:T(8,128)(2,1)S(1)}, u32[]{:S(2)}, u32[]{:S(2)}) %collective-permute-start.9) | collective-permute-done | bytes 208928 | tf_op jit(solution)/shard_map/ppermute | solution.py:118
  30.9 1.6 %collective-permute-start.10 = (bf16[48,2176]{1,0:T(8,128)(2,1)S(1)}, bf16[48,2176]{1,0:T(8,128)(2,1)S(1)}, u32[]{:S(2)}, u32[]{:S(2)}) collective-permute-start(bf16[48,2176]{1,0:T(8,128)(2,1)S(1)} %collective-permute-done.9), channel_id=1, source_target_pairs={{0,4},{4,0},{1,5},{5,1},{2,6},{6,2},{3,7},{7,3},{8,12},{12,8},{9,1... | collective-permute-start | bytes 626696 | tf_op jit(solution)/shard_map/ppermute | solution.py:117
  32.5 1.2 %collective-permute-done.7 = bf16[48,2176]{1,0:T(8,128)(2,1)S(1)} collective-permute-done((bf16[48,2176]{1,0:T(8,128)(2,1)S(1)}, bf16[48,2176]{1,0:T(8,128)(2,1)S(1)}, u32[]{:S(2)}, u32[]{:S(2)}) %collective-permute-start.7) | collective-permute-done | bytes 208928 | tf_op jit(solution)/shard_map/ppermute | solution.py:118
  33.7 3.0 %collective-permute-done.10 = bf16[48,2176]{1,0:T(8,128)(2,1)S(1)} collective-permute-done((bf16[48,2176]{1,0:T(8,128)(2,1)S(1)}, bf16[48,2176]{1,0:T(8,128)(2,1)S(1)}, u32[]{:S(2)}, u32[]{:S(2)}) %collective-permute-start.10) | collective-permute-done | bytes 208928 | tf_op jit(solution)/shard_map/ppermute | solution.py:117
  37.5 2.4 %collective-permute-done.12 = bf16[144,2176]{1,0:T(8,128)(2,1)S(1)} collective-permute-done((bf16[144,2176]{1,0:T(8,128)(2,1)S(1)}, bf16[144,2176]{1,0:T(8,128)(2,1)S(1)}, u32[]{:S(2)}, u32[]{:S(2)}) %collective-permute-start.12) | collective-permute-done | bytes 626720 | tf_op jit(solution)/shard_map/ppermute | solution.py:121
  40.8 1.7 %collective-permute-done.14.refs_4_ = bf16[192,2176]{1,0:T(8,128)(2,1)} collective-permute-done((bf16[192,2176]{1,0:T(8,128)(2,1)S(1)}, bf16[192,2176]{1,0:T(8,128)(2,1)}, u32[]{:S(2)}, u32[]{:S(2)}) %collective-permute-start.14) | collective-permute-done | bytes 835616 | tf_op jit(solution)/shard_map/ppermute | solution.py:119
  42.5 11.7 %ffn.2 = (bf16[192,2048]{1,0:T(8,128)(2,1)S(1)}, bf16[192,2048]{1,0:T(8,128)(2,1)S(1)}, bf16[192,2048]{1,0:T(8,128)(2,1)S(1)}, bf16[192,2048]{1,0:T(8,128)(2,1)S...) custom-call(s32[2]{0:T(128)S(1)} %pad_add_fusion.refs_0_.refs_2_, ...), custom_call_target="tpu_custom_call" | custom-call | flops 7247757312 | bytes 25165824 | tf_op jit(solution)/shard_map/ffn/pallas_call | solution.py:86
  55.2 1.4 %collective-permute-done.16 = bf16[192,2048]{1,0:T(8,128)(2,1)S(1)} collective-permute-done((bf16[192,2048]{1,0:T(8,128)(2,1)S(1)}, bf16[192,2048]{1,0:T(8,128)(2,1)S(1)}, u32[]{:S(2)}, u32[]{:S(2)}) %collective-permute-start.16) | collective-permute-done | bytes 786464 | tf_op jit(solution)/shard_map/ppermute | solution.py:119
  56.9 1.4 %collective-permute-start.19 = (bf16[144,2048]{1,0:T(8,128)(2,1)S(1)}, bf16[144,2048]{1,0:T(8,128)(2,1)S(1)}, u32[]{:S(2)}, u32[]{:S(2)}) collective-permute-start(bf16[144,2048]{1,0:T(8,128)(2,1)S(1)} %slice.21), channel_id=1, source_target_pairs={{0,8},{8,0},{16,24},{24,16},{1,9},{9,1},{17,25},{25,17},{2,10},{10... | collective-permute-start | bytes 1769480 | tf_op jit(solution)/shard_map/ppermute | solution.py:121
  59.3 2.0 %collective-permute-start.21 = (bf16[48,2048]{1,0:T(8,128)(2,1)S(1)}, bf16[48,2048]{1,0:T(8,128)(2,1)S(1)}, u32[]{:S(2)}, u32[]{:S(2)}) collective-permute-start(bf16[48,2048]{1,0:T(8,128)(2,1)S(1)} %get-tuple-element.72), channel_id=1, source_target_pairs={{0,1},{1,0},{2,3},{3,2},{4,5},{5,4},{6,7},{7,6},{8,9},{9,8},{10,11... | collective-permute-start | bytes 589832 | tf_op jit(solution)/shard_map/ppermute | solution.py:118
  62.3 8.5 %ffn.3 = (bf16[192,2048]{1,0:T(8,128)(2,1)S(1)}, bf16[192,2048]{1,0:T(8,128)(2,1)S(1)}, bf16[192,2048]{1,0:T(8,128)(2,1)S(1)}, bf16[192,2048]{1,0:T(8,128)(2,1)S(1)}) custom-call(bf16[192,2048]{1,0:T(8,128)(2,1)S(1)} %add_convert_fusion.3.refs_0_, bf16[192,2048]{1,0:T(8,128)(2,1)S(1)} %add_convert_fusion.2.refs_1_, s32[2]{0:T(128)S(1)} %pad_add_fusion.refs_0_.refs_2_, ...), custom_call_target="tpu_custom_call" | custom-call | flops 7247757312 | bytes 25165824 | tf_op jit(solution)/shard_map/ffn/pallas_call | solution.py:86
  70.9 1.5 %collective-permute-done.19 = bf16[144,2048]{1,0:T(8,128)(2,1)S(1)} collective-permute-done((bf16[144,2048]{1,0:T(8,128)(2,1)S(1)}, bf16[144,2048]{1,0:T(8,128)(2,1)S(1)}, u32[]{:S(2)}, u32[]{:S(2)}) %collective-permute-start.19) | collective-permute-done | bytes 589856 | tf_op jit(solution)/shard_map/ppermute | solution.py:121
  73.0 5.4 %collective-permute-start.28 = (bf16[48,2048]{1,0:T(8,128)(2,1)S(1)}, bf16[48,2048]{1,0:T(8,128)(2,1)S(1)}, u32[]{:S(2)}, u32[]{:S(2)}) collective-permute-start(bf16[48,2048]{1,0:T(8,128)(2,1)S(1)} %add_convert_fusion.6), channel_id=1, source_target_pairs={{0,24},{8,16},{16,8},{24,0},{1,25},{9,17},{17,9},{25,1},{2,26},{10... | collective-permute-start | bytes 589832 | tf_op jit(solution)/shard_map/ppermute | solution.py:121
  79.8 2.4 %collective-permute-start.32 = (bf16[48,2048]{1,0:T(8,128)(2,1)S(1)}, bf16[48,2048]{1,0:T(8,128)(2,1)S(1)}, u32[]{:S(2)}, u32[]{:S(2)}) collective-permute-start(bf16[48,2048]{1,0:T(8,128)(2,1)S(1)} %get-tuple-element.69), channel_id=1, source_target_pairs={{0,5},{1,4},{4,1},{5,0},{2,7},{3,6},{6,3},{7,2},{8,13},{9,12},{12,... | collective-permute-start | bytes 589832 | tf_op jit(solution)/shard_map/ppermute | solution.py:120
  82.7 3.9 %collective-permute-done.30 = bf16[48,2048]{1,0:T(8,128)(2,1)S(1)} collective-permute-done((bf16[48,2048]{1,0:T(8,128)(2,1)S(1)}, bf16[48,2048]{1,0:T(8,128)(2,1)S(1)}, u32[]{:S(2)}, u32[]{:S(2)}) %collective-permute-start.30) | collective-permute-done | bytes 196640 | tf_op jit(solution)/shard_map/ppermute | solution.py:117
  87.1 1.9 %collective-permute-done.31 = bf16[48,2048]{1,0:T(8,128)(2,1)S(1)} collective-permute-done((bf16[48,2048]{1,0:T(8,128)(2,1)S(1)}, bf16[48,2048]{1,0:T(8,128)(2,1)S(1)}, u32[]{:S(2)}, u32[]{:S(2)}) %collective-permute-start.31) | collective-permute-done | bytes 196640 | tf_op jit(solution)/shard_map/ppermute | solution.py:118
  89.0 1.7 %collective-permute-done.32 = bf16[48,2048]{1,0:T(8,128)(2,1)S(1)} collective-permute-done((bf16[48,2048]{1,0:T(8,128)(2,1)S(1)}, bf16[48,2048]{1,0:T(8,128)(2,1)S(1)}, u32[]{:S(2)}, u32[]{:S(2)}) %collective-permute-start.32) | collective-permute-done | bytes 196640 | tf_op jit(solution)/shard_map/ppermute | solution.py:120
  90.8 2.9 %collective-permute-start.26 = (bf16[48,2048]{1,0:T(8,128)(2,1)S(1)}, bf16[48,2048]{1,0:T(8,128)(2,1)S(1)}, u32[]{:S(2)}, u32[]{:S(2)}) collective-permute-start(bf16[48,2048]{1,0:T(8,128)(2,1)S(1)} %get-tuple-element.66), channel_id=1, source_target_pairs={{0,5},{1,4},{4,1},{5,0},{2,7},{3,6},{6,3},{7,2},{8,13},{9,12},{12,... | collective-permute-start | bytes 589832 | tf_op jit(solution)/shard_map/ppermute | solution.py:120
  95.0 3.8 %collective-permute-done.25 = bf16[48,2048]{1,0:T(8,128)(2,1)S(1)} collective-permute-done((bf16[48,2048]{1,0:T(8,128)(2,1)S(1)}, bf16[48,2048]{1,0:T(8,128)(2,1)S(1)}, u32[]{:S(2)}, u32[]{:S(2)}) %collective-permute-start.25) | collective-permute-done | bytes 196640 | tf_op jit(solution)/shard_map/ppermute | solution.py:118
  98.8 3.7 %collective-permute-done.33 = bf16[48,2048]{1,0:T(8,128)(2,1)S(1)} collective-permute-done((bf16[48,2048]{1,0:T(8,128)(2,1)S(1)}, bf16[48,2048]{1,0:T(8,128)(2,1)S(1)}, u32[]{:S(2)}, u32[]{:S(2)}) %collective-permute-start.33) | collective-permute-done | bytes 196640 | tf_op jit(solution)/shard_map/ppermute | solution.py:121
  (82 shorter events, 13.7 us)
Async XLA Ops:
  2.0 11.1 %collective-permute-start = (bf16[48,2176]{1,0:T(8,128)(2,1)S(1)}, bf16[48,2176]{1,0:T(8,128)(2,1)S(1)}, u32[]{:S(2)}, u32[]{:S(2)}) collective-permute-start(bf16[48,2176]{1,0:T(8,128)(2,1)S(1)} %concatenate.24), channel_id=1, source_target_pairs={{0,24},{8,16},{16,8},{24,0},{1,25},{9,17},{17,9},{25,1},{2,26},{10... | collective-permute-start | bytes 626696 | tf_op jit(solution)/shard_map/ppermute | solution.py:121
  7.1 11.5 %collective-permute-start.4 = (bf16[48,2176]{1,0:T(8,128)(2,1)S(1)}, bf16[48,2176]{1,0:T(8,128)(2,1)S(1)}, u32[]{:S(2)}, u32[]{:S(2)}) collective-permute-start(bf16[48,2176]{1,0:T(8,128)(2,1)S(1)} %concatenate.24), channel_id=1, source_target_pairs={{0,4},{4,0},{1,5},{5,1},{2,6},{6,2},{3,7},{7,3},{8,12},{12,8},{9,1... | collective-permute-start | bytes 626696 | tf_op jit(solution)/shard_map/ppermute | solution.py:117
  8.6 11.6 %collective-permute-start.5 = (bf16[48,2176]{1,0:T(8,128)(2,1)S(1)}, bf16[48,2176]{1,0:T(8,128)(2,1)S(1)}, u32[]{:S(2)}, u32[]{:S(2)}) collective-permute-start(bf16[48,2176]{1,0:T(8,128)(2,1)S(1)} %concatenate.24), channel_id=1, source_target_pairs={{0,1},{1,0},{2,3},{3,2},{4,5},{5,4},{6,7},{7,6},{8,9},{9,8},{10,11... | collective-permute-start | bytes 626696 | tf_op jit(solution)/shard_map/ppermute | solution.py:118
  10.1 10.6 %collective-permute-start.6 = (bf16[48,2176]{1,0:T(8,128)(2,1)S(1)}, bf16[48,2176]{1,0:T(8,128)(2,1)S(1)}, u32[]{:S(2)}, u32[]{:S(2)}) collective-permute-start(bf16[48,2176]{1,0:T(8,128)(2,1)S(1)} %concatenate.24), channel_id=1, source_target_pairs={{0,5},{1,4},{4,1},{5,0},{2,7},{3,6},{6,3},{7,2},{8,13},{9,12},{12,... | collective-permute-start | bytes 626696 | tf_op jit(solution)/shard_map/ppermute | solution.py:120
  10.6 6.4 %collective-permute-start.11 = (bf16[48,2176]{1,0:T(8,128)(2,1)S(1)}, bf16[48,2176]{1,0:T(8,128)(2,1)S(1)}, u32[]{:S(2)}, u32[]{:S(2)}) collective-permute-start(bf16[48,2176]{1,0:T(8,128)(2,1)S(1)} %concatenate.24), channel_id=1, source_target_pairs={{0,8},{8,0},{16,24},{24,16},{1,9},{9,1},{17,25},{25,17},{2,10},{10... | collective-permute-start | bytes 626696 | tf_op jit(solution)/shard_map/ppermute | solution.py:121
  13.1 9.6 %collective-permute-start.2 = (bf16[48,2176]{1,0:T(8,128)(2,1)S(1)}, bf16[48,2176]{1,0:T(8,128)(2,1)S(1)}, u32[]{:S(2)}, u32[]{:S(2)}) collective-permute-start(bf16[48,2176]{1,0:T(8,128)(2,1)S(1)} %collective-permute-done), channel_id=1, source_target_pairs={{0,4},{4,0},{1,5},{5,1},{2,6},{6,2},{3,7},{7,3},{8,12},{12,8},{9,1... | collective-permute-start | bytes 626696 | tf_op jit(solution)/shard_map/ppermute | solution.py:117
  17.0 5.9 %collective-permute-start.3 = (bf16[48,2176]{1,0:T(8,128)(2,1)S(1)}, bf16[48,2176]{1,0:T(8,128)(2,1)S(1)}, u32[]{:S(2)}, u32[]{:S(2)}) collective-permute-start(bf16[48,2176]{1,0:T(8,128)(2,1)S(1)} %collective-permute-done), channel_id=1, source_target_pairs={{0,8},{8,0},{16,24},{24,16},{1,9},{9,1},{17,25},{25,17},{2,10},{10... | collective-permute-start | bytes 626696 | tf_op jit(solution)/shard_map/ppermute | solution.py:121
  18.5 9.7 %collective-permute-start.1 = (bf16[48,2176]{1,0:T(8,128)(2,1)S(1)}, bf16[48,2176]{1,0:T(8,128)(2,1)S(1)}, u32[]{:S(2)}, u32[]{:S(2)}) collective-permute-start(bf16[48,2176]{1,0:T(8,128)(2,1)S(1)} %collective-permute-done), channel_id=1, source_target_pairs={{0,1},{1,0},{2,3},{3,2},{4,5},{5,4},{6,7},{7,6},{8,9},{9,8},{10,11... | collective-permute-start | bytes 626696 | tf_op jit(solution)/shard_map/ppermute | solution.py:118
  22.8 8.0 %collective-permute-start.9 = (bf16[48,2176]{1,0:T(8,128)(2,1)S(1)}, bf16[48,2176]{1,0:T(8,128)(2,1)S(1)}, u32[]{:S(2)}, u32[]{:S(2)}) collective-permute-start(bf16[48,2176]{1,0:T(8,128)(2,1)S(1)} %collective-permute-done.3), channel_id=1, source_target_pairs={{0,1},{1,0},{2,3},{3,2},{4,5},{5,4},{6,7},{7,6},{8,9},{9,8},{10,11... | collective-permute-start | bytes 626696 | tf_op jit(solution)/shard_map/ppermute | solution.py:118
  24.4 8.1 %collective-permute-start.8 = (bf16[48,2176]{1,0:T(8,128)(2,1)S(1)}, bf16[48,2176]{1,0:T(8,128)(2,1)S(1)}, u32[]{:S(2)}, u32[]{:S(2)}) collective-permute-start(bf16[48,2176]{1,0:T(8,128)(2,1)S(1)} %collective-permute-done.3), channel_id=1, source_target_pairs={{0,4},{4,0},{1,5},{5,1},{2,6},{6,2},{3,7},{7,3},{8,12},{12,8},{9,1... | collective-permute-start | bytes 626696 | tf_op jit(solution)/shard_map/ppermute | solution.py:117
  25.9 14.0 %collective-permute-start.12 = (bf16[144,2176]{1,0:T(8,128)(2,1)S(1)}, bf16[144,2176]{1,0:T(8,128)(2,1)S(1)}, u32[]{:S(2)}, u32[]{:S(2)}) collective-permute-start(bf16[144,2176]{1,0:T(8,128)(2,1)S(1)} %pad_maximum_fusion.1), channel_id=1, source_target_pairs={{0,8},{8,0},{16,24},{24,16},{1,9},{9,1},{17,25},{25,17},{2,10},{10... | collective-permute-start | bytes 1880072 | tf_op jit(solution)/shard_map/ppermute | solution.py:121
  27.7 6.0 %collective-permute-start.7 = (bf16[48,2176]{1,0:T(8,128)(2,1)S(1)}, bf16[48,2176]{1,0:T(8,128)(2,1)S(1)}, u32[]{:S(2)}, u32[]{:S(2)}) collective-permute-start(bf16[48,2176]{1,0:T(8,128)(2,1)S(1)} %collective-permute-done.2), channel_id=1, source_target_pairs={{0,1},{1,0},{2,3},{3,2},{4,5},{5,4},{6,7},{7,6},{8,9},{9,8},{10,11... | collective-permute-start | bytes 626696 | tf_op jit(solution)/shard_map/ppermute | solution.py:118
  30.9 5.8 %collective-permute-start.10 = (bf16[48,2176]{1,0:T(8,128)(2,1)S(1)}, bf16[48,2176]{1,0:T(8,128)(2,1)S(1)}, u32[]{:S(2)}, u32[]{:S(2)}) collective-permute-start(bf16[48,2176]{1,0:T(8,128)(2,1)S(1)} %collective-permute-done.9), channel_id=1, source_target_pairs={{0,4},{4,0},{1,5},{5,1},{2,6},{6,2},{3,7},{7,3},{8,12},{12,8},{9,1... | collective-permute-start | bytes 626696 | tf_op jit(solution)/shard_map/ppermute | solution.py:117
  37.4 3.4 %collective-permute-start.13 = (bf16[192,2176]{1,0:T(8,128)(2,1)S(1)}, bf16[192,2176]{1,0:T(8,128)(2,1)S(1)}, u32[]{:S(2)}, u32[]{:S(2)}) collective-permute-start(bf16[192,2176]{1,0:T(8,128)(2,1)S(1)} %constant_dynamic-update-slice_fusion.refs_1_), channel_id=1, source_target_pairs={{0,2},{2,0},{1,3},{3,1},{4,6},{6,4},{5,7},{7,5},{8,10},{10,8},{9,1... | collective-permute-start | bytes 2506760 | tf_op jit(solution)/shard_map/ppermute | solution.py:119
  40.2 21.2 %collective-permute-start.18 = (bf16[192,2176]{1,0:T(8,128)(2,1)S(1)}, bf16[192,2176]{1,0:T(8,128)(2,1)S(1)}, u32[]{:S(2)}, u32[]{:S(2)}) collective-permute-start(bf16[192,2176]{1,0:T(8,128)(2,1)S(1)} %pad_maximum_fusion.refs_4_), channel_id=1, source_target_pairs={{0,2},{2,0},{1,3},{3,1},{4,6},{6,4},{5,7},{7,5},{8,10},{10,8},{9,1... | collective-permute-start | bytes 2506760 | tf_op jit(solution)/shard_map/ppermute | solution.py:119
  54.5 3.9 %collective-permute-start.15 = (bf16[192,2048]{1,0:T(8,128)(2,1)S(1)}, bf16[192,2048]{1,0:T(8,128)(2,1)S(1)}, u32[]{:S(2)}, u32[]{:S(2)}) collective-permute-start(bf16[192,2048]{1,0:T(8,128)(2,1)S(1)} %get-tuple-element.42), channel_id=1, source_target_pairs={{0,2},{2,0},{1,3},{3,1},{4,6},{6,4},{5,7},{7,5},{8,10},{10,8},{9,1... | collective-permute-start | bytes 2359304 | tf_op jit(solution)/shard_map/ppermute | solution.py:119
  55.0 7.3 %collective-permute-start.17 = (bf16[192,2176]{1,0:T(8,128)(2,1)S(1)}, bf16[192,2176]{1,0:T(8,128)(2,1)S(1)}, u32[]{:S(2)}, u32[]{:S(2)}) collective-permute-start(bf16[192,2176]{1,0:T(8,128)(2,1)S(1)} %constant_dynamic-update-slice_fusion.6.refs_3_), channel_id=1, source_target_pairs={{0,2},{2,0},{1,3},{3,1},{4,6},{6,4},{5,7},{7,5},{8,10},{10,8},{9,1... | collective-permute-start | bytes 2506760 | tf_op jit(solution)/shard_map/ppermute | solution.py:119
  56.9 15.4 %collective-permute-start.19 = (bf16[144,2048]{1,0:T(8,128)(2,1)S(1)}, bf16[144,2048]{1,0:T(8,128)(2,1)S(1)}, u32[]{:S(2)}, u32[]{:S(2)}) collective-permute-start(bf16[144,2048]{1,0:T(8,128)(2,1)S(1)} %slice.21), channel_id=1, source_target_pairs={{0,8},{8,0},{16,24},{24,16},{1,9},{9,1},{17,25},{25,17},{2,10},{10... | collective-permute-start | bytes 1769480 | tf_op jit(solution)/shard_map/ppermute | solution.py:121
  58.7 12.1 %collective-permute-start.20 = (bf16[48,2048]{1,0:T(8,128)(2,1)S(1)}, bf16[48,2048]{1,0:T(8,128)(2,1)S(1)}, u32[]{:S(2)}, u32[]{:S(2)}) collective-permute-start(bf16[48,2048]{1,0:T(8,128)(2,1)S(1)} %get-tuple-element.73), channel_id=1, source_target_pairs={{0,4},{4,0},{1,5},{5,1},{2,6},{6,2},{3,7},{7,3},{8,12},{12,8},{9,1... | collective-permute-start | bytes 589832 | tf_op jit(solution)/shard_map/ppermute | solution.py:117
  59.3 11.5 %collective-permute-start.21 = (bf16[48,2048]{1,0:T(8,128)(2,1)S(1)}, bf16[48,2048]{1,0:T(8,128)(2,1)S(1)}, u32[]{:S(2)}, u32[]{:S(2)}) collective-permute-start(bf16[48,2048]{1,0:T(8,128)(2,1)S(1)} %get-tuple-element.72), channel_id=1, source_target_pairs={{0,1},{1,0},{2,3},{3,2},{4,5},{5,4},{6,7},{7,6},{8,9},{9,8},{10,11... | collective-permute-start | bytes 589832 | tf_op jit(solution)/shard_map/ppermute | solution.py:118
  61.4 9.5 %collective-permute-start.22 = (bf16[48,2048]{1,0:T(8,128)(2,1)S(1)}, bf16[48,2048]{1,0:T(8,128)(2,1)S(1)}, u32[]{:S(2)}, u32[]{:S(2)}) collective-permute-start(bf16[48,2048]{1,0:T(8,128)(2,1)S(1)} %get-tuple-element.71), channel_id=1, source_target_pairs={{0,5},{1,4},{4,1},{5,0},{2,7},{3,6},{6,3},{7,2},{8,13},{9,12},{12,... | collective-permute-start | bytes 589832 | tf_op jit(solution)/shard_map/ppermute | solution.py:120
  72.4 6.0 %collective-permute-start.29 = (bf16[192,2048]{1,0:T(8,128)(2,1)S(1)}, bf16[192,2048]{1,0:T(8,128)(2,1)S(1)}, u32[]{:S(2)}, u32[]{:S(2)}) collective-permute-start(bf16[192,2048]{1,0:T(8,128)(2,1)S(1)} %get-tuple-element.64), channel_id=1, source_target_pairs={{0,2},{2,0},{1,3},{3,1},{4,6},{6,4},{5,7},{7,5},{8,10},{10,8},{9,1... | collective-permute-start | bytes 2359304 | tf_op jit(solution)/shard_map/ppermute | solution.py:119
  72.4 7.4 %collective-permute-start.23 = (bf16[192,2048]{1,0:T(8,128)(2,1)S(1)}, bf16[192,2048]{1,0:T(8,128)(2,1)S(1)}, u32[]{:S(2)}, u32[]{:S(2)}) collective-permute-start(bf16[192,2048]{1,0:T(8,128)(2,1)S(1)} %get-tuple-element.56), channel_id=1, source_target_pairs={{0,2},{2,0},{1,3},{3,1},{4,6},{6,4},{5,7},{7,5},{8,10},{10,8},{9,1... | collective-permute-start | bytes 2359304 | tf_op jit(solution)/shard_map/ppermute | solution.py:119
  73.0 20.8 %collective-permute-start.28 = (bf16[48,2048]{1,0:T(8,128)(2,1)S(1)}, bf16[48,2048]{1,0:T(8,128)(2,1)S(1)}, u32[]{:S(2)}, u32[]{:S(2)}) collective-permute-start(bf16[48,2048]{1,0:T(8,128)(2,1)S(1)} %add_convert_fusion.6), channel_id=1, source_target_pairs={{0,24},{8,16},{16,8},{24,0},{1,25},{9,17},{17,9},{25,1},{2,26},{10... | collective-permute-start | bytes 589832 | tf_op jit(solution)/shard_map/ppermute | solution.py:121
  78.4 15.7 %collective-permute-start.27 = (bf16[48,2048]{1,0:T(8,128)(2,1)S(1)}, bf16[48,2048]{1,0:T(8,128)(2,1)S(1)}, u32[]{:S(2)}, u32[]{:S(2)}) collective-permute-start(bf16[48,2048]{1,0:T(8,128)(2,1)S(1)} %slice.20), channel_id=1, source_target_pairs={{0,8},{8,0},{16,24},{24,16},{1,9},{9,1},{17,25},{25,17},{2,10},{10... | collective-permute-start | bytes 589832 | tf_op jit(solution)/shard_map/ppermute | solution.py:121
  78.7 7.9 %collective-permute-start.30 = (bf16[48,2048]{1,0:T(8,128)(2,1)S(1)}, bf16[48,2048]{1,0:T(8,128)(2,1)S(1)}, u32[]{:S(2)}, u32[]{:S(2)}) collective-permute-start(bf16[48,2048]{1,0:T(8,128)(2,1)S(1)} %get-tuple-element.68), channel_id=1, source_target_pairs={{0,4},{4,0},{1,5},{5,1},{2,6},{6,2},{3,7},{7,3},{8,12},{12,8},{9,1... | collective-permute-start | bytes 589832 | tf_op jit(solution)/shard_map/ppermute | solution.py:117
  79.3 9.7 %collective-permute-start.31 = (bf16[48,2048]{1,0:T(8,128)(2,1)S(1)}, bf16[48,2048]{1,0:T(8,128)(2,1)S(1)}, u32[]{:S(2)}, u32[]{:S(2)}) collective-permute-start(bf16[48,2048]{1,0:T(8,128)(2,1)S(1)} %get-tuple-element.70), channel_id=1, source_target_pairs={{0,1},{1,0},{2,3},{3,2},{4,5},{5,4},{6,7},{7,6},{8,9},{9,8},{10,11... | collective-permute-start | bytes 589832 | tf_op jit(solution)/shard_map/ppermute | solution.py:118
  79.8 11.0 %collective-permute-start.32 = (bf16[48,2048]{1,0:T(8,128)(2,1)S(1)}, bf16[48,2048]{1,0:T(8,128)(2,1)S(1)}, u32[]{:S(2)}, u32[]{:S(2)}) collective-permute-start(bf16[48,2048]{1,0:T(8,128)(2,1)S(1)} %get-tuple-element.69), channel_id=1, source_target_pairs={{0,5},{1,4},{4,1},{5,0},{2,7},{3,6},{6,3},{7,2},{8,13},{9,12},{12,... | collective-permute-start | bytes 589832 | tf_op jit(solution)/shard_map/ppermute | solution.py:120
  86.6 8.5 %collective-permute-start.24 = (bf16[48,2048]{1,0:T(8,128)(2,1)S(1)}, bf16[48,2048]{1,0:T(8,128)(2,1)S(1)}, u32[]{:S(2)}, u32[]{:S(2)}) collective-permute-start(bf16[48,2048]{1,0:T(8,128)(2,1)S(1)} %get-tuple-element.65), channel_id=1, source_target_pairs={{0,4},{4,0},{1,5},{5,1},{2,6},{6,2},{3,7},{7,3},{8,12},{12,8},{9,1... | collective-permute-start | bytes 589832 | tf_op jit(solution)/shard_map/ppermute | solution.py:117
  89.0 9.8 %collective-permute-start.25 = (bf16[48,2048]{1,0:T(8,128)(2,1)S(1)}, bf16[48,2048]{1,0:T(8,128)(2,1)S(1)}, u32[]{:S(2)}, u32[]{:S(2)}) collective-permute-start(bf16[48,2048]{1,0:T(8,128)(2,1)S(1)} %get-tuple-element.67), channel_id=1, source_target_pairs={{0,1},{1,0},{2,3},{3,2},{4,5},{5,4},{6,7},{7,6},{8,9},{9,8},{10,11... | collective-permute-start | bytes 589832 | tf_op jit(solution)/shard_map/ppermute | solution.py:118
  90.8 8.1 %collective-permute-start.26 = (bf16[48,2048]{1,0:T(8,128)(2,1)S(1)}, bf16[48,2048]{1,0:T(8,128)(2,1)S(1)}, u32[]{:S(2)}, u32[]{:S(2)}) collective-permute-start(bf16[48,2048]{1,0:T(8,128)(2,1)S(1)} %get-tuple-element.66), channel_id=1, source_target_pairs={{0,5},{1,4},{4,1},{5,0},{2,7},{3,6},{6,3},{7,2},{8,13},{9,12},{12,... | collective-permute-start | bytes 589832 | tf_op jit(solution)/shard_map/ppermute | solution.py:120
  93.8 8.7 %collective-permute-start.33 = (bf16[48,2048]{1,0:T(8,128)(2,1)S(1)}, bf16[48,2048]{1,0:T(8,128)(2,1)S(1)}, u32[]{:S(2)}, u32[]{:S(2)}) collective-permute-start(bf16[48,2048]{1,0:T(8,128)(2,1)S(1)} %add_convert_fusion.5), channel_id=1, source_target_pairs={{0,16},{8,24},{16,0},{24,8},{1,17},{9,25},{17,1},{25,9},{2,18},{10... | collective-permute-start | bytes 589832 | tf_op jit(solution)/shard_map/ppermute | solution.py:121
  (8 other events, 52.0 us)
